TPU v7x, 32 devices: a whole 2x2x4 slice. The times are simulated.
32 devices in a mesh: section: 2 (over x), dp: 4 (over y, core), seq: 4 (over z).
Axes of the slice: x: 2, y: 2, z: 4, core: 2. Of those that a mesh axis runs over, the one named last changes fastest.
Arguments:
- tokens: bfloat16 [2, 4, 1024, 768], P(None, 'dp', 'seq'), may hold values from -6 to 6
- cotangent: bfloat16 [2, 4, 1024, 768], P(None, 'dp', 'seq'), may hold values from -6 to 6
- in_weight: bfloat16 [2, 768, 3352], P('section', ('dp', 'seq')), may hold values from -0.21875 to 0.21875
- out_weight: bfloat16 [2, 1536, 768], P('section', ('dp', 'seq')), may hold values from -0.15625 to 0.15625
- conv_weight: bfloat16 [2, 4, 1792], P('section', None, ('dp', 'seq')), may hold values from -3 to 3
- conv_bias: bfloat16 [2, 1792], P('section', ('dp', 'seq')), may hold values from -2.5 to 2.5
- norm_gain: bfloat16 [2, 768], P('section', ('dp', 'seq')), may hold values from 0.25 to 1.75
- gate_gain: bfloat16 [2, 1536], P('section', ('dp', 'seq')), may hold values from 0.25 to 1.75
- dt_bias: float32 [2, 24], P('section'), may hold values from -6 to -3.5
- a_log: float32 [2, 24], P('section'), as said below
- d_skip: float32 [2, 24], P('section'), may hold values from 0.5 to 1.5
Outputs:
- activations: bfloat16 [2, 2, 4, 1024, 768], P('section', None, 'dp', 'seq')
- input_grads: float32 [2, 2, 4, 1024, 768], P('section', None, 'dp', 'seq')
- in_weight_grad: float32 [2, 768, 3352], P('section', ('dp', 'seq'))
- out_weight_grad: float32 [2, 1536, 768], P('section', ('dp', 'seq'))
- conv_weight_grad: float32 [2, 4, 1792], P('section', None, ('dp', 'seq'))
- conv_bias_grad: float32 [2, 1792], P('section', ('dp', 'seq'))
- norm_gain_grad: float32 [2, 768], P('section', ('dp', 'seq'))
- gate_gain_grad: float32 [2, 1536], P('section', ('dp', 'seq'))
- dt_bias_grad: float32 [2, 24], P('section')
- a_log_grad: float32 [2, 24], P('section')
- d_skip_grad: float32 [2, 24], P('section')
Inputs may be any that keep to these rules, and one draw needn't show every extreme that they name: `a_log`: each head's decay rate, with its step size bias.
All inputs are finite; a program needn't handle non-finite values.
Results may differ from a plain program's by a relative error of at most 0.02.
Values may be sent and summed in bfloat16 or wider, within the bound.
A program may use at most 256 MiB of HBM per device.

v0:
```python
import jax
import jax.numpy as jnp
from jax import lax
from jax.sharding import PartitionSpec as P

D = 768
DI = 1536
P_SIZE = 64
N = 128
CONVK = 4
MB = 2
H = 24
CH = 1792
E = 3352


EPSILON = 1e-05
PRECISE = lax.Precision.HIGHEST


def shifted(x, axis, by):
    length = lax.axis_size(axis)
    pairs = [(i, i + by) for i in range(length) if 0 <= i + by < length]
    return lax.ppermute(x, axis, pairs)


def as_sent(x):
    return jax.tree.map(lambda a: a.astype(jnp.bfloat16) if a.dtype == jnp.float32 else a, x)


def contract_rows(left, right):
    return lax.dot_general(
        left, right, (((0,), (0,)), ((), ())), preferred_element_type=jnp.float32
    )


def contract_cols(left, right):
    return lax.dot_general(
        left, right, (((1,), (1,)), ((), ())), preferred_element_type=jnp.float32
    )


def silu_slope(values):
    sigma = jax.nn.sigmoid(values)
    return sigma * (1.0 + values * (1.0 - sigma))


def convolve(padded, conv_w, conv_b, tok_rows):
    conv_out = conv_b.astype(jnp.float32)
    for k in range(CONVK):
        conv_out = conv_out + conv_w[k].astype(jnp.float32) * padded[k : k + tok_rows].astype(
            jnp.float32
        )
    return conv_out


def gated_parts(projected, y_out):
    gate_cols = projected[:, :DI].astype(jnp.float32)
    gate_swish = jax.nn.silu(gate_cols)
    gated_y = y_out * gate_swish
    inv_rms = lax.rsqrt(jnp.mean(gated_y * gated_y, axis=-1, keepdims=True) + EPSILON)
    return (gate_cols, gate_swish, inv_rms, gated_y * inv_rms)


def zero_fill(specs):
    return tuple((jnp.zeros(shape, dtype) for shape, dtype in specs))


def spare_branch(specs):
    return lambda *operands: zero_fill(specs)


def stash_slot(buffer, value, slot_idx, is_active):
    previous = lax.dynamic_index_in_dim(buffer, slot_idx, 0, keepdims=False)
    return lax.dynamic_update_index_in_dim(
        buffer, jnp.where(is_active, value, previous), slot_idx, 0
    )


def norm_project(layer_in, norm_g, w_in):
    values = layer_in.astype(jnp.float32)
    inv_rms = lax.rsqrt(jnp.mean(values * values, axis=-1, keepdims=True) + EPSILON)
    normed = (values * inv_rms * norm_g.astype(jnp.float32)).astype(jnp.bfloat16)
    return (jnp.dot(normed, w_in, preferred_element_type=jnp.float32).astype(jnp.bfloat16),)


def scan_local(projected, conv_rows, conv_w, conv_b, bias_dt, log_rate):
    tok_rows = projected.shape[0]
    padded = jnp.concatenate([conv_rows, projected[:, DI : DI + CH]], axis=0)
    activated = jax.nn.silu(convolve(padded, conv_w, conv_b, tok_rows)).astype(jnp.bfloat16)
    heads_x = activated[:, :DI].reshape(tok_rows, H, P_SIZE)
    b_proj = activated[:, DI : DI + N]
    c_proj = activated[:, DI + N :]
    dt_step = jax.nn.softplus(projected[:, DI + CH :].astype(jnp.float32) + bias_dt)
    cumulative = jnp.cumsum(dt_step * -jnp.exp(log_rate), axis=0)
    c_left = c_proj.astype(jnp.float32)[None] * jnp.exp(cumulative).T[:, :, None]
    b_right = b_proj.astype(jnp.float32)[None] * (jnp.exp(-cumulative) * dt_step).T[:, :, None]
    raw_mix = jnp.einsum("htn,hsn->hts", c_left, b_right, precision=PRECISE)
    causal = jnp.tril(jnp.ones((tok_rows, tok_rows), jnp.bool_))[None]
    mixing = jnp.where(causal, raw_mix, 0.0).astype(jnp.bfloat16)
    y_intra = jnp.einsum("hts,shp->thp", mixing, heads_x, preferred_element_type=jnp.float32)
    to_end = jnp.exp(cumulative[-1:] - cumulative)
    weighted = (heads_x.astype(jnp.float32) * (dt_step * to_end)[:, :, None]).astype(jnp.bfloat16)
    states = jnp.einsum("shp,sn->hpn", weighted, b_proj, preferred_element_type=jnp.float32)
    totals = jnp.exp(cumulative[-1])
    return (padded, activated, mixing, y_intra, states, totals, dt_step, cumulative)


def mix_output(
    layer_in, projected, activated, y_intra, cumulative, incoming, skip_gain, gate_g, w_out
):
    tok_rows = projected.shape[0]
    heads_x = activated[:, :DI].reshape(tok_rows, H, P_SIZE).astype(jnp.float32)
    c_decayed = (
        activated[:, None, DI + N :].astype(jnp.float32) * jnp.exp(cumulative)[:, :, None]
    ).astype(jnp.bfloat16)
    y_inter = jnp.einsum(
        "thn,hpn->thp", c_decayed, incoming.astype(jnp.bfloat16), preferred_element_type=jnp.float32
    )
    y_out = (y_intra + y_inter + skip_gain[None, :, None] * heads_x).reshape(tok_rows, DI)
    gate_cols, gate_swish, inv_rms, normed = gated_parts(projected, y_out)
    to_proj = (normed * gate_g.astype(jnp.float32)).astype(jnp.bfloat16)
    mixed_out = layer_in.astype(jnp.float32) + jnp.dot(
        to_proj, w_out, preferred_element_type=jnp.float32
    )
    return (mixed_out.astype(jnp.bfloat16), y_out)


def back_first(
    grad_v,
    projected,
    activated,
    mixing,
    y_out,
    cumulative,
    dt_step,
    incoming,
    skip_gain,
    gate_g,
    w_out,
):
    tok_rows = projected.shape[0]
    grad_out = grad_v.astype(jnp.bfloat16)
    gate_cols, gate_swish, inv_rms, normed = gated_parts(projected, y_out)
    gain_vals = gate_g.astype(jnp.float32)
    to_proj = (normed * gain_vals).astype(jnp.bfloat16)
    grad_wout = contract_rows(to_proj, grad_out)
    grad_shown = contract_cols(grad_out, w_out)
    grad_gain = jnp.sum(grad_shown * normed, axis=0)
    grad_norm = grad_shown * gain_vals
    grad_gated = inv_rms * (
        grad_norm - normed * jnp.mean(grad_norm * normed, axis=-1, keepdims=True)
    )
    grad_gate = grad_gated * y_out * silu_slope(gate_cols)
    grad_y = (grad_gated * gate_swish).astype(jnp.bfloat16).reshape(tok_rows, H, P_SIZE)
    heads_x = activated[:, :DI].reshape(tok_rows, H, P_SIZE)
    b_proj = activated[:, DI : DI + N]
    c_proj = activated[:, DI + N :]
    grad_yf = grad_y.astype(jnp.float32)
    grad_skip = jnp.sum(grad_yf * heads_x.astype(jnp.float32), axis=(0, 2))
    exp_cum = jnp.exp(cumulative)
    c_decayed = (c_proj[:, None, :].astype(jnp.float32) * exp_cum[:, :, None]).astype(jnp.bfloat16)
    grad_cdec = jnp.einsum(
        "thp,hpn->thn", grad_y, incoming.astype(jnp.bfloat16), preferred_element_type=jnp.float32
    )
    grad_in = jnp.einsum("thp,thn->hpn", grad_y, c_decayed, preferred_element_type=jnp.float32)
    grad_c = jnp.sum(grad_cdec * exp_cum[:, :, None], axis=1)
    grad_cum = exp_cum * jnp.sum(grad_cdec * c_proj[:, None, :].astype(jnp.float32), axis=2)
    grad_mix = jnp.einsum("thp,shp->hts", grad_y, heads_x, preferred_element_type=jnp.float32)
    grad_x = skip_gain[None, :, None] * grad_yf + jnp.einsum(
        "hts,thp->shp", mixing, grad_y, preferred_element_type=jnp.float32
    )
    inner_cb = contract_cols(c_proj, b_proj)
    causal = jnp.tril(jnp.ones((tok_rows, tok_rows), jnp.bool_))[None]
    masked = jnp.where(
        causal, grad_mix * exp_cum.T[:, :, None] * jnp.exp(-cumulative).T[:, None, :], 0.0
    )
    step_rows = dt_step.T
    grad_inner = jnp.einsum("hts,hs->ts", masked, step_rows, precision=PRECISE)
    with_inner = masked * inner_cb[None]
    grad_step = jnp.sum(with_inner, axis=1).T
    row_part = jnp.einsum("hts,hs->th", with_inner, step_rows, precision=PRECISE)
    grad_cum = grad_cum + row_part - grad_step * dt_step
    grad_c = grad_c + jnp.dot(grad_inner, b_proj.astype(jnp.float32), precision=PRECISE)
    grad_b = jnp.dot(grad_inner.T, c_proj.astype(jnp.float32), precision=PRECISE)
    return (
        grad_wout,
        grad_gain,
        grad_skip,
        grad_gate,
        grad_x,
        grad_b,
        grad_c,
        grad_cum,
        grad_step,
        grad_in,
    )


def back_second(
    grad_leave,
    incoming,
    totals,
    activated,
    dt_step,
    cumulative,
    padded,
    conv_w,
    conv_b,
    projected,
    bias_dt,
    log_rate,
    grad_x,
    grad_b,
    grad_c,
    grad_cum,
    grad_step,
):
    tok_rows = activated.shape[0]
    grad_states = grad_leave.astype(jnp.bfloat16)
    heads_x = activated[:, :DI].reshape(tok_rows, H, P_SIZE)
    b_proj = activated[:, DI : DI + N]
    to_end = jnp.exp(cumulative[-1:] - cumulative)
    factor = dt_step * to_end
    weighted = (heads_x.astype(jnp.float32) * factor[:, :, None]).astype(jnp.bfloat16)
    grad_b = grad_b + jnp.einsum(
        "shp,hpn->sn", weighted, grad_states, preferred_element_type=jnp.float32
    )
    grad_weighted = jnp.einsum(
        "sn,hpn->shp", b_proj, grad_states, preferred_element_type=jnp.float32
    )
    grad_x = grad_x + grad_weighted * factor[:, :, None]
    grad_factor = jnp.sum(grad_weighted * heads_x.astype(jnp.float32), axis=2)
    grad_step = grad_step + grad_factor * to_end
    grad_end = grad_factor * factor
    grad_cum = grad_cum - grad_end
    last_add = jnp.sum(grad_end, axis=0) + jnp.sum(grad_leave * incoming, axis=(1, 2)) * totals
    grad_cum = grad_cum.at[-1].add(last_add)
    grad_rate = jnp.flip(jnp.cumsum(jnp.flip(grad_cum, 0), axis=0), 0)
    rate_vals = -jnp.exp(log_rate)
    grad_step = grad_step + grad_rate * rate_vals
    grad_alog = jnp.sum(grad_rate * dt_step, axis=0) * rate_vals
    grad_raw = grad_step * jax.nn.sigmoid(projected[:, DI + CH :].astype(jnp.float32) + bias_dt)
    grad_dtb = jnp.sum(grad_raw, axis=0)
    grad_acts = jnp.concatenate([grad_x.reshape(tok_rows, DI), grad_b, grad_c], axis=1)
    grad_conv = grad_acts * silu_slope(convolve(padded, conv_w, conv_b, tok_rows))
    grad_cb = jnp.sum(grad_conv, axis=0)
    grad_cw = jnp.stack(
        [
            jnp.sum(grad_conv * padded[k : k + tok_rows].astype(jnp.float32), axis=0)
            for k in range(CONVK)
        ]
    )
    grad_pad = jnp.zeros((tok_rows + CONVK - 1, CH), jnp.float32)
    for k in range(CONVK):
        grad_pad = grad_pad.at[k : k + tok_rows].add(conv_w[k].astype(jnp.float32) * grad_conv)
    return (grad_cw, grad_cb, grad_dtb, grad_alog, grad_raw, grad_pad)


def back_third(grad_pad, edge_back, grad_gate, grad_raw, layer_in, grad_v, norm_g, w_in):
    tok_rows = grad_gate.shape[0]
    tail_rows = jnp.concatenate(
        [jnp.zeros((tok_rows - CONVK + 1, CH), jnp.float32), edge_back], axis=0
    )
    grad_xbc = grad_pad[CONVK - 1 :] + tail_rows
    grad_proj = jnp.concatenate([grad_gate, grad_xbc, grad_raw], axis=1).astype(jnp.bfloat16)
    values = layer_in.astype(jnp.float32)
    inv_rms = lax.rsqrt(jnp.mean(values * values, axis=-1, keepdims=True) + EPSILON)
    normed = values * inv_rms
    gain_vals = norm_g.astype(jnp.float32)
    to_proj = (normed * gain_vals).astype(jnp.bfloat16)
    grad_win = contract_rows(to_proj, grad_proj)
    grad_shown = contract_cols(grad_proj, w_in)
    grad_norm_gain = jnp.sum(grad_shown * normed, axis=0)
    grad_norm = grad_shown * gain_vals
    grad_u = grad_v + inv_rms * (
        grad_norm - normed * jnp.mean(grad_norm * normed, axis=-1, keepdims=True)
    )
    return (grad_u, grad_win, grad_norm_gain)


def body(
    tokens,
    cotangent,
    in_weight,
    out_weight,
    conv_weight,
    conv_bias,
    norm_gain,
    gate_gain,
    dt_bias,
    a_log,
    d_skip,
):
    section_idx = lax.axis_index("section")
    section_count = lax.axis_size("section")
    seq_count = lax.axis_size("seq")
    token_feed = tokens[:, 0]
    cot_feed = cotangent[:, 0]
    tok_rows = token_feed.shape[1]
    is_first = section_idx == 0
    is_last = section_idx == section_count - 1
    bias_dt = dt_bias[0]
    log_rate = a_log[0]
    skip_gain = d_skip[0]
    f32 = jnp.float32
    bf16 = jnp.bfloat16
    own_shards = (
        in_weight[0],
        out_weight[0],
        conv_weight[0],
        conv_bias[0],
        norm_gain[0],
        gate_gain[0],
    )
    w_in, w_out, conv_w, conv_b, norm_g, gate_g = (
        lax.all_gather(own_shards[0], ("dp", "seq"), axis=0, tiled=True),
        lax.all_gather(own_shards[1], ("dp", "seq"), axis=0, tiled=True),
        lax.all_gather(own_shards[2], ("dp", "seq"), axis=1, tiled=True),
        lax.all_gather(own_shards[3], ("dp", "seq"), axis=0, tiled=True),
        lax.all_gather(own_shards[4], ("dp", "seq"), axis=0, tiled=True),
        lax.all_gather(own_shards[5], ("dp", "seq"), axis=0, tiled=True),
    )
    front_spec = (((tok_rows, E), bf16),)
    local_spec = (
        ((tok_rows + CONVK - 1, CH), bf16),
        ((tok_rows, CH), bf16),
        ((H, tok_rows, tok_rows), bf16),
        ((tok_rows, H, P_SIZE), f32),
        ((H, P_SIZE, N), f32),
        ((H,), f32),
        ((tok_rows, H), f32),
        ((tok_rows, H), f32),
    )
    output_spec = (((tok_rows, D), bf16), ((tok_rows, DI), f32))
    first_spec = (
        ((DI, D), f32),
        ((DI,), f32),
        ((H,), f32),
        ((tok_rows, DI), f32),
        ((tok_rows, H, P_SIZE), f32),
        ((tok_rows, N), f32),
        ((tok_rows, N), f32),
        ((tok_rows, H), f32),
        ((tok_rows, H), f32),
        ((H, P_SIZE, N), f32),
    )
    second_spec = (
        ((CONVK, CH), f32),
        ((CH,), f32),
        ((H,), f32),
        ((H,), f32),
        ((tok_rows, H), f32),
        ((tok_rows + CONVK - 1, CH), f32),
    )
    third_spec = (((tok_rows, D), f32), ((D, E), f32), ((D,), f32))
    from_prev = jnp.zeros((tok_rows, D), bf16)
    kept_bufs = None
    act_store = jnp.zeros((MB, tok_rows, D), bf16)
    for tick_idx in range(MB + section_count - 1):
        micro_idx = tick_idx - section_idx
        is_active = (micro_idx >= 0) & (micro_idx < MB)
        slot_idx = jnp.clip(micro_idx, 0, MB - 1)
        layer_in = jnp.where(
            is_first, lax.dynamic_index_in_dim(token_feed, slot_idx, 0, keepdims=False), from_prev
        )
        (projected,) = lax.cond(
            is_active, norm_project, spare_branch(front_spec), layer_in, norm_g, w_in
        )
        conv_rows = shifted(projected[tok_rows - CONVK + 1 :, DI : DI + CH], "seq", 1)
        local_out = lax.cond(
            is_active,
            scan_local,
            spare_branch(local_spec),
            projected,
            conv_rows,
            conv_w,
            conv_b,
            bias_dt,
            log_rate,
        )
        padded, activated, mixing, y_intra, states, totals, dt_step, cumulative = local_out
        incoming = jnp.zeros((H, P_SIZE, N), f32)
        for hop_idx in range(seq_count - 1):
            incoming = shifted(as_sent(totals[:, None, None] * incoming + states), "seq", 1)
        mixed_out, y_out = lax.cond(
            is_active,
            mix_output,
            spare_branch(output_spec),
            layer_in,
            projected,
            activated,
            y_intra,
            cumulative,
            incoming,
            skip_gain,
            gate_g,
            w_out,
        )
        from_prev = shifted(mixed_out, "section", 1)
        kept_now = (
            layer_in,
            projected,
            padded,
            activated,
            mixing,
            y_out,
            incoming,
            dt_step,
            cumulative,
        )
        if kept_bufs is None:
            kept_bufs = jax.tree.map(lambda v: jnp.zeros((MB,) + v.shape, v.dtype), kept_now)
        kept_bufs = jax.tree.map(
            lambda buf, v: stash_slot(buf, v, slot_idx, is_active), kept_bufs, kept_now
        )
        act_store = stash_slot(act_store, mixed_out, slot_idx, is_active)
    w_in, w_out, conv_w, conv_b, norm_g, gate_g = (
        lax.all_gather(own_shards[0], ("dp", "seq"), axis=0, tiled=True),
        lax.all_gather(own_shards[1], ("dp", "seq"), axis=0, tiled=True),
        lax.all_gather(own_shards[2], ("dp", "seq"), axis=1, tiled=True),
        lax.all_gather(own_shards[3], ("dp", "seq"), axis=0, tiled=True),
        lax.all_gather(own_shards[4], ("dp", "seq"), axis=0, tiled=True),
        lax.all_gather(own_shards[5], ("dp", "seq"), axis=0, tiled=True),
    )
    from_next = jnp.zeros((tok_rows, D), bf16)
    grad_store = jnp.zeros((MB, tok_rows, D), f32)
    grad_shares = None
    head_total = (jnp.zeros((H,), f32), jnp.zeros((H,), f32), jnp.zeros((H,), f32))
    for tick_idx in range(MB + section_count - 1):
        micro_idx = tick_idx - (section_count - 1 - section_idx)
        is_active = (micro_idx >= 0) & (micro_idx < MB)
        slot_idx = jnp.clip(micro_idx, 0, MB - 1)
        grad_v = jnp.where(
            is_last,
            lax.dynamic_index_in_dim(cot_feed, slot_idx, 0, keepdims=False).astype(f32),
            from_next.astype(f32),
        )
        kept_now = jax.tree.map(
            lambda buf: lax.dynamic_index_in_dim(buf, slot_idx, 0, keepdims=False), kept_bufs
        )
        layer_in, projected, padded, activated, mixing, y_out, incoming, dt_step, cumulative = (
            kept_now
        )
        first_out = lax.cond(
            is_active,
            back_first,
            spare_branch(first_spec),
            grad_v,
            projected,
            activated,
            mixing,
            y_out,
            cumulative,
            dt_step,
            incoming,
            skip_gain,
            gate_g,
            w_out,
        )
        (
            grad_wout,
            grad_gain,
            grad_skip,
            grad_gate,
            grad_x,
            grad_b,
            grad_c,
            grad_cum,
            grad_step,
            grad_in,
        ) = first_out
        totals = jnp.exp(cumulative[-1])
        grad_leave = jnp.zeros((H, P_SIZE, N), f32)
        for hop_idx in range(seq_count - 1):
            grad_leave = shifted(as_sent(totals[:, None, None] * grad_leave + grad_in), "seq", -1)
        second_out = lax.cond(
            is_active,
            back_second,
            spare_branch(second_spec),
            grad_leave,
            incoming,
            totals,
            activated,
            dt_step,
            cumulative,
            padded,
            conv_w,
            conv_b,
            projected,
            bias_dt,
            log_rate,
            grad_x,
            grad_b,
            grad_c,
            grad_cum,
            grad_step,
        )
        grad_cw, grad_cb, grad_dtb, grad_alog, grad_raw, grad_pad = second_out
        edge_back = shifted(grad_pad[: CONVK - 1], "seq", -1)
        grad_u, grad_win, grad_norm_gain = lax.cond(
            is_active,
            back_third,
            spare_branch(third_spec),
            grad_pad,
            edge_back,
            grad_gate,
            grad_raw,
            layer_in,
            grad_v,
            norm_g,
            w_in,
        )
        from_next = shifted(grad_u.astype(bf16), "section", -1)
        grad_store = stash_slot(grad_store, grad_u, slot_idx, is_active)
        local_grads = (grad_win, grad_wout, grad_cw, grad_cb, grad_norm_gain, grad_gain)
        head_total = (
            head_total[0] + grad_dtb,
            head_total[1] + grad_alog,
            head_total[2] + grad_skip,
        )
        shares_now = (
            lax.psum_scatter(local_grads[0], ("dp", "seq"), scatter_dimension=0, tiled=True),
            lax.psum_scatter(local_grads[1], ("dp", "seq"), scatter_dimension=0, tiled=True),
            lax.psum_scatter(local_grads[2], ("dp", "seq"), scatter_dimension=1, tiled=True),
            lax.psum_scatter(local_grads[3], ("dp", "seq"), scatter_dimension=0, tiled=True),
            lax.psum_scatter(local_grads[4], ("dp", "seq"), scatter_dimension=0, tiled=True),
            lax.psum_scatter(local_grads[5], ("dp", "seq"), scatter_dimension=0, tiled=True),
        )
        grad_shares = (
            shares_now if grad_shares is None else jax.tree.map(jnp.add, grad_shares, shares_now)
        )
    head_sums = lax.psum((head_total[0], head_total[1], head_total[2]), ("dp", "seq"))
    share_win, share_wout, share_cw, share_cb, share_norm, share_gate = grad_shares
    return (
        act_store[None, :, None],
        grad_store[None, :, None],
        share_win[None],
        share_wout[None],
        share_cw[None],
        share_cb[None],
        share_norm[None],
        share_gate[None],
        head_sums[0][None],
        head_sums[1][None],
        head_sums[2][None],
    )


def solution(mesh):
    in_specs = (
        P(None, "dp", "seq", None),
        P(None, "dp", "seq", None),
        P("section", ("dp", "seq"), None),
        P("section", ("dp", "seq"), None),
        P("section", None, ("dp", "seq")),
        P("section", ("dp", "seq")),
        P("section", ("dp", "seq")),
        P("section", ("dp", "seq")),
        P("section", None),
        P("section", None),
        P("section", None),
    )
    out_specs = (
        P("section", None, "dp", "seq", None),
        P("section", None, "dp", "seq", None),
        P("section", ("dp", "seq"), None),
        P("section", ("dp", "seq"), None),
        P("section", None, ("dp", "seq")),
        P("section", ("dp", "seq")),
        P("section", ("dp", "seq")),
        P("section", ("dp", "seq")),
        P("section", None),
        P("section", None),
        P("section", None),
    )
    return jax.shard_map(body, mesh=mesh, in_specs=in_specs, out_specs=out_specs, check_vma=False)
```

profile of v0, /device:TPU:0, one launch (start us, length us, event | category | flops | bytes accessed | tf_op | source)
XLA Modules:
  0.0 1430.8 jit_solution(14053912193552634307)
XLA Ops:
  15.8 56.2 %all-gather.3 = bf16[1,4,1792]{1,0,2:T(2,128)(2,1)S(1)} all-gather(bf16[1,4,112]{1,0,2:T(2,128)(2,1)S(1)} %copy.905), channel_id=5, replica_groups=mesh['section'=2,'dp'=4,'seq'=4] {'dp','seq'}, dimensions={2}, use_global_device_ids=true | all-gather | bytes 15232 | tf_op jit(solution)/shard_map/all_gather | solution.py:319
  75.2 60.9 %all-reduce.13 = (bf16[768]{0:T(1024)(128)(2,1)}, bf16[1792]{0:T(1024)(128)(2,1)}, bf16[1536]{0:T(1024)(128)(2,1)}) all-reduce(bf16[768]{0:T(1024)(128)(2,1)S(1)} %dynamic-update-slice.57, bf16[1792]{0:T(1024)(128)(2,1)S(1)} %dynamic-update-slice.58, ...), channel_id=2, replica_groups=mesh['section'=2,'dp'=4,'seq'=4] {'dp','seq'}, use_global_device_ids=true, to_apply=%add.6 | all-reduce | flops 4096 | bytes 16384 | tf_op jit(solution)/shard_map/all_gather | solution.py:321
  157.0 54.5 %conditional.19 = (bf16[256,1792]{1,0:T(8,128)(2,1)}, bf16[24,256,256]{2,1,0:T(8,128)(2,1)}, f32[256,24,64]{0,2,1:T(8,128)}, f32[24,64,128]{2,1,0:T(8,128)}, f32...) conditional(s32[]{:T(128)} %convert_element_type.864, ...), branch_computations={%region_3.4_spmd, %region_4.7_spmd} | conditional | flops 2738603776 | bytes 32459336 | solution.py:371
  198.5 8.9 select_convert_fusion
  230.3 7.4 collective-permute-done.2
  252.7 22.0 %conditional.20 = (bf16[256,768]{1,0:T(8,128)(2,1)}, f32[256,1536]{1,0:T(8,128)}) conditional(s32[]{:T(128)} %convert_element_type.864, () %tuple.230, (bf16[256,768]{1,0:T(8,128)(2,1)}, bf16[256,1792]{1,0:T(8,128)(2,1)}, f32[256,24]{1,0:T(8,128)}, bf16[24,64,128]{2,1,0:T(8,128)(2,1)}, f32[256,24,64]{0,2,1:T(8,128)}, /*index=5*/f32[1,24]{1,0:T(1,128)}, ...), branch_computations={%region_7.8_spmd, %region_8.10_spmd} | conditional | flops 712738560 | bytes 37588192 | solution.py:386
  284.9 7.9 conditional.21
  318.0 25.6 %conditional.22 = (bf16[256,1792]{1,0:T(8,128)(2,1)S(1)}, bf16[24,256,256]{2,1,0:T(8,128)(2,1)}, f32[256,24,64]{0,2,1:T(8,128)}, f32[24,64,128]{2,1,0:T(8,128)},...) conditional(s32[]{:T(128)} %convert_element_type.870, ...), branch_computations={%region_13.14_spmd, %region_14.17_spmd} | conditional | flops 2738603776 | bytes 33815860 | solution.py:371
  331.6 7.8 select_convert_fusion.1
  362.6 6.6 collective-permute-done.7
  380.9 14.5 %conditional.23 = (bf16[256,768]{1,0:T(8,128)(2,1)S(1)}, f32[256,1536]{1,0:T(8,128)}) conditional(s32[]{:T(128)} %convert_element_type.870, () %tuple.236, (bf16[256,768]{1,0:T(8,128)(2,1)}, bf16[256,1792]{1,0:T(8,128)(2,1)S(1)}, f32[256,24]{1,0:T(8,128)S(1)}, bf16[24,64,128]{2,1,0:T(8,128)(2,1)}, f32[256,24,64]{0,2,1:T(8,128)}, ...), branch_computations={%region_17.18_spmd, %region_18.20_spmd} | conditional | flops 712738560 | bytes 30510328 | solution.py:386
  431.7 6.6 conditional.25
  479.0 9.3 conditional.27
  493.0 8.9 collective-permute-done.14
  506.4 9.9 collective-permute-done.15
  519.4 8.2 collective-permute-done.16
  550.3 201.4 %collective-permute-done.18 = bf16[256,768]{1,0:T(8,128)(2,1)S(1)} collective-permute-done((bf16[256,768]{1,0:T(8,128)(2,1)S(1)}, bf16[256,768]{1,0:T(8,128)(2,1)S(1)}, u32[]{:S(2)}, u32[]{:S(2)}) %collective-permute-start.18) | collective-permute-done | bytes 393248 | tf_op jit(solution)/shard_map/ppermute | solution.py:24
  753.6 50.4 %conditional.30 = (f32[1536,768]{1,0:T(8,128)}, f32[1536]{0:T(1024)}, f32[24]{0:T(128)}, bf16[256,1536]{1,0:T(8,128)(2,1)}, f32[256,24,64]{0,2,1:T(8,128)}, /*in...) conditional(s32[]{:T(128)} %convert_element_type.889, ...), branch_computations={%region_59.60_spmd, %region_60.69_spmd} | conditional | flops 2096548096 | bytes 129827704 | solution.py:445
  796.3 6.3 fusion.156
  806.1 9.0 collective-permute-done.19
  817.2 8.4 collective-permute-done.20
  827.1 8.4 collective-permute-done.21
  835.5 96.6 %conditional.31 = (f32[4,1792]{1,0:T(4,128)S(1)}, f32[1792]{0:T(1024)}, f32[24]{0:T(128)}, f32[24]{0:T(128)}, bf16[256,24]{1,0:T(8,128)(2,1)S(1)}, /*index=5*/f32[259,1792]{0,1:T(8,128)}) conditional(s32[]{:T(128)} %convert_element_type.889, () %tuple.257, (bf16[256,1792]{1,0:T(8,128)(2,1)}, bf16[24,64,128]{2,1,0:T(8,128)(2,1)S(1)}, ...), branch_computations={%region_69.70_spmd, %region_70.83_spmd} | conditional | flops 224703616 | bytes 77764288 | solution.py:477
  888.9 10.8 scatter-add.41
  904.1 10.8 scatter-add.44
  915.0 6.2 fusion.311
  921.2 10.8 scatter-add.45
  943.2 21.1 %conditional.32 = (f32[256,768]{1,0:T(8,128)S(1)}, f32[768,3352]{0,1:T(8,128)}, f32[768]{0:T(1024)S(1)}) conditional(s32[]{:T(128)} %convert_element_type.889, () %tuple.254, (bf16[2,256,768]{2,1,0:T(8,128)(2,1)}, s32[]{:T(128)}, bf16[256,1536]{1,0:T(8,128)(2,1)}, f32[259,1792]{0,1:T(8,128)}, f32[3,1792]{1,0:T(4,128)}, ...), branch_computations={%region_83.84_spmd, %region_84.88_spmd} | conditional | flops 2651463936 | bytes 30189716 | solution.py:501
  957.5 6.8 fusion.85
  967.8 7.1 collective-permute-done.23
  976.9 50.8 %conditional.33 = (f32[1536,768]{1,0:T(8,128)}, f32[1536]{0:T(1024)}, f32[24]{0:T(128)}, bf16[256,1536]{1,0:T(8,128)(2,1)}, f32[256,24,64]{0,2,1:T(8,128)}, /*in...) conditional(s32[]{:T(128)} %convert_element_type.899, ...), branch_computations={%region_88.89_spmd, %region_89.98_spmd} | conditional | flops 2096548096 | bytes 129827704 | solution.py:445
  1019.8 6.3 fusion.195
  1029.8 12.2 collective-permute-done.24
  1044.1 8.4 collective-permute-done.25
  1054.0 8.4 collective-permute-done.26
  1062.4 95.5 %conditional.34 = (f32[4,1792]{1,0:T(4,128)S(1)}, f32[1792]{0:T(1024)}, f32[24]{0:T(128)}, f32[24]{0:T(128)}, bf16[256,24]{1,0:T(8,128)(2,1)}, /*index=5*/f32[259,1792]{0,1:T(8,128)}) conditional(s32[]{:T(128)} %convert_element_type.899, () %tuple.263, (bf16[256,1792]{1,0:T(8,128)(2,1)}, bf16[24,64,128]{2,1,0:T(8,128)(2,1)S(1)}, ...), branch_computations={%region_98.99_spmd, %region_99.112_spmd} | conditional | flops 224703616 | bytes 77764704 | solution.py:477
  1115.0 10.8 scatter-add.50
  1130.1 10.8 scatter-add.51
  1140.8 6.2 fusion.327
  1147.0 10.8 scatter-add.54
  1166.6 17.1 %conditional.35 = (f32[256,768]{1,0:T(8,128)S(1)}, f32[768,3352]{0,1:T(8,128)}, f32[768]{0:T(1024)S(1)}) conditional(s32[]{:T(128)} %convert_element_type.899, () %tuple.260, (bf16[2,256,768]{2,1,0:T(8,128)(2,1)}, s32[]{:T(128)}, bf16[256,1536]{1,0:T(8,128)(2,1)}, f32[259,1792]{0,1:T(8,128)}, f32[3,1792]{1,0:T(4,128)S(1)}, ...), branch_computations={%region_112.113_spmd, %region_113.117_spmd} | conditional | flops 2651463936 | bytes 30165028 | solution.py:501
  1176.9 6.7 fusion.107
  1183.6 15.1 %add_add_fusion = f32[768,3352]{0,1:T(8,128)} fusion(f32[768,3352]{0,1:T(8,128)} %get-tuple-element.1225, f32[768,3352]{0,1:T(8,128)} %get-tuple-element.1223, f32[768,3352]{0,1:T(8,128)} %get-tuple-element.1224), kind=kLoop, calls=%fused_computation.651 | loop fusion | flops 5148672 | bytes 41189376 | tf_op jit(solution)/shard_map/add | solution.py:531
  1198.7 11.4 copy.999
  1210.1 8.3 add_add_fusion.1
  1228.9 61.5 %all-reduce.12 = (f32[1792]{0:T(1024)S(1)}, f32[768]{0:T(1024)S(1)}, f32[1536]{0:T(1024)S(1)}, f32[1,24]{1,0:T(1,128)}, f32[1,24]{1,0:T(1,128)}, /*index=5*/f32[1,24]{1,0:T(1,128)}) all-reduce(f32[1792]{0:T(1024)S(1)} %add_add_fusion.4, ...), channel_id=23, replica_groups=mesh['section'=2,'dp'=4,'seq'=4] {'dp','seq'}, use_global_device_ids=true, to_apply=%region_126.127.clone | all-reduce | flops 4168 | bytes 33344
  1294.6 49.2 %reduce-scatter.10.cloned.1.call-done = f32[48,3352]{1,0:T(8,128)} async-done(((f32[768,3352]{1,0:T(8,128)}), f32[48,3352]{1,0:T(8,128)}) %reduce-scatter.10.cloned.1.call-update) | async-done | bytes 643600
  1346.7 77.1 %reduce-scatter.8.cloned.1.call-done = f32[96,768]{1,0:T(8,128)} async-done(((f32[1536,768]{1,0:T(8,128)}), f32[96,768]{1,0:T(8,128)}) %reduce-scatter.8.cloned.1.call-update) | async-done | bytes 294928 | tf_op jit(solution)/shard_map/reduce_scatter | solution.py:524
  (843 shorter events, 661.1 us)
Async XLA Ops:
  7.2 129.9 %all-gather.9.cloned.1.call-start = ((), (), s32[]{:S(2)}) async-start(), calls=%async_computation.3 | async-start | bytes 5640192 | tf_op jit(solution)/shard_map/all_gather | solution.py:317
  7.9 239.2 %all-gather.11.cloned.1.call-start = ((), (), s32[]{:S(2)}) async-start(), calls=%async_computation.4 | async-start | bytes 2506752 | tf_op jit(solution)/shard_map/all_gather | solution.py:318
  8.7 1284.5 %reduce-scatter.12.cloned.1.call-start = ((), (), s32[]{:S(2)}) async-start(), calls=%async_computation.7 | async-start | bytes 974848
  13.9 123.2 %copy-start.63 = (bf16[256,768]{1,0:T(8,128)(2,1)}, bf16[256,768]{1,0:T(8,128)(2,1)S(1)}, u32[]{:S(2)}) copy-start(bf16[256,768]{1,0:T(8,128)(2,1)S(1)} %fusion.338) | copy-start | bytes 1179652
  14.9 59.6 %copy-start.229 = (bf16[1,48]{1,0:T(2,128)(2,1)S(1)}, bf16[1,48]{1,0:T(2,128)(2,1)}, u32[]{:S(2)}) copy-start(bf16[1,48]{1,0:T(2,128)(2,1)} %param.83) | copy-start | bytes 292
  14.9 59.8 %copy-start.230 = (bf16[1,96]{1,0:T(2,128)(2,1)S(1)}, bf16[1,96]{1,0:T(2,128)(2,1)}, u32[]{:S(2)}) copy-start(bf16[1,96]{1,0:T(2,128)(2,1)} %param.84) | copy-start | bytes 580
  14.9 60.1 %copy-start.231 = (bf16[1,112]{1,0:T(2,128)(2,1)S(1)}, bf16[1,112]{1,0:T(2,128)(2,1)}, u32[]{:S(2)}) copy-start(bf16[1,112]{1,0:T(2,128)(2,1)} %param.82) | copy-start | bytes 676
  14.9 121.2 %copy-start.75 = (bf16[2,1,256,768]{3,2,1,0:T(8,128)(2,1)S(1)}, bf16[2,1,256,768]{3,2,1,0:T(8,128)(2,1)}, u32[]{:S(2)}) copy-start(bf16[2,1,256,768]{3,2,1,0:T(8,128)(2,1)} %param.78) | copy-start | bytes 2359300
  145.8 11.2 collective-permute-start
  213.5 10.6 collective-permute-start.1
  216.4 29.2 %copy-start.94 = (f32[2,256,24]{1,2,0:T(8,128)}, f32[2,256,24]{1,2,0:T(8,128)S(1)}, u32[]{:S(2)}) copy-start(f32[2,256,24]{1,2,0:T(8,128)S(1)} %bitcast_dynamic-update-slice_fusion.29) | copy-start | bytes 147460
  224.0 20.9 %copy-start.100 = (f32[2,256,24]{1,2,0:T(8,128)}, f32[2,256,24]{1,2,0:T(8,128)S(1)}, u32[]{:S(2)}) copy-start(f32[2,256,24]{1,2,0:T(8,128)S(1)} %bitcast_dynamic-update-slice_fusion.26) | copy-start | bytes 147460
  225.4 12.4 collective-permute-start.2
  239.8 12.9 collective-permute-start.3
  274.6 9.2 collective-permute-start.4
  305.9 12.1 collective-permute-start.5
  344.9 13.4 collective-permute-start.6
  359.7 9.5 collective-permute-start.7
  362.5 18.4 %copy-start.23 = (bf16[2,256,1792]{2,1,0:T(8,128)(2,1)}, bf16[2,256,1792]{2,1,0:T(8,128)(2,1)S(1)}, u32[]{:S(2)}) copy-start(bf16[2,256,1792]{2,1,0:T(8,128)(2,1)S(1)} %bitcast_dynamic-update-slice_fusion.10) | copy-start | bytes 5505028
  362.5 18.4 %copy-start = (bf16[1,1536,768]{2,1,0:T(8,128)(2,1)S(1)}, bf16[1,1536,768]{2,1,0:T(8,128)(2,1)}, u32[]{:S(2)}) copy-start(bf16[1,1536,768]{2,1,0:T(8,128)(2,1)} %all-gather.11.cloned.1.call-done) | copy-start | bytes 7077892
  362.5 18.4 %copy-start.112 = (f32[256,24]{1,0:T(8,128)S(1)}, f32[256,24]{1,0:T(8,128)}, u32[]{:S(2)}) copy-start(f32[256,24]{1,0:T(8,128)} %copy-done.111) | copy-start | bytes 73732
  362.6 18.4 %copy-start.147 = (bf16[1536]{0:T(1024)(128)(2,1)S(1)}, bf16[1536]{0:T(1024)(128)(2,1)}, u32[]{:S(2)}) copy-start(bf16[1536]{0:T(1024)(128)(2,1)} %get-tuple-element.2927) | copy-start | bytes 9220
  370.5 10.4 collective-permute-start.8
  395.4 13.3 collective-permute-start.9
  421.9 9.8 collective-permute-start.10
  439.8 39.2 %copy-start.122 = (f32[256,24]{0,1:T(8,128)}, f32[256,24]{0,1:T(8,128)S(1)}, u32[]{:S(2)}) copy-start(f32[256,24]{0,1:T(8,128)S(1)} %get-tuple-element.3043) | copy-start | bytes 73732
  442.9 7.8 collective-permute-start.11
  452.0 9.8 collective-permute-start.12
  463.1 9.7 collective-permute-start.13
  489.5 12.3 collective-permute-start.14
  503.1 13.2 collective-permute-start.15
  517.6 10.0 collective-permute-start.16
  536.2 5.9 collective-permute-start.17
  547.8 203.9 %collective-permute-start.18 = (bf16[256,768]{1,0:T(8,128)(2,1)S(1)}, bf16[256,768]{1,0:T(8,128)(2,1)S(1)}, u32[]{:S(2)}, u32[]{:S(2)}) collective-permute-start(bf16[256,768]{1,0:T(8,128)(2,1)S(1)} %convert_element_type.892), channel_id=1, source_target_pairs={{16,0},{17,1},{18,2},{19,3},{20,4},{21,5},{22,6},{23,7},{24,8},{25... | collective-permute-start | bytes 1179656 | tf_op jit(solution)/shard_map/ppermute | solution.py:24
  804.0 21.6 %copy-start.211 = (f32[24]{0:T(128)S(1)}, f32[24]{0:T(128)}, u32[]{:S(2)}) copy-start(f32[24]{0:T(128)} %get-tuple-element.3034) | copy-start | bytes 292
  804.8 10.3 collective-permute-start.19
  815.9 9.7 collective-permute-start.20
  825.8 9.7 collective-permute-start.21
  937.4 5.9 collective-permute-start.22
  965.3 9.7 collective-permute-start.23
  1027.7 24.8 %copy-start.210 = (f32[24]{0:T(128)S(1)}, f32[24]{0:T(128)}, u32[]{:S(2)}) copy-start(f32[24]{0:T(128)} %get-tuple-element.2976) | copy-start | bytes 292
  1028.5 13.5 collective-permute-start.24
  1042.8 9.7 collective-permute-start.25
  1052.7 9.7 collective-permute-start.26
  1069.5 17.1 %copy-start.228 = (f32[24]{0:T(128)}, f32[24]{0:T(128)S(1)}, u32[]{:S(2)}) copy-start(f32[24]{0:T(128)S(1)} %slice_bitcast_fusion.2) | copy-start | bytes 292 | tf_op jit(solution)/shard_map/cond
  1160.7 5.9 collective-permute-start.27
  1163.4 180.3 %reduce-scatter.10.cloned.1.call-start = ((), (), s32[]{:S(2)}) async-start(), calls=%async_computation.6 | async-start | bytes 11280384
  1210.1 213.8 %reduce-scatter.8.cloned.1.call-start = ((), (), s32[]{:S(2)}) async-start(), calls=%async_computation.5 | async-start | bytes 5013504 | tf_op jit(solution)/shard_map/reduce_scatter | solution.py:524
  (168 other events, 676.5 us)
Sparse Core Ops, SparseCore 0:
  10.2 69.4 all-gather.8
  82.0 42.2 all-gather.10
  1163.5 56.4 reduce-scatter.11
  1224.5 119.2 reduce-scatter.9
  1348.5 75.2 reduce-scatter.7
where the time goes:
time: 1450 us; the launch traced here: 1430 us
  waiting for transfers between devices  460 us (32%)
  local copies, waits for them, and re-layouts  312 us (22%)
  other arithmetic  250 us (17%)
  blocking collectives  179 us (12%)
  matrix products  139 us (10%)
  starting transfers between devices  70 us (5%)
  between operations  19.4 us (1%)
    ppermute x28, waiting for transfers between devices, shifted(): return lax.ppermute(x, axis, pairs)  332 us
    reduce_scatter x1, waiting for transfers between devices, body(): lax.psum_scatter(local_grads[1], ('dp', 'seq'), scatter_dimension=0, tile...  77.1 us
    ppermute x28, starting transfers between devices, shifted(): return lax.ppermute(x, axis, pairs)  69.8 us
    scatter-add x8, local copies, waits for them, and re-layouts, back_second(): grad_pad.at[k:k + tok_rows].add(conv_w[k].astype(jnp.float32) * grad_conv)  68.3 us
    another operation x71, local copies, waits for them, and re-layouts  67.1 us
    unnamed x1, blocking collectives  61.5 us
    all_gather x1, blocking collectives, body(): lax.all_gather(own_shards[4], ('dp', 'seq'), axis=0, tiled=True)  60.9 us
    all_gather x1, blocking collectives, body(): lax.all_gather(own_shards[2], ('dp', 'seq'), axis=1, tiled=True)  56.2 us
  transfers between devices with their start and end apart: 33, of which 24 were waited for; matrix products, arithmetic and copies ran while one was open for 15% of the time, Pallas kernels for 0%

commit v1 on v0

v1 whole, which is shorter than its diff:
```python
import jax
import jax.numpy as jnp
from jax import lax
from jax.experimental import pallas as pl
from jax.experimental.pallas import tpu as pltpu
from jax.sharding import PartitionSpec as P

D = 768
DI = 1536
P_SIZE = 64
N = 128
CONVK = 4
MB = 2
H = 24
CH = 1792
E = 3352
PAIRS = H // 2
PAIR = 2 * P_SIZE
EDGE = 16

EPSILON = 1e-05
PRECISE = lax.Precision.HIGHEST
f32 = jnp.float32
bf16 = jnp.bfloat16
WEIGHT_AXES = ("dp", "seq")


def dot(left, right, dims=((1,), (0,)), precision=None):
    return lax.dot_general(left, right, (dims, ((), ())), preferred_element_type=f32, precision=precision)


def rows_dot(left, right, precision=None):
    return dot(left, right, ((0,), (0,)), precision)


def cols_dot(left, right, precision=None):
    return dot(left, right, ((1,), (1,)), precision)


def shifted(x, axis, by):
    length = lax.axis_size(axis)
    pairs = [(i, i + by) for i in range(length) if 0 <= i + by < length]
    return lax.ppermute(x, axis, pairs)


def swapped(x):
    return lax.ppermute(x, "section", [(0, 1), (1, 0)])


def head_matrix():
    rows = lax.broadcasted_iota(jnp.int32, (H, DI), 0)
    cols = lax.broadcasted_iota(jnp.int32, (H, DI), 1)
    return (rows == cols // P_SIZE).astype(f32)


def expand(values):
    return dot(values, head_matrix(), precision=PRECISE)


def head_sums(values):
    return cols_dot(values, head_matrix(), precision=PRECISE)


def silu_slope(values):
    sigma = jax.nn.sigmoid(values)
    return sigma * (1.0 + values * (1.0 - sigma))


def lower_half(shape):
    return lax.broadcasted_iota(jnp.int32, shape, 1) < P_SIZE


def causal_decay(col, row):
    rows = col.shape[0]
    mask = lax.broadcasted_iota(jnp.int32, (rows, rows), 0) >= lax.broadcasted_iota(
        jnp.int32, (rows, rows), 1
    )
    return jnp.exp(jnp.where(mask, col - row, -1e30))


def intra_kernel(x_ref, b_ref, c_ref, cum_ref, cumt_ref, dtt_ref, skip_ref, y_ref, cb_ref):
    @pl.when(pl.program_id(0) == 0)
    def _():
        cb_ref[...] = cols_dot(c_ref[...], b_ref[...])

    x = x_ref[...]
    parts = []
    for i in range(2):
        decay = causal_decay(cum_ref[:, i * P_SIZE : i * P_SIZE + 1], cumt_ref[0, i : i + 1, :])
        mix = (cb_ref[...] * decay * dtt_ref[0, i : i + 1, :]).astype(bf16)
        parts.append(dot(mix, x))
    y = jnp.where(lower_half(x.shape), parts[0], parts[1])
    y_ref[...] = y + skip_ref[...] * x.astype(f32)


def inter_kernel(c_ref, cum_ref, held_ref, part_ref, y_ref):
    c = c_ref[...].astype(f32)
    parts = []
    for i in range(2):
        cdec = (c * jnp.exp(cum_ref[:, i * P_SIZE : i * P_SIZE + 1])).astype(bf16)
        parts.append(dot(cdec, held_ref[...]))
    y_ref[...] = part_ref[...] + jnp.where(lower_half(parts[0].shape), parts[0], parts[1])


def held_grad_kernel(c_ref, cum_ref, dy_ref, out_ref):
    c = c_ref[...].astype(f32)
    parts = []
    for i in range(2):
        cdec = (c * jnp.exp(cum_ref[:, i * P_SIZE : i * P_SIZE + 1])).astype(bf16)
        parts.append(rows_dot(cdec, dy_ref[...]))
    out_ref[...] = jnp.where(lower_half(parts[0].shape), parts[0], parts[1])


def mix_grad_kernel(
    dy_ref,
    x_ref,
    b_ref,
    c_ref,
    cum_ref,
    cumt_ref,
    dtt_ref,
    held_ref,
    skip_ref,
    dx_ref,
    dstep_ref,
    dcum_ref,
    db_ref,
    dc_ref,
    cb_ref,
    dcb_ref,
):
    step = pl.program_id(0)

    @pl.when(step == 0)
    def _():
        cb_ref[...] = cols_dot(c_ref[...], b_ref[...])
        dcb_ref[...] = jnp.zeros_like(dcb_ref)
        dc_ref[...] = jnp.zeros_like(dc_ref)
        dcum_ref[...] = jnp.zeros_like(dcum_ref)

    dy = dy_ref[...]
    x = x_ref[...]
    c = c_ref[...].astype(f32)
    low = lower_half(dy.shape)
    lane = lax.broadcasted_iota(jnp.int32, dcum_ref.shape, 1)
    dx_parts = []
    for i in range(2):
        cum_col = cum_ref[:, i * P_SIZE : i * P_SIZE + 1]
        dt_row = dtt_ref[0, i : i + 1, :]
        decay = causal_decay(cum_col, cumt_ref[0, i : i + 1, :])
        cb_decay = cb_ref[...] * decay
        mix = (cb_decay * dt_row).astype(bf16)
        dx_parts.append(rows_dot(mix, dy))
        own = jnp.where(low if i == 0 else jnp.logical_not(low), dy, jnp.zeros_like(dy))
        dmix = cols_dot(own, x)
        dcb_ref[...] += dmix * decay * dt_row
        inner = dmix * cb_decay
        dstep_ref[0, i : i + 1, :] = jnp.sum(inner, axis=0, keepdims=True)
        grow = jnp.sum(inner * dt_row, axis=1, keepdims=True)
        dcdec = cols_dot(own, held_ref[...])
        grown = dcdec * jnp.exp(cum_col)
        dc_ref[...] += grown
        grow = grow + jnp.sum(grown * c, axis=1, keepdims=True)
        dcum_ref[...] += jnp.where(lane == 2 * step + i, grow, 0.0)
    dx_ref[...] = jnp.where(low, dx_parts[0], dx_parts[1]) + skip_ref[...] * dy.astype(f32)

    @pl.when(step == PAIRS - 1)
    def _():
        dc_ref[...] += dot(dcb_ref[...], b_ref[...].astype(f32), precision=PRECISE)
        db_ref[...] = rows_dot(dcb_ref[...], c, precision=PRECISE)


def by_pair(rows):
    return pl.BlockSpec((rows, PAIR), lambda j: (0, j))


def fixed(rows, block):
    return pl.BlockSpec((rows, PAIR), lambda j: (0, block))


def head_rows(rows):
    return pl.BlockSpec((1, 2, rows), lambda j: (j, 0, 0))


def call(kernel, out_shape, in_specs, out_specs, scratch=()):
    return pl.pallas_call(
        kernel,
        grid=(PAIRS,),
        out_shape=out_shape,
        in_specs=in_specs,
        out_specs=out_specs,
        scratch_shapes=list(scratch),
        compiler_params=pltpu.CompilerParams(vmem_limit_bytes=32 * 1024 * 1024),
    )


def shaped(*shape, dtype=f32):
    return jax.ShapeDtypeStruct(shape, dtype)


B_BLOCK = DI // PAIR
C_BLOCK = B_BLOCK + 1


def intra(acts, cum_wide, cum_t, dt_t, skip_wide):
    t = acts.shape[0]
    return call(
        intra_kernel,
        shaped(t, DI),
        [by_pair(t), fixed(t, B_BLOCK), fixed(t, C_BLOCK), by_pair(t), head_rows(t), head_rows(t), by_pair(1)],
        by_pair(t),
        [pltpu.VMEM((t, t), f32)],
    )(acts, acts, acts, cum_wide, cum_t, dt_t, skip_wide)


def inter(acts, cum_wide, held, part):
    t = acts.shape[0]
    return call(
        inter_kernel,
        shaped(t, DI),
        [fixed(t, C_BLOCK), by_pair(t), by_pair(N), by_pair(t)],
        by_pair(t),
    )(acts, cum_wide, held, part)


def held_grad(acts, cum_wide, dy):
    t = acts.shape[0]
    return call(
        held_grad_kernel,
        shaped(N, DI),
        [fixed(t, C_BLOCK), by_pair(t), by_pair(t)],
        by_pair(N),
    )(acts, cum_wide, dy)


def mix_grad(dy, acts, cum_wide, cum_t, dt_t, held, skip_wide):
    t = acts.shape[0]
    return call(
        mix_grad_kernel,
        (shaped(t, DI), shaped(PAIRS, 2, t), shaped(t, PAIR), shaped(t, N), shaped(t, N)),
        [
            by_pair(t),
            by_pair(t),
            fixed(t, B_BLOCK),
            fixed(t, C_BLOCK),
            by_pair(t),
            head_rows(t),
            head_rows(t),
            by_pair(N),
            by_pair(1),
        ],
        (by_pair(t), head_rows(t), fixed(t, 0), fixed(t, 0), fixed(t, 0)),
        [pltpu.VMEM((t, t), f32), pltpu.VMEM((t, t), f32)],
    )(dy, acts, acts, acts, cum_wide, cum_t, dt_t, held, skip_wide)


def lower_triangle(rows):
    return (
        lax.broadcasted_iota(jnp.int32, (rows, rows), 0)
        >= lax.broadcasted_iota(jnp.int32, (rows, rows), 1)
    ).astype(f32)


def rms_parts(values):
    inv_rms = lax.rsqrt(jnp.mean(values * values, axis=-1, keepdims=True) + EPSILON)
    return inv_rms, values * inv_rms


def layer_forward(layer_in, weights):
    w_in, w_out, conv_w, conv_b, norm_g, gate_g, bias_dt, log_rate, skip_gain = weights
    t = layer_in.shape[0]
    _, normed = rms_parts(layer_in.astype(f32))
    projected = dot((normed * norm_g).astype(bf16), w_in).astype(bf16)
    xbc = projected[:, DI : DI + CH]
    edge = shifted(xbc[t - EDGE :], "seq", 1)
    padded = jnp.concatenate([edge[EDGE - CONVK + 1 :], xbc], axis=0)
    conv = conv_b
    for k in range(CONVK):
        conv = conv + conv_w[k : k + 1] * padded[k : k + t].astype(f32)
    acts = jax.nn.silu(conv).astype(bf16)
    dt = jax.nn.softplus(projected[:, DI + CH :].astype(f32) + bias_dt)
    cum = dot(lower_triangle(t), dt * -jnp.exp(log_rate), precision=PRECISE)
    to_end = jnp.exp(cum[-1:] - cum)
    factor_wide = expand(dt * to_end)
    weighted = (acts[:, :DI].astype(f32) * factor_wide).astype(bf16)
    states = rows_dot(acts[:, DI : DI + N], weighted)
    totals = jnp.exp(cum[-1:])
    totals_wide = expand(totals)
    incoming = shifted(states.astype(bf16), "seq", 1)
    for _ in range(lax.axis_size("seq") - 2):
        incoming = shifted((totals_wide * incoming.astype(f32) + states).astype(bf16), "seq", 1)
    cum_wide = expand(cum)
    cum_t = cum.T.reshape(PAIRS, 2, t)
    dt_t = dt.T.reshape(PAIRS, 2, t)
    skip_wide = expand(skip_gain)
    part = intra(acts, cum_wide, cum_t, dt_t, skip_wide)
    y = inter(acts, cum_wide, incoming, part)
    gate_cols = projected[:, :DI].astype(f32)
    _, q = rms_parts(y * jax.nn.silu(gate_cols))
    mixed = layer_in.astype(f32) + dot((q * gate_g).astype(bf16), w_out)
    kept = (layer_in, projected, padded, acts, conv, dt, cum, cum_wide, cum_t, dt_t, skip_wide, incoming, y, weighted, factor_wide, totals, totals_wide)
    return mixed.astype(bf16), kept


def layer_backward(grad_v, kept, weights):
    w_in, w_out, conv_w, conv_b, norm_g, gate_g, bias_dt, log_rate, skip_gain = weights
    (layer_in, projected, padded, acts, conv, dt, cum, cum_wide, cum_t, dt_t, skip_wide, incoming, y, weighted, factor_wide, totals, totals_wide) = kept
    t = layer_in.shape[0]
    dob = grad_v.astype(bf16)
    z = projected[:, :DI].astype(f32)
    swish = jax.nn.silu(z)
    r2, q = rms_parts(y * swish)
    dyn = cols_dot(dob, w_out)
    grad_gate_gain = jnp.sum(dyn * q, axis=0)
    dq = dyn * gate_g
    dgated = r2 * (dq - q * jnp.mean(dq * q, axis=-1, keepdims=True))
    dz = (dgated * y * silu_slope(z)).astype(bf16)
    dy = (dgated * swish).astype(bf16)
    x = acts[:, :DI].astype(f32)
    grad_skip = head_sums(jnp.sum(dy.astype(f32) * x, axis=0, keepdims=True))[0]
    dheld = held_grad(acts, cum_wide, dy)
    leave = shifted(dheld.astype(bf16), "seq", -1)
    for _ in range(lax.axis_size("seq") - 2):
        leave = shifted((totals_wide * leave.astype(f32) + dheld).astype(bf16), "seq", -1)
    grad_wout = rows_dot((q * gate_g).astype(bf16), dob)
    dx, dstep_t, dcum, db, dc = mix_grad(dy, acts, cum_wide, cum_t, dt_t, incoming, skip_wide)
    dstep = dstep_t.reshape(H, t).T
    dcum = dcum[:, :H] - dstep * dt
    db = db + cols_dot(weighted, leave)
    dweighted = dot(acts[:, DI : DI + N], leave)
    dx = dx + dweighted * factor_wide
    to_end = jnp.exp(cum[-1:] - cum)
    dfactor = head_sums(dweighted * x)
    dstep = dstep + dfactor * to_end
    dend = dfactor * dt * to_end
    at_total = head_sums(jnp.sum(leave.astype(f32) * incoming.astype(f32), axis=0, keepdims=True))
    last = jnp.sum(dend, axis=0, keepdims=True) + at_total * totals
    is_end = lax.broadcasted_iota(jnp.int32, (t, 1), 0) == t - 1
    dcum = dcum - dend + jnp.where(is_end, last, 0.0)
    drate = rows_dot(lower_triangle(t), dcum, precision=PRECISE)
    rates = -jnp.exp(log_rate)
    dstep = dstep + drate * rates
    grad_alog = jnp.sum(drate * dt, axis=0) * rates[0]
    draw = dstep * jax.nn.sigmoid(projected[:, DI + CH :].astype(f32) + bias_dt)
    grad_dtb = jnp.sum(draw, axis=0)
    dconv = jnp.concatenate([dx, db, dc], axis=1) * silu_slope(conv)
    edge = shifted(dconv[:8], "seq", -1)
    grad_cb = jnp.sum(dconv, axis=0)
    grad_cw = jnp.stack([jnp.sum(dconv * padded[k : k + t].astype(f32), axis=0) for k in range(CONVK)])
    ext = jnp.concatenate([dconv, edge[: CONVK - 1]], axis=0)
    dxbc = jnp.zeros((t, CH), f32)
    for k in range(CONVK):
        dxbc = dxbc + conv_w[k : k + 1] * ext[CONVK - 1 - k : CONVK - 1 - k + t]
    dproj = jnp.concatenate([dz, dxbc.astype(bf16), draw.astype(bf16)], axis=1)
    inv_rms, normed = rms_parts(layer_in.astype(f32))
    grad_win = rows_dot((normed * norm_g).astype(bf16), dproj)
    dun = cols_dot(dproj, w_in)
    grad_norm_gain = jnp.sum(dun * normed, axis=0)
    dnorm = dun * norm_g
    grad_u = grad_v.astype(f32) + inv_rms * (dnorm - normed * jnp.mean(dnorm * normed, axis=-1, keepdims=True))
    return grad_u, grad_win, grad_wout, (grad_cw, grad_cb, grad_norm_gain, grad_gate_gain, grad_dtb, grad_alog, grad_skip)


def reduced(grad):
    return lax.psum_scatter(grad.astype(bf16), WEIGHT_AXES, scatter_dimension=0, tiled=True)


def body(tokens, cotangent, in_weight, out_weight, conv_weight, conv_bias, norm_gain, gate_gain, dt_bias, a_log, d_skip):
    first = lax.axis_index("section") == 0
    share_count = lax.axis_size("dp") * lax.axis_size("seq")
    share_idx = lax.axis_index("dp") * lax.axis_size("seq") + lax.axis_index("seq")

    def pick(a, b):
        return jnp.where(first, a, b)

    mine = (in_weight[0], out_weight[0])
    theirs = tuple(swapped(w) for w in mine)
    small = jnp.concatenate([conv_weight[0].reshape(-1), conv_bias[0], norm_gain[0], gate_gain[0]])
    smalls = lax.all_gather(small, ("section",) + WEIGHT_AXES, axis=0, tiled=False)
    smalls = smalls.reshape(2, share_count, small.shape[0]).astype(f32)
    heads = jnp.stack([dt_bias[0], a_log[0], d_skip[0]])
    other_heads = swapped(heads)
    head_params = (pick(heads, other_heads), pick(other_heads, heads))
    c_loc, n_loc, g_loc = conv_bias.shape[1], norm_gain.shape[1], gate_gain.shape[1]
    weights = []
    for layer in range(2):
        shards = tuple(pick(m, o) if layer == 0 else pick(o, m) for m, o in zip(mine, theirs))
        w_in, w_out = (lax.all_gather(s, WEIGHT_AXES, axis=0, tiled=True) for s in shards)
        own = smalls[layer]
        cuts = [0, CONVK * c_loc, CONVK * c_loc + c_loc, CONVK * c_loc + c_loc + n_loc]
        conv_w = own[:, : cuts[1]].reshape(share_count, CONVK, c_loc).transpose(1, 0, 2).reshape(CONVK, CH)
        conv_b = own[:, cuts[1] : cuts[2]].reshape(1, CH)
        norm_g = own[:, cuts[2] : cuts[3]].reshape(1, D)
        gate_g = own[:, cuts[3] :].reshape(1, DI)
        hp = head_params[layer]
        weights.append((w_in, w_out, conv_w, conv_b, norm_g, gate_g, hp[0:1], hp[1:2], hp[2:3]))

    stream = pick(tokens[0, 0], tokens[1, 0])
    acts, kept = [], []
    for layer in range(2):
        stream, saved = layer_forward(stream, weights[layer])
        acts.append(stream)
        kept.append(saved)
    grad = pick(cotangent[0, 0], cotangent[1, 0])
    grads, shares, packs = [None, None], [None, None], [None, None]
    for layer in (1, 0):
        grad, grad_win, grad_wout, rest = layer_backward(grad, kept[layer], weights[layer])
        grads[layer] = grad
        shares[layer] = (reduced(grad_win), reduced(grad_wout))
        packs[layer] = jnp.concatenate([r.reshape(-1) for r in rest])
        grad = grad.astype(bf16)

    def finish(low, high):
        own = pick(low, high)
        return own, swapped(pick(high, low))

    def by_micro(low, high):
        own, other = finish(low, high)
        return jnp.stack([pick(own, other), pick(other, own)])[None, :, None]

    act_out = by_micro(*acts)
    grad_out = by_micro(*grads)
    sums = []
    for low, high in zip(*shares):
        own, other = finish(low, high)
        sums.append((own.astype(f32) + other.astype(f32))[None])
    totals = lax.psum(jnp.stack(packs), WEIGHT_AXES)
    own, other = finish(totals[0], totals[1])
    total = own + other
    sizes = [CONVK * CH, CH, D, DI, H, H, H]
    parts, start = [], 0
    for size in sizes:
        parts.append(total[start : start + size])
        start += size
    share = lambda a, width: lax.dynamic_slice_in_dim(a, share_idx * width, width, axis=a.ndim - 1)
    return (
        act_out,
        grad_out,
        sums[0],
        sums[1],
        share(parts[0].reshape(CONVK, CH), c_loc)[None],
        share(parts[1], c_loc)[None],
        share(parts[2], n_loc)[None],
        share(parts[3], g_loc)[None],
        parts[4][None],
        parts[5][None],
        parts[6][None],
    )


def solution(mesh):
    in_specs = (
        P(None, "dp", "seq", None),
        P(None, "dp", "seq", None),
        P("section", ("dp", "seq"), None),
        P("section", ("dp", "seq"), None),
        P("section", None, ("dp", "seq")),
        P("section", ("dp", "seq")),
        P("section", ("dp", "seq")),
        P("section", ("dp", "seq")),
        P("section", None),
        P("section", None),
        P("section", None),
    )
    out_specs = (
        P("section", None, "dp", "seq", None),
        P("section", None, "dp", "seq", None),
        P("section", ("dp", "seq"), None),
        P("section", ("dp", "seq"), None),
        P("section", None, ("dp", "seq")),
        P("section", ("dp", "seq")),
        P("section", ("dp", "seq")),
        P("section", ("dp", "seq")),
        P("section", None),
        P("section", None),
        P("section", None),
    )
    return jax.shard_map(body, mesh=mesh, in_specs=in_specs, out_specs=out_specs, check_vma=False)
```

time: 1450 us -> 836 us (0.58)
  local copies, waits for them, and re-layouts: 312 us -> 28.9 us
  other arithmetic: 250 us -> 57.4 us
  blocking collectives: 179 us -> 41.1 us
  matrix products: 139 us -> 70.6 us
  Pallas kernels: 0 us -> 53.3 us
  waiting for transfers between devices: 460 us -> 498 us
    ppermute x28 -> x16, waiting for transfers between devices: 332 us -> 91.8 us  [shifted(): return lax.ppermute(x, axis, pairs)]
    reduce_scatter x1 -> x4, waiting for transfers between devices: 77.1 us -> 287 us  [reduced(): lax.psum_scatter(grad.astype(bf16), WEIGHT_AXES, scatter_dimension=0, til...]
    all_gather x2 -> x0, blocking collectives: 117 us -> none  [the longest x1 60.9 us: body(): lax.all_gather(own_shards[4], ('dp', 'seq'), axis=0, tiled=True)]
    scatter-add x10 -> x0, local copies, waits for them, and re-layouts: 69.7 us -> none  [the longest x8 68.3 us: back_second(): grad_pad.at[k:k + tok_rows].add(conv_w[k].astype(jnp.float32) * grad_conv)]
    dot_general x40 -> x36, matrix products: 139 us -> 70.6 us  [dot(): lax.dot_general(left, right, (dims, ((), ())), preferred_element_type=f32...]
    another operation x79 -> x11, local copies, waits for them, and re-layouts: 67.2 us -> 0.87 us  [the longest x2 0.69 us: body(): totals = lax.psum(jnp.stack(packs), WEIGHT_AXES)]
    pallas_call x0 -> x8, Pallas kernels: none -> 53.3 us  [the longest x2 22.2 us: mix_grad(): call(mix_grad_kernel, (shaped(t, DI), shaped(PAIRS, 2, t), shaped(t, PAIR...]
    unnamed x7 -> x9, waiting for transfers between devices: 50.6 us -> 0.81 us
  transfers between devices with their start and end apart: 33 -> 33, of which waited for: 24 -> 24; matrix products, arithmetic and copies ran while one was open for 15% -> 10% of each run, Pallas kernels for 0% -> 5%
where the time goes in v1:
time: 836 us; the launch traced here: 825 us
  waiting for transfers between devices  498 us (60%)
  matrix products  70.6 us (8%)
  starting transfers between devices  59.5 us (7%)
  other arithmetic  57.4 us (7%)
  Pallas kernels  53.3 us (6%)
  blocking collectives  41.1 us (5%)
  local copies, waits for them, and re-layouts  28.9 us (3%)
  between operations  16.7 us (2%)
    reduce_scatter x4, waiting for transfers between devices, reduced(): lax.psum_scatter(grad.astype(bf16), WEIGHT_AXES, scatter_dimension=0, til...  287 us
    ppermute x16, waiting for transfers between devices, shifted(): return lax.ppermute(x, axis, pairs)  91.8 us
    dot_general x36, matrix products, dot(): lax.dot_general(left, right, (dims, ((), ())), preferred_element_type=f32...  70.6 us
    psum x1, waiting for transfers between devices, body(): totals = lax.psum(jnp.stack(packs), WEIGHT_AXES)  49.5 us
    ppermute x16, starting transfers between devices, shifted(): return lax.ppermute(x, axis, pairs)  44.6 us
    unnamed x1, blocking collectives  41.1 us
    all_gather x4, waiting for transfers between devices, body(): lax.all_gather(s, WEIGHT_AXES, axis=0, tiled=True)  39.9 us
    ppermute x8, waiting for transfers between devices, swapped(): return lax.ppermute(x, 'section', [(0, 1), (1, 0)])  28.1 us
  transfers between devices with their start and end apart: 33, of which 24 were waited for; matrix products, arithmetic and copies ran while one was open for 10% of the time, Pallas kernels for 5%

profile of v1, /device:TPU:0, one launch (start us, length us, event | category | flops | bytes accessed | tf_op | source)
XLA Modules:
  0.0 825.1 jit_solution(11955550557411507996)
XLA Ops:
  10.3 8.0 collective-permute-done
  22.1 3.6 collective-permute-done.6
  30.4 41.1 %all-reduce = bf16[22528]{0:T(1024)(128)(2,1)S(1)} all-reduce(bf16[22528]{0:T(1024)(128)(2,1)S(1)} %dynamic-update-slice), channel_id=2, replica_groups=mesh['section'=2,'dp'=4,'seq'=4] {'section','dp','seq'}, use_global_device_ids=true, to_apply=%add | all-reduce | flops 22528 | bytes 90112
  73.1 5.3 all-gather.6.cloned.1.call-done
  78.4 4.2 convolution_convert_fusion.3
  82.6 3.4 collective-permute-start.1
  89.6 4.3 collective-permute-start.3
  95.9 7.9 collective-permute-done.3
  104.6 4.4 collective-permute-start.4
  109.3 14.9 %collective-permute-done.4 = bf16[128,1536]{1,0:T(8,128)(2,1)S(1)} collective-permute-done((bf16[128,1536]{1,0:T(8,128)(2,1)}, bf16[128,1536]{1,0:T(8,128)(2,1)S(1)}, u32[]{:S(2)}, u32[]{:S(2)}) %collective-permute-start.4) | collective-permute-done | bytes 393248 | tf_op jit(solution)/shard_map/ppermute | solution.py:43
  125.1 4.3 collective-permute-start.5
  131.2 4.7 shard_map.194.part_ref
  139.2 4.3 shard_map.195
  150.0 34.6 %all-gather.10.cloned.1.call-done = bf16[768,3352]{1,0:T(8,128)(2,1)} async-done(((bf16[48,3352]{1,0:T(8,128)(2,1)}), bf16[768,3352]{1,0:T(8,128)(2,1)}) %all-gather.10.cloned.1.call-update) | async-done | bytes 5148688 | tf_op jit(solution)/shard_map/all_gather | solution.py:388
  184.6 4.2 convolution_convert_fusion.2
  188.8 3.7 collective-permute-start.7
  200.3 9.5 %collective-permute-done.8 = bf16[128,1536]{1,0:T(8,128)(2,1)S(1)} collective-permute-done((bf16[128,1536]{1,0:T(8,128)(2,1)S(1)}, bf16[128,1536]{1,0:T(8,128)(2,1)S(1)}, u32[]{:S(2)}, u32[]{:S(2)}) %collective-permute-start.8) | collective-permute-done | bytes 393248 | tf_op jit(solution)/shard_map/ppermute | solution.py:43
  210.7 5.1 collective-permute-start.9
  216.1 13.3 %collective-permute-done.9 = bf16[128,1536]{1,0:T(8,128)(2,1)} collective-permute-done((bf16[128,1536]{1,0:T(8,128)(2,1)}, bf16[128,1536]{1,0:T(8,128)(2,1)}, u32[]{:S(2)}, u32[]{:S(2)}) %collective-permute-start.9) | collective-permute-done | bytes 393248 | tf_op jit(solution)/shard_map/ppermute | solution.py:43
  231.5 5.1 collective-permute-start.10
  242.2 4.7 shard_map.196.part_ref
  246.9 6.9 shard_map.197
  253.8 3.4 multiply_reduce_fusion.4
  257.3 4.1 multiply_reduce_fusion
  261.4 4.0 fusion.46
  265.4 5.2 shard_map.199
  272.0 10.7 %collective-permute-done.12 = bf16[128,1536]{1,0:T(8,128)(2,1)S(1)} collective-permute-done((bf16[128,1536]{1,0:T(8,128)(2,1)S(1)}, bf16[128,1536]{1,0:T(8,128)(2,1)S(1)}, u32[]{:S(2)}, u32[]{:S(2)}) %collective-permute-start.12) | collective-permute-done | bytes 393248 | tf_op jit(solution)/shard_map/ppermute | solution.py:43
  284.0 9.7 %collective-permute-done.13 = bf16[128,1536]{1,0:T(8,128)(2,1)S(1)} collective-permute-done((bf16[128,1536]{1,0:T(8,128)(2,1)S(1)}, bf16[128,1536]{1,0:T(8,128)(2,1)S(1)}, u32[]{:S(2)}, u32[]{:S(2)}) %collective-permute-start.13) | collective-permute-done | bytes 393248 | tf_op jit(solution)/shard_map/ppermute | solution.py:43
  296.9 11.4 %shard_map.198 = (f32[256,1536]{1,0:T(8,128)S(1)}, f32[12,2,256]{2,1,0:T(2,128)S(1)}, f32[256,128]{1,0:T(8,128)S(1)}, f32[256,128]{1,0:T(8,128)S(1)}, f32[256,128]{1,0:T(8,128)S(1)}) custom-call(bf16[256,1536]{1,0:T(8,128)(2,1)S(1)} %get-tuple-element.108.dy_ref, bf16[256,1792]{1,0:T(8,128)(2,1)S(1)} %multiply_convert_fusion.x_ref.b_ref.c_ref, ...), custom_call_target="tpu_custom_call" | custom-call | tf_op jit(solution)/shard_map/pallas_call | solution.py:238
  322.9 4.2 fusion.222
  330.0 3.9 collective-permute-done.15
  334.8 4.6 fusion.77
  345.8 5.2 shard_map.201
  352.5 8.8 %collective-permute-done.16 = bf16[128,1536]{1,0:T(8,128)(2,1)S(1)} collective-permute-done((bf16[128,1536]{1,0:T(8,128)(2,1)S(1)}, bf16[128,1536]{1,0:T(8,128)(2,1)S(1)}, u32[]{:S(2)}, u32[]{:S(2)}) %collective-permute-start.16) | collective-permute-done | bytes 393248 | tf_op jit(solution)/shard_map/ppermute | solution.py:43
  363.0 8.9 %collective-permute-done.17 = bf16[128,1536]{1,0:T(8,128)(2,1)S(1)} collective-permute-done((bf16[128,1536]{1,0:T(8,128)(2,1)S(1)}, bf16[128,1536]{1,0:T(8,128)(2,1)S(1)}, u32[]{:S(2)}, u32[]{:S(2)}) %collective-permute-start.17) | collective-permute-done | bytes 393248 | tf_op jit(solution)/shard_map/ppermute | solution.py:43
  377.8 10.8 %shard_map.200 = (f32[256,1536]{1,0:T(8,128)S(1)}, f32[12,2,256]{2,1,0:T(2,128)S(1)}, f32[256,128]{1,0:T(8,128)S(1)}, f32[256,128]{1,0:T(8,128)S(1)}, f32[256,128]{1,0:T(8,128)S(1)}) custom-call(bf16[256,1536]{1,0:T(8,128)(2,1)S(1)} %copy-done.7, bf16[256,1792]{1,0:T(8,128)(2,1)S(1)} %multiply_convert_fusion.1.x_ref.b_ref.c_ref, ...), custom_call_target="tpu_custom_call" | custom-call | tf_op jit(solution)/shard_map/pallas_call | solution.py:238
  399.4 3.5 fusion.221
  410.9 6.0 fusion.84
  423.1 3.5 convolution_convert_fusion.5
  427.9 5.2 convolution_convert_fusion
  434.3 5.2 convolution_convert_fusion.1
  444.9 10.5 %collective-permute-done.11 = bf16[256,768]{1,0:T(8,128)(2,1)S(1)} collective-permute-done((bf16[256,768]{1,0:T(8,128)(2,1)}, bf16[256,768]{1,0:T(8,128)(2,1)S(1)}, u32[]{:S(2)}, u32[]{:S(2)}) %collective-permute-start.11) | collective-permute-done | bytes 393248 | tf_op jit(solution)/shard_map/ppermute | solution.py:47
  459.1 49.5 %all-reduce.3.cloned.1.call-done = f32[2,11336]{1,0:T(2,128)} async-done(((f32[2,11336]{1,0:T(2,128)}), f32[2,11336]{1,0:T(2,128)}) %all-reduce.3.cloned.1.call-update) | async-done | bytes 90704 | tf_op jit(solution)/shard_map/psum | solution.py:427
  518.5 57.4 %reduce-scatter.11.cloned.1.call-done = bf16[96,768]{1,0:T(8,128)(2,1)} async-done(((bf16[1536,768]{1,0:T(8,128)(2,1)}), bf16[96,768]{1,0:T(8,128)(2,1)}) %reduce-scatter.11.cloned.1.call-update) | async-done | bytes 147472 | tf_op jit(solution)/shard_map/reduce_scatter | solution.py:365
  575.9 65.8 %reduce-scatter.9.cloned.1.call-done = bf16[96,768]{1,0:T(8,128)(2,1)} async-done(((bf16[1536,768]{1,0:T(8,128)(2,1)}), bf16[96,768]{1,0:T(8,128)(2,1)}) %reduce-scatter.9.cloned.1.call-update) | async-done | bytes 147472 | tf_op jit(solution)/shard_map/reduce_scatter | solution.py:365
  644.1 81.0 %reduce-scatter.7.cloned.1.call-done = bf16[48,3352]{1,0:T(8,128)(2,1)} async-done(((bf16[768,3352]{1,0:T(8,128)(2,1)}), bf16[48,3352]{1,0:T(8,128)(2,1)}) %reduce-scatter.7.cloned.1.call-update) | async-done | bytes 321808 | tf_op jit(solution)/shard_map/reduce_scatter | solution.py:365
  725.1 83.2 %reduce-scatter.5.cloned.1.call-done = bf16[48,3352]{1,0:T(8,128)(2,1)} async-done(((bf16[768,3352]{1,0:T(8,128)(2,1)}), bf16[48,3352]{1,0:T(8,128)(2,1)}) %reduce-scatter.5.cloned.1.call-update) | async-done | bytes 321808 | tf_op jit(solution)/shard_map/reduce_scatter | solution.py:365
  813.0 4.4 collective-permute-done.21
  (562 shorter events, 140.9 us)
Async XLA Ops:
  7.3 65.2 %copy-start.63 = (bf16[2,1,256,768]{3,2,1,0:T(8,128)(2,1)S(1)}, bf16[2,1,256,768]{3,2,1,0:T(8,128)(2,1)}, u32[]{:S(2)}) copy-start(bf16[2,1,256,768]{3,2,1,0:T(8,128)(2,1)} %param.11) | copy-start | bytes 2359300
  7.3 71.1 %all-gather.6.cloned.1.call-start = ((), (), s32[]{:S(2)}) async-start(), calls=%async_computation.4 | async-start | bytes 5640192 | tf_op jit(solution)/shard_map/all_gather | solution.py:388
  7.3 11.0 %collective-permute-start = (bf16[48,3352]{1,0:T(8,128)(2,1)}, bf16[48,3352]{1,0:T(8,128)(2,1)S(1)}, u32[]{:S(2)}, u32[]{:S(2)}) collective-permute-start(bf16[48,3352]{1,0:T(8,128)(2,1)} %bitcast.163), channel_id=1, source_target_pairs={{0,16},{16,0},{1,17},{17,1},{2,18},{18,2},{3,19},{19,3},{4,20},{20... | collective-permute-start | bytes 965384 | tf_op jit(solution)/shard_map/ppermute | solution.py:47
  20.2 126.7 %all-gather.8.cloned.1.call-start = ((), (), s32[]{:S(2)}) async-start(), calls=%async_computation.5 | async-start | bytes 2506752 | tf_op jit(solution)/shard_map/all_gather | solution.py:388
  20.3 5.4 collective-permute-start.6
  27.4 157.2 %all-gather.10.cloned.1.call-start = ((), (), s32[]{:S(2)}) async-start(), calls=%async_computation.6 | async-start | bytes 5640192 | tf_op jit(solution)/shard_map/all_gather | solution.py:388
  28.1 229.2 %all-gather.12.cloned.1.call-start = ((), (), s32[]{:S(2)}) async-start(), calls=%async_computation.7 | async-start | bytes 2506752 | tf_op jit(solution)/shard_map/all_gather | solution.py:388
  28.2 44.8 %collective-permute-start.2 = (f32[3,24]{1,0:T(4,128)S(1)}, f32[3,24]{1,0:T(4,128)S(1)}, u32[]{:S(2)}, u32[]{:S(2)}) collective-permute-start(f32[3,24]{1,0:T(4,128)S(1)} %pad_maximum_fusion.14), channel_id=1, source_target_pairs={{0,16},{16,0},{1,17},{17,1},{2,18},{18,2},{3,19},{19,3},{4,20},{20... | collective-permute-start | bytes 872 | tf_op jit(solution)/shard_map/ppermute | solution.py:47
  72.4 120.7 %copy-start.106 = (pred[1536]{0:T(1024)(128)(4,1)}, pred[1536]{0:T(1024)(128)(4,1)S(1)}, u32[]{:S(2)}) copy-start(pred[1536]{0:T(1024)(128)(4,1)S(1)} %fusion.202) | copy-start | bytes 4612
  72.5 168.1 %copy-start.66 = (s32[1536]{0:T(1024)}, s32[1536]{0:T(1024)S(1)}, u32[]{:S(2)}) copy-start(s32[1536]{0:T(1024)S(1)} %iota_shift-right-logical_fusion) | copy-start | bytes 18436
  72.7 74.2 %copy-start.41 = (bf16[1,1,256,768]{3,2,1,0:T(8,128)(2,1)}, bf16[1,1,256,768]{3,2,1,0:T(8,128)(2,1)S(1)}, u32[]{:S(2)}) copy-start(bf16[1,1,256,768]{3,2,1,0:T(8,128)(2,1)S(1)} %get-tuple-element.117) | copy-start | bytes 1179652
  82.6 5.2 collective-permute-start.1
  89.6 14.2 %collective-permute-start.3 = (bf16[128,1536]{1,0:T(8,128)(2,1)S(1)}, bf16[128,1536]{1,0:T(8,128)(2,1)S(1)}, u32[]{:S(2)}, u32[]{:S(2)}) collective-permute-start(bf16[128,1536]{1,0:T(8,128)(2,1)S(1)} %get-tuple-element.147), channel_id=1, source_target_pairs={{0,1},{1,2},{2,3},{4,5},{5,6},{6,7},{8,9},{9,10},{10,11},{12,13},{... | collective-permute-start | bytes 1179656 | tf_op jit(solution)/shard_map/ppermute | solution.py:43
  94.6 52.3 %copy-start.99 = (f32[1536]{0:T(1024)}, f32[1536]{0:T(1024)S(1)}, u32[]{:S(2)}) copy-start(f32[1536]{0:T(1024)S(1)} %mul.661) | copy-start | bytes 18436
  94.7 89.9 %copy-start.123 = (f32[768]{0:T(1024)}, f32[768]{0:T(1024)S(1)}, u32[]{:S(2)}) copy-start(f32[768]{0:T(1024)S(1)} %mul.669) | copy-start | bytes 9220
  95.4 99.8 %copy-start.88 = (f32[1792]{0:T(1024)}, f32[1792]{0:T(1024)S(1)}, u32[]{:S(2)}) copy-start(f32[1792]{0:T(1024)S(1)} %mul.664) | copy-start | bytes 21508
  95.5 99.7 %copy-start.90 = (f32[1792]{0:T(1024)}, f32[1792]{0:T(1024)S(1)}, u32[]{:S(2)}) copy-start(f32[1792]{0:T(1024)S(1)} %mul.679) | copy-start | bytes 21508
  95.6 99.6 %copy-start.92 = (f32[1792]{0:T(1024)}, f32[1792]{0:T(1024)S(1)}, u32[]{:S(2)}) copy-start(f32[1792]{0:T(1024)S(1)} %mul.676) | copy-start | bytes 21508
  95.7 99.6 %copy-start.94 = (f32[1792]{0:T(1024)}, f32[1792]{0:T(1024)S(1)}, u32[]{:S(2)}) copy-start(f32[1792]{0:T(1024)S(1)} %mul.673) | copy-start | bytes 21508
  104.6 19.6 %collective-permute-start.4 = (bf16[128,1536]{1,0:T(8,128)(2,1)}, bf16[128,1536]{1,0:T(8,128)(2,1)S(1)}, u32[]{:S(2)}, u32[]{:S(2)}) collective-permute-start(bf16[128,1536]{1,0:T(8,128)(2,1)} %add_convert_fusion.7), channel_id=1, source_target_pairs={{0,1},{1,2},{2,3},{4,5},{5,6},{6,7},{8,9},{9,10},{10,11},{12,13},{... | collective-permute-start | bytes 1179656 | tf_op jit(solution)/shard_map/ppermute | solution.py:43
  109.0 83.5 %copy-start.164 = (f32[24]{0:T(128)}, f32[24]{0:T(128)S(1)}, u32[]{:S(2)}) copy-start(f32[24]{0:T(128)S(1)} %get-tuple-element.144) | copy-start | bytes 292
  109.0 84.1 %copy-start.136 = (f32[24]{0:T(128)}, f32[24]{0:T(128)S(1)}, u32[]{:S(2)}) copy-start(f32[24]{0:T(128)S(1)} %get-tuple-element.143) | copy-start | bytes 292
  109.3 399.3 %all-reduce.3.cloned.1.call-start = ((), (), s32[]{:S(2)}) async-start(), calls=%async_computation.12 | async-start | bytes 182272 | tf_op jit(solution)/shard_map/psum | solution.py:427
  125.1 14.1 %collective-permute-start.5 = (bf16[128,1536]{1,0:T(8,128)(2,1)}, bf16[128,1536]{1,0:T(8,128)(2,1)S(1)}, u32[]{:S(2)}, u32[]{:S(2)}) collective-permute-start(bf16[128,1536]{1,0:T(8,128)(2,1)} %add_convert_fusion.6), channel_id=1, source_target_pairs={{0,1},{1,2},{2,3},{4,5},{5,6},{6,7},{8,9},{9,10},{10,11},{12,13},{... | collective-permute-start | bytes 1179656 | tf_op jit(solution)/shard_map/ppermute | solution.py:43
  188.8 6.4 collective-permute-start.7
  196.9 12.9 %collective-permute-start.8 = (bf16[128,1536]{1,0:T(8,128)(2,1)S(1)}, bf16[128,1536]{1,0:T(8,128)(2,1)S(1)}, u32[]{:S(2)}, u32[]{:S(2)}) collective-permute-start(bf16[128,1536]{1,0:T(8,128)(2,1)S(1)} %get-tuple-element.151), channel_id=1, source_target_pairs={{0,1},{1,2},{2,3},{4,5},{5,6},{6,7},{8,9},{9,10},{10,11},{12,13},{... | collective-permute-start | bytes 1179656 | tf_op jit(solution)/shard_map/ppermute | solution.py:43
  210.7 18.7 %collective-permute-start.9 = (bf16[128,1536]{1,0:T(8,128)(2,1)}, bf16[128,1536]{1,0:T(8,128)(2,1)}, u32[]{:S(2)}, u32[]{:S(2)}) collective-permute-start(bf16[128,1536]{1,0:T(8,128)(2,1)} %add_convert_fusion.5), channel_id=1, source_target_pairs={{0,1},{1,2},{2,3},{4,5},{5,6},{6,7},{8,9},{9,10},{10,11},{12,13},{... | collective-permute-start | bytes 1179656 | tf_op jit(solution)/shard_map/ppermute | solution.py:43
  215.9 45.4 %copy-start.73 = (f32[1536]{0:T(1024)}, f32[1536]{0:T(1024)S(1)}, u32[]{:S(2)}) copy-start(f32[1536]{0:T(1024)S(1)} %mul.696) | copy-start | bytes 18436
  231.5 15.4 %collective-permute-start.10 = (bf16[128,1536]{1,0:T(8,128)(2,1)}, bf16[128,1536]{1,0:T(8,128)(2,1)}, u32[]{:S(2)}, u32[]{:S(2)}) collective-permute-start(bf16[128,1536]{1,0:T(8,128)(2,1)} %add_convert_fusion.4), channel_id=1, source_target_pairs={{0,1},{1,2},{2,3},{4,5},{5,6},{6,7},{8,9},{9,10},{10,11},{12,13},{... | collective-permute-start | bytes 1179656 | tf_op jit(solution)/shard_map/ppermute | solution.py:43
  270.7 12.0 %collective-permute-start.12 = (bf16[128,1536]{1,0:T(8,128)(2,1)S(1)}, bf16[128,1536]{1,0:T(8,128)(2,1)S(1)}, u32[]{:S(2)}, u32[]{:S(2)}) collective-permute-start(bf16[128,1536]{1,0:T(8,128)(2,1)S(1)} %convert_element_type.309), channel_id=1, source_target_pairs={{1,0},{2,1},{3,2},{5,4},{6,5},{7,6},{9,8},{10,9},{11,10},{13,12},{... | collective-permute-start | bytes 1179656 | tf_op jit(solution)/shard_map/ppermute | solution.py:43
  282.7 11.0 %collective-permute-start.13 = (bf16[128,1536]{1,0:T(8,128)(2,1)S(1)}, bf16[128,1536]{1,0:T(8,128)(2,1)S(1)}, u32[]{:S(2)}, u32[]{:S(2)}) collective-permute-start(bf16[128,1536]{1,0:T(8,128)(2,1)S(1)} %add_convert_fusion.3), channel_id=1, source_target_pairs={{1,0},{2,1},{3,2},{5,4},{6,5},{7,6},{9,8},{10,9},{11,10},{13,12},{... | collective-permute-start | bytes 1179656 | tf_op jit(solution)/shard_map/ppermute | solution.py:43
  294.6 17.6 %collective-permute-start.14 = (bf16[128,1536]{1,0:T(8,128)(2,1)}, bf16[128,1536]{1,0:T(8,128)(2,1)}, u32[]{:S(2)}, u32[]{:S(2)}) collective-permute-start(bf16[128,1536]{1,0:T(8,128)(2,1)} %add_convert_fusion.2), channel_id=1, source_target_pairs={{1,0},{2,1},{3,2},{5,4},{6,5},{7,6},{9,8},{10,9},{11,10},{13,12},{... | collective-permute-start | bytes 1179656 | tf_op jit(solution)/shard_map/ppermute | solution.py:43
  327.2 6.7 collective-permute-start.15
  351.1 10.2 %collective-permute-start.16 = (bf16[128,1536]{1,0:T(8,128)(2,1)S(1)}, bf16[128,1536]{1,0:T(8,128)(2,1)S(1)}, u32[]{:S(2)}, u32[]{:S(2)}) collective-permute-start(bf16[128,1536]{1,0:T(8,128)(2,1)S(1)} %convert_element_type.322), channel_id=1, source_target_pairs={{1,0},{2,1},{3,2},{5,4},{6,5},{7,6},{9,8},{10,9},{11,10},{13,12},{... | collective-permute-start | bytes 1179656 | tf_op jit(solution)/shard_map/ppermute | solution.py:43
  361.4 10.5 %collective-permute-start.17 = (bf16[128,1536]{1,0:T(8,128)(2,1)S(1)}, bf16[128,1536]{1,0:T(8,128)(2,1)S(1)}, u32[]{:S(2)}, u32[]{:S(2)}) collective-permute-start(bf16[128,1536]{1,0:T(8,128)(2,1)S(1)} %add_convert_fusion.1), channel_id=1, source_target_pairs={{1,0},{2,1},{3,2},{5,4},{6,5},{7,6},{9,8},{10,9},{11,10},{13,12},{... | collective-permute-start | bytes 1179656 | tf_op jit(solution)/shard_map/ppermute | solution.py:43
  372.8 18.5 %collective-permute-start.18 = (bf16[128,1536]{1,0:T(8,128)(2,1)}, bf16[128,1536]{1,0:T(8,128)(2,1)}, u32[]{:S(2)}, u32[]{:S(2)}) collective-permute-start(bf16[128,1536]{1,0:T(8,128)(2,1)} %add_convert_fusion), channel_id=1, source_target_pairs={{1,0},{2,1},{3,2},{5,4},{6,5},{7,6},{9,8},{10,9},{11,10},{13,12},{... | collective-permute-start | bytes 1179656 | tf_op jit(solution)/shard_map/ppermute | solution.py:43
  403.0 7.0 collective-permute-start.19
  419.3 156.6 %reduce-scatter.11.cloned.1.call-start = ((), (), s32[]{:S(2)}) async-start(), calls=%async_computation.11 | async-start | bytes 2506752 | tf_op jit(solution)/shard_map/reduce_scatter | solution.py:365
  421.7 219.9 %reduce-scatter.9.cloned.1.call-start = ((), (), s32[]{:S(2)}) async-start(), calls=%async_computation.10 | async-start | bytes 2506752 | tf_op jit(solution)/shard_map/reduce_scatter | solution.py:365
  426.6 298.5 %reduce-scatter.7.cloned.1.call-start = ((), (), s32[]{:S(2)}) async-start(), calls=%async_computation.9 | async-start | bytes 5640192 | tf_op jit(solution)/shard_map/reduce_scatter | solution.py:365
  433.1 375.3 %reduce-scatter.5.cloned.1.call-start = ((), (), s32[]{:S(2)}) async-start(), calls=%async_computation.8 | async-start | bytes 5640192 | tf_op jit(solution)/shard_map/reduce_scatter | solution.py:365
  443.4 12.0 %collective-permute-start.11 = (bf16[256,768]{1,0:T(8,128)(2,1)}, bf16[256,768]{1,0:T(8,128)(2,1)S(1)}, u32[]{:S(2)}, u32[]{:S(2)}) collective-permute-start(bf16[256,768]{1,0:T(8,128)(2,1)} %get-tuple-element.153), channel_id=1, source_target_pairs={{0,16},{16,0},{1,17},{17,1},{2,18},{18,2},{3,19},{19,3},{4,20},{20... | collective-permute-start | bytes 1179656 | tf_op jit(solution)/shard_map/ppermute | solution.py:47
  457.5 59.6 %collective-permute-start.20 = (f32[256,768]{1,0:T(8,128)S(1)}, f32[256,768]{1,0:T(8,128)}, u32[]{:S(2)}, u32[]{:S(2)}) collective-permute-start(f32[256,768]{1,0:T(8,128)S(1)} %fusion.95), channel_id=1, source_target_pairs={{0,16},{16,0},{1,17},{17,1},{2,18},{18,2},{3,19},{19,3},{4,20},{20... | collective-permute-start | bytes 2359304 | tf_op jit(solution)/shard_map/ppermute | solution.py:47
  509.8 4.2 collective-permute-start.23
  642.6 169.6 %copy-start.64 = (bf16[96,768]{1,0:T(8,128)(2,1)S(1)}, bf16[96,768]{1,0:T(8,128)(2,1)}, u32[]{:S(2)}) copy-start(bf16[96,768]{1,0:T(8,128)(2,1)} %reduce-scatter.11.cloned.1.call-done) | copy-start | bytes 442372
  642.6 169.6 %copy-start.65 = (bf16[96,768]{1,0:T(8,128)(2,1)S(1)}, bf16[96,768]{1,0:T(8,128)(2,1)}, u32[]{:S(2)}) copy-start(bf16[96,768]{1,0:T(8,128)(2,1)} %reduce-scatter.9.cloned.1.call-done) | copy-start | bytes 442372
  642.6 169.6 %collective-permute-start.22 = (bf16[96,768]{1,0:T(8,128)(2,1)S(1)}, bf16[96,768]{1,0:T(8,128)(2,1)S(1)}, u32[]{:S(2)}, u32[]{:S(2)}) collective-permute-start(bf16[96,768]{1,0:T(8,128)(2,1)S(1)} %broadcast_select_fusion.5), channel_id=1, source_target_pairs={{0,16},{16,0},{1,17},{17,1},{2,18},{18,2},{3,19},{19,3},{4,20},{20... | collective-permute-start | bytes 442376 | tf_op jit(solution)/shard_map/ppermute | solution.py:47
  809.4 7.9 collective-permute-start.21
  (158 other events, 1192.2 us)
Sparse Core Ops, SparseCore 0:
  20.3 58.0 all-gather.5
  81.3 42.1 all-gather.7
  126.3 58.2 all-gather.9
  186.8 41.5 all-gather.11
  419.4 89.1 all-reduce.2
  512.7 63.1 reduce-scatter.10
  579.7 61.9 reduce-scatter.8
  646.2 78.8 reduce-scatter.6
  729.7 78.6 reduce-scatter.4

commit v2 on v1

--- a/solution.py
+++ b/solution.py
@@ -64,6 +64,66 @@
 def silu_slope(values):
     sigma = jax.nn.sigmoid(values)
     return sigma * (1.0 + values * (1.0 - sigma))
+
+
+def tied(*values):
+    return lax.optimization_barrier(values)
+
+
+class Halving:
+    def __init__(self, grad, late_dp, wire=bf16):
+        sizes = {a: lax.axis_size(a) for a in WEIGHT_AXES}
+        self.bits = [(a, b) for a in WEIGHT_AXES for b in reversed(range(sizes[a].bit_length() - 1))]
+        count = sizes["dp"] * sizes["seq"]
+        self.value = grad.astype(wire).reshape(count, grad.shape[0] // count, grad.shape[1])
+        dp = sorted(b for b in self.bits if b[0] == "dp")
+        seq = sorted(b for b in self.bits if b[0] == "seq")
+        self.order = dp[:1] + (seq + dp[1:] if late_dp else dp[1:] + seq)
+        self.wire = wire
+
+    def done(self):
+        return not self.order
+
+    def step(self):
+        if self.done():
+            return
+        axis, bit = self.order.pop(0)
+        place = self.bits.index((axis, bit))
+        del self.bits[place]
+        rows, cols = self.value.shape[1:]
+        halves = self.value.reshape(2**place, 2, 2 ** (len(self.bits) - place), rows, cols)
+        upper = (lax.axis_index(axis) >> bit) & 1 == 1
+        low, high = halves[:, 0], halves[:, 1]
+        keep = jnp.where(upper, high, low)
+        pairs = [(i, i ^ (1 << bit)) for i in range(lax.axis_size(axis))]
+        got = lax.ppermute(jnp.where(upper, low, high), axis, pairs)
+        total = keep.astype(f32) + got.astype(f32)
+        if self.bits:
+            total = total.astype(self.wire)
+        self.value = total.reshape(2 ** len(self.bits), rows, cols)
+
+
+class Queue:
+    def __init__(self):
+        self.streams = []
+
+    def add(self, grad, late_dp, wire=bf16):
+        stream = Halving(grad, late_dp, wire)
+        self.streams.append(stream)
+        return stream
+
+    def advance(self, *main):
+        live = [s for s in self.streams if not s.done()]
+        out = lax.optimization_barrier((main, tuple(s.value for s in live)))
+        for stream, value in zip(live, out[1]):
+            stream.value = value
+            stream.step()
+        return out[0] if len(main) > 1 else out[0][0]
+
+    def finish(self):
+        while any(not s.done() for s in self.streams):
+            for s in self.streams:
+                s.step()
 
 
 def lower_half(shape):
@@ -278,7 +338,7 @@
     for k in range(CONVK):
         conv = conv + conv_w[k : k + 1] * padded[k : k + t].astype(f32)
     acts = jax.nn.silu(conv).astype(bf16)
-    dt = jax.nn.softplus(projected[:, DI + CH :].astype(f32) + bias_dt)
+    dt = jax.nn.softplus(projected[:, DI + CH : E].astype(f32) + bias_dt)
     cum = dot(lower_triangle(t), dt * -jnp.exp(log_rate), precision=PRECISE)
     to_end = jnp.exp(cum[-1:] - cum)
     factor_wide = expand(dt * to_end)
@@ -287,13 +347,14 @@
     totals = jnp.exp(cum[-1:])
     totals_wide = expand(totals)
     incoming = shifted(states.astype(bf16), "seq", 1)
-    for _ in range(lax.axis_size("seq") - 2):
-        incoming = shifted((totals_wide * incoming.astype(f32) + states).astype(bf16), "seq", 1)
     cum_wide = expand(cum)
     cum_t = cum.T.reshape(PAIRS, 2, t)
     dt_t = dt.T.reshape(PAIRS, 2, t)
     skip_wide = expand(skip_gain)
     part = intra(acts, cum_wide, cum_t, dt_t, skip_wide)
+    incoming, part = tied(incoming, part)
+    for _ in range(lax.axis_size("seq") - 2):
+        incoming = shifted((totals_wide * incoming.astype(f32) + states).astype(bf16), "seq", 1)
     y = inter(acts, cum_wide, incoming, part)
     gate_cols = projected[:, :DI].astype(f32)
     _, q = rms_parts(y * jax.nn.silu(gate_cols))
@@ -302,7 +363,7 @@
     return mixed.astype(bf16), kept
 
 
-def layer_backward(grad_v, kept, weights):
+def layer_backward(grad_v, kept, weights, queue):
     w_in, w_out, conv_w, conv_b, norm_g, gate_g, bias_dt, log_rate, skip_gain = weights
     (layer_in, projected, padded, acts, conv, dt, cum, cum_wide, cum_t, dt_t, skip_wide, incoming, y, weighted, factor_wide, totals, totals_wide) = kept
     t = layer_in.shape[0]
@@ -320,10 +381,18 @@
     grad_skip = head_sums(jnp.sum(dy.astype(f32) * x, axis=0, keepdims=True))[0]
     dheld = held_grad(acts, cum_wide, dy)
     leave = shifted(dheld.astype(bf16), "seq", -1)
-    for _ in range(lax.axis_size("seq") - 2):
+    grad_wout = rows_dot((q * gate_g).astype(bf16), dob)
+    inv_rms, normed = rms_parts(layer_in.astype(f32))
+    un = (normed * norm_g).astype(bf16)
+    grad_win_z = rows_dot(un, dz)
+    wout_sum = queue.add(grad_wout, False)
+    winz_sum = queue.add(grad_win_z, True)
+    leave, dy = queue.advance(leave, dy)
+    for hop in range(lax.axis_size("seq") - 2):
         leave = shifted((totals_wide * leave.astype(f32) + dheld).astype(bf16), "seq", -1)
-    grad_wout = rows_dot((q * gate_g).astype(bf16), dob)
-    dx, dstep_t, dcum, db, dc = mix_grad(dy, acts, cum_wide, cum_t, dt_t, incoming, skip_wide)
+        if hop == 0:
+            dx, dstep_t, dcum, db, dc = mix_grad(dy, acts, cum_wide, cum_t, dt_t, incoming, skip_wide)
+            leave, dx = queue.advance(leave, dx)
     dstep = dstep_t.reshape(H, t).T
     dcum = dcum[:, :H] - dstep * dt
     db = db + cols_dot(weighted, leave)
@@ -341,7 +410,7 @@
     rates = -jnp.exp(log_rate)
     dstep = dstep + drate * rates
     grad_alog = jnp.sum(drate * dt, axis=0) * rates[0]
-    draw = dstep * jax.nn.sigmoid(projected[:, DI + CH :].astype(f32) + bias_dt)
+    draw = dstep * jax.nn.sigmoid(projected[:, DI + CH : E].astype(f32) + bias_dt)
     grad_dtb = jnp.sum(draw, axis=0)
     dconv = jnp.concatenate([dx, db, dc], axis=1) * silu_slope(conv)
     edge = shifted(dconv[:8], "seq", -1)
@@ -351,33 +420,49 @@
     dxbc = jnp.zeros((t, CH), f32)
     for k in range(CONVK):
         dxbc = dxbc + conv_w[k : k + 1] * ext[CONVK - 1 - k : CONVK - 1 - k + t]
-    dproj = jnp.concatenate([dz, dxbc.astype(bf16), draw.astype(bf16)], axis=1)
-    inv_rms, normed = rms_parts(layer_in.astype(f32))
-    grad_win = rows_dot((normed * norm_g).astype(bf16), dproj)
-    dun = cols_dot(dproj, w_in)
+    dxbc = dxbc.astype(bf16)
+    draw = draw.astype(bf16)
+    half = CH // 2
+    winx_sum = queue.add(rows_dot(un, dxbc[:, :half]), False)
+    wind_sum = queue.add(rows_dot(un, jnp.concatenate([dxbc[:, half:], draw], axis=1)), True)
+    dxbc = queue.advance(dxbc)
+    filler = jnp.zeros((t, w_in.shape[1] - E), bf16)
+    dun = cols_dot(jnp.concatenate([dz, dxbc, draw, filler], axis=1), w_in)
     grad_norm_gain = jnp.sum(dun * normed, axis=0)
     dnorm = dun * norm_g
     grad_u = grad_v.astype(f32) + inv_rms * (dnorm - normed * jnp.mean(dnorm * normed, axis=-1, keepdims=True))
-    return grad_u, grad_win, grad_wout, (grad_cw, grad_cb, grad_norm_gain, grad_gate_gain, grad_dtb, grad_alog, grad_skip)
-
-
-def reduced(grad):
-    return lax.psum_scatter(grad.astype(bf16), WEIGHT_AXES, scatter_dimension=0, tiled=True)
+    count = lax.axis_size("dp") * lax.axis_size("seq")
+    heads = jnp.concatenate([grad_dtb, grad_alog, grad_skip])
+    rest = jnp.concatenate(
+        [
+            grad_cw.reshape(CONVK, count, -1).transpose(1, 0, 2).reshape(count, -1),
+            grad_cb.reshape(count, -1),
+            grad_norm_gain.reshape(count, -1),
+            grad_gate_gain.reshape(count, -1),
+            jnp.broadcast_to(heads[None], (count, 3 * H)),
+        ],
+        axis=1,
+    )
+    rest_sum = queue.add(rest, False, f32)
+    return grad_u, (wout_sum, winz_sum, winx_sum, wind_sum, rest_sum)
 
 
 def body(tokens, cotangent, in_weight, out_weight, conv_weight, conv_bias, norm_gain, gate_gain, dt_bias, a_log, d_skip):
     first = lax.axis_index("section") == 0
     share_count = lax.axis_size("dp") * lax.axis_size("seq")
-    share_idx = lax.axis_index("dp") * lax.axis_size("seq") + lax.axis_index("seq")
 
     def pick(a, b):
         return jnp.where(first, a, b)
 
-    mine = (in_weight[0], out_weight[0])
+    small = jnp.concatenate([conv_weight[0].reshape(-1), conv_bias[0], norm_gain[0], gate_gain[0]])
+    rows = in_weight.shape[1]
+    extra = -E % 128
+    small_count = small.shape[0]
+    while rows * extra < small_count:
+        extra += 128
+    small = jnp.pad(small, (0, rows * extra - small_count)).reshape(rows, extra)
+    mine = (jnp.concatenate([in_weight[0], small], axis=1), out_weight[0])
     theirs = tuple(swapped(w) for w in mine)
-    small = jnp.concatenate([conv_weight[0].reshape(-1), conv_bias[0], norm_gain[0], gate_gain[0]])
-    smalls = lax.all_gather(small, ("section",) + WEIGHT_AXES, axis=0, tiled=False)
-    smalls = smalls.reshape(2, share_count, small.shape[0]).astype(f32)
     heads = jnp.stack([dt_bias[0], a_log[0], d_skip[0]])
     other_heads = swapped(heads)
     head_params = (pick(heads, other_heads), pick(other_heads, heads))
@@ -386,7 +471,7 @@
     for layer in range(2):
         shards = tuple(pick(m, o) if layer == 0 else pick(o, m) for m, o in zip(mine, theirs))
         w_in, w_out = (lax.all_gather(s, WEIGHT_AXES, axis=0, tiled=True) for s in shards)
-        own = smalls[layer]
+        own = w_in[:, E:].reshape(share_count, rows * extra)[:, :small_count].astype(f32)
         cuts = [0, CONVK * c_loc, CONVK * c_loc + c_loc, CONVK * c_loc + c_loc + n_loc]
         conv_w = own[:, : cuts[1]].reshape(share_count, CONVK, c_loc).transpose(1, 0, 2).reshape(CONVK, CH)
         conv_b = own[:, cuts[1] : cuts[2]].reshape(1, CH)
@@ -402,13 +487,15 @@
         acts.append(stream)
         kept.append(saved)
     grad = pick(cotangent[0, 0], cotangent[1, 0])
-    grads, shares, packs = [None, None], [None, None], [None, None]
+    grads, sums = [None, None], [None, None]
+    queue = Queue()
     for layer in (1, 0):
-        grad, grad_win, grad_wout, rest = layer_backward(grad, kept[layer], weights[layer])
+        grad, sums[layer] = layer_backward(grad, kept[layer], weights[layer], queue)
         grads[layer] = grad
-        shares[layer] = (reduced(grad_win), reduced(grad_wout))
-        packs[layer] = jnp.concatenate([r.reshape(-1) for r in rest])
         grad = grad.astype(bf16)
+        if layer == 1:
+            grad = queue.advance(grad)
+    queue.finish()
 
     def finish(low, high):
         own = pick(low, high)
@@ -420,28 +507,26 @@
 
     act_out = by_micro(*acts)
     grad_out = by_micro(*grads)
-    sums = []
-    for low, high in zip(*shares):
-        own, other = finish(low, high)
-        sums.append((own.astype(f32) + other.astype(f32))[None])
-    totals = lax.psum(jnp.stack(packs), WEIGHT_AXES)
-    own, other = finish(totals[0], totals[1])
-    total = own + other
-    sizes = [CONVK * CH, CH, D, DI, H, H, H]
+    shares = []
+    for low, high in zip(*sums):
+        own = pick(low.value[0], high.value[0])
+        other = swapped(pick(high.value[0], low.value[0]).astype(low.wire))
+        shares.append(own + other.astype(f32))
+    wout, winz, winx, wind, rest = shares
+    rest = rest[0]
     parts, start = [], 0
-    for size in sizes:
-        parts.append(total[start : start + size])
+    for size in [CONVK * c_loc, c_loc, n_loc, g_loc, H, H, H]:
+        parts.append(rest[start : start + size])
         start += size
-    share = lambda a, width: lax.dynamic_slice_in_dim(a, share_idx * width, width, axis=a.ndim - 1)
     return (
         act_out,
         grad_out,
-        sums[0],
-        sums[1],
-        share(parts[0].reshape(CONVK, CH), c_loc)[None],
-        share(parts[1], c_loc)[None],
-        share(parts[2], n_loc)[None],
-        share(parts[3], g_loc)[None],
+        jnp.concatenate([winz, winx, wind], axis=1)[None],
+        wout[None],
+        parts[0].reshape(CONVK, c_loc)[None],
+        parts[1][None],
+        parts[2][None],
+        parts[3][None],
         parts[4][None],
         parts[5][None],
         parts[6][None],

time: 836 us -> 677 us (0.81)
  waiting for transfers between devices: 498 us -> 242 us
  other arithmetic: 57.4 us -> 123 us
  blocking collectives: 41.1 us -> 0 us
  starting transfers between devices: 59.5 us -> 99.3 us
  local copies, waits for them, and re-layouts: 28.9 us -> 59.1 us
    reduce_scatter x4 -> x0, waiting for transfers between devices: 287 us -> none  [reduced(): lax.psum_scatter(grad.astype(bf16), WEIGHT_AXES, scatter_dimension=0, til...]
    ppermute x0 -> x40, waiting for transfers between devices: none -> 68.3 us  [step(): got = lax.ppermute(jnp.where(upper, low, high), axis, pairs)]
    all_gather x4, waiting for transfers between devices: 39.9 us -> 106 us  [body(): lax.all_gather(s, WEIGHT_AXES, axis=0, tiled=True)]
    ppermute x16, waiting for transfers between devices: 91.8 us -> 36.4 us  [shifted(): return lax.ppermute(x, axis, pairs)]
    psum x1 -> x0, waiting for transfers between devices: 49.5 us -> none  [body(): totals = lax.psum(jnp.stack(packs), WEIGHT_AXES)]
    ppermute x0 -> x40, starting transfers between devices: none -> 47.1 us  [step(): got = lax.ppermute(jnp.where(upper, low, high), axis, pairs)]
    unnamed x1 -> x0, blocking collectives: 41.1 us -> none
    select_n x0 -> x40, other arithmetic: none -> 25.8 us  [step(): got = lax.ppermute(jnp.where(upper, low, high), axis, pairs)]
  transfers between devices with their start and end apart: 33 -> 70, of which waited for: 24 -> 33; matrix products, arithmetic and copies ran while one was open for 10% -> 31% of each run, Pallas kernels for 5% -> 7%
where the time goes in v2:
time: 677 us; the launch traced here: 665 us
  waiting for transfers between devices  242 us (36%)
  other arithmetic  123 us (18%)
  starting transfers between devices  99.3 us (15%)
  matrix products  71.5 us (11%)
  local copies, waits for them, and re-layouts  59.1 us (9%)
  Pallas kernels  53.4 us (8%)
  between operations  17.1 us (3%)
    all_gather x4, waiting for transfers between devices, body(): lax.all_gather(s, WEIGHT_AXES, axis=0, tiled=True)  106 us
    dot_general x40, matrix products, dot(): lax.dot_general(left, right, (dims, ((), ())), preferred_element_type=f32...  71.5 us
    ppermute x40, waiting for transfers between devices, step(): got = lax.ppermute(jnp.where(upper, low, high), axis, pairs)  68.3 us
    ppermute x40, starting transfers between devices, step(): got = lax.ppermute(jnp.where(upper, low, high), axis, pairs)  47.1 us
    ppermute x16, starting transfers between devices, shifted(): return lax.ppermute(x, axis, pairs)  44.1 us
    ppermute x16, waiting for transfers between devices, shifted(): return lax.ppermute(x, axis, pairs)  36.4 us
    ppermute x10, waiting for transfers between devices, swapped(): return lax.ppermute(x, 'section', [(0, 1), (1, 0)])  29.9 us
    select_n x40, other arithmetic, step(): got = lax.ppermute(jnp.where(upper, low, high), axis, pairs)  25.8 us
  transfers between devices with their start and end apart: 70, of which 33 were waited for; matrix products, arithmetic and copies ran while one was open for 31% of the time, Pallas kernels for 7%

profile of v2, /device:TPU:0, one launch (start us, length us, event | category | flops | bytes accessed | tf_op | source)
XLA Modules:
  0.0 665.3 jit_solution(16008442331082354570)
XLA Ops:
  13.0 7.8 %collective-permute-done = bf16[48,3456]{1,0:T(8,128)(2,1)S(1)} collective-permute-done((bf16[48,3456]{1,0:T(8,128)(2,1)S(1)}, bf16[48,3456]{1,0:T(8,128)(2,1)S(1)}, u32[]{:S(2)}, u32[]{:S(2)}) %collective-permute-start) | collective-permute-done | bytes 331808 | tf_op jit(solution)/shard_map/ppermute | solution.py:47
  30.7 50.1 %all-gather.5.cloned.1.call-done = bf16[768,3456]{1,0:T(8,128)(2,1)} async-done(((bf16[48,3456]{1,0:T(8,128)(2,1)}), bf16[768,3456]{1,0:T(8,128)(2,1)}) %all-gather.5.cloned.1.call-update) | async-done | bytes 5308432 | tf_op jit(solution)/shard_map/all_gather | solution.py:473
  82.2 56.2 %all-gather.9.cloned.1.call-done = bf16[768,3456]{1,0:T(8,128)(2,1)} async-done(((bf16[48,3456]{1,0:T(8,128)(2,1)}), bf16[768,3456]{1,0:T(8,128)(2,1)}) %all-gather.9.cloned.1.call-update) | async-done | bytes 5308432 | tf_op jit(solution)/shard_map/all_gather | solution.py:473
  140.0 4.2 convolution_convert_fusion.1
  144.2 3.4 collective-permute-start.1
  155.9 3.6 collective-permute-start.3
  163.0 4.7 shard_map.194.part_ref
  171.8 4.4 collective-permute-start.4
  176.3 9.2 %collective-permute-done.4 = bf16[128,1536]{1,0:T(8,128)(2,1)S(1)} collective-permute-done((bf16[128,1536]{1,0:T(8,128)(2,1)S(1)}, bf16[128,1536]{1,0:T(8,128)(2,1)S(1)}, u32[]{:S(2)}, u32[]{:S(2)}) %collective-permute-start.4) | collective-permute-done | bytes 393248 | tf_op jit(solution)/shard_map/ppermute | solution.py:43
  185.6 4.4 collective-permute-start.5
  192.4 4.7 collective-permute-done.5.held_ref
  198.5 4.3 shard_map.195
  202.8 3.3 multiply_reduce_fusion.5
  209.4 4.3 convolution_convert_fusion
  213.7 4.8 collective-permute-start.7
  224.2 4.2 collective-permute-start.8
  234.0 4.7 shard_map.196.part_ref
  243.9 5.6 collective-permute-done.9
  250.3 5.2 collective-permute-start.10
  263.1 6.9 %shard_map.197 = f32[256,1536]{1,0:T(8,128)S(1)} custom-call(bf16[256,1792]{1,0:T(8,128)(2,1)S(1)} %multiply_convert_fusion.x_ref.b_ref.c_ref, f32[256,1536]{1,0:T(8,128)S(1)} %copy-done.1, bf16[128,1536]{1,0:T(8,128)(2,1)} %collective-permute-done.10.held_ref, f32[256,1536]{1,0:T(8,128)S(1)} %copy-done.16), custom_call_target="tpu_custom_call" | custom-call | tf_op jit(solution)/shard_map/pallas_call | solution.py:278
  270.1 3.3 multiply_reduce_fusion.4
  273.9 4.2 broadcast_select_fusion.2
  284.5 5.2 shard_map.198
  307.3 11.5 %shard_map.199 = (f32[256,1536]{1,0:T(8,128)S(1)}, f32[12,2,256]{2,1,0:T(2,128)S(1)}, f32[256,128]{1,0:T(8,128)S(1)}, f32[256,128]{1,0:T(8,128)S(1)}, f32[256,128]{1,0:T(8,128)S(1)}) custom-call(bf16[256,1536]{1,0:T(8,128)(2,1)S(1)} %copy-done.14, bf16[256,1792]{1,0:T(8,128)(2,1)S(1)} %multiply_convert_fusion.x_ref.b_ref.c_ref, ...), custom_call_target="tpu_custom_call" | custom-call | tf_op jit(solution)/shard_map/pallas_call | solution.py:298
  335.4 4.0 collective-permute-start.19
  339.4 6.4 collective-permute-done.16
  378.6 3.6 concatenate.69
  382.2 5.5 fusion.91
  391.8 4.2 collective-permute-start.21
  417.4 3.3 fusion.40
  420.7 5.2 shard_map.200
  435.1 3.6 convolution_convert_fusion.2
  457.1 10.8 %shard_map.201 = (f32[256,1536]{1,0:T(8,128)S(1)}, f32[12,2,256]{2,1,0:T(2,128)S(1)}, f32[256,128]{1,0:T(8,128)S(1)}, f32[256,128]{1,0:T(8,128)S(1)}, f32[256,128]{1,0:T(8,128)S(1)}) custom-call(bf16[256,1536]{1,0:T(8,128)(2,1)S(1)} %copy-done.12, bf16[256,1792]{1,0:T(8,128)(2,1)S(1)} %multiply_convert_fusion.1.x_ref.b_ref.c_ref, ...), custom_call_target="tpu_custom_call" | custom-call | tf_op jit(solution)/shard_map/pallas_call | solution.py:298
  472.4 4.2 collective-permute-start.30
  477.8 8.3 %collective-permute-done.30 = bf16[2,1,48,920]{3,2,0,1:T(8,128)(2,1)S(1)} collective-permute-done((bf16[2,1,48,920]{3,2,0,1:T(8,128)(2,1)}, bf16[2,1,48,920]{3,2,0,1:T(8,128)(2,1)S(1)}, u32[]{:S(2)}, u32[]{:S(2)}) %collective-permute-start.30) | collective-permute-done | bytes 176672 | tf_op jit(solution)/shard_map/ppermute | solution.py:99
  492.8 5.9 collective-permute-done.28
  507.9 3.7 collective-permute-done.36
  516.0 3.5 fusion.308
  539.5 5.8 fusion.98
  572.7 9.6 %collective-permute-done.40 = bf16[2,1,48,1536]{3,2,0,1:T(8,128)(2,1)} collective-permute-done((bf16[2,1,48,1536]{3,2,0,1:T(8,128)(2,1)}, bf16[2,1,48,1536]{3,2,0,1:T(8,128)(2,1)}, u32[]{:S(2)}, u32[]{:S(2)}) %collective-permute-start.40) | collective-permute-done | bytes 294944 | tf_op jit(solution)/shard_map/ppermute | solution.py:99
  583.6 7.9 %collective-permute-done.56 = bf16[2,1,96,768]{3,2,0,1:T(8,128)(2,1)S(1)} collective-permute-done((bf16[2,1,96,768]{3,2,0,1:T(8,128)(2,1)}, bf16[2,1,96,768]{3,2,0,1:T(8,128)(2,1)S(1)}, u32[]{:S(2)}, u32[]{:S(2)}) %collective-permute-start.56) | collective-permute-done | bytes 294944 | tf_op jit(solution)/shard_map/ppermute | solution.py:99
  593.5 3.2 collective-permute-done.41
  597.8 6.7 %collective-permute-done.57 = bf16[1,1,96,768]{3,2,1,0:T(8,128)(2,1)S(1)} collective-permute-done((bf16[1,1,96,768]{3,2,1,0:T(8,128)(2,1)S(1)}, bf16[1,1,96,768]{3,2,1,0:T(8,128)(2,1)S(1)}, u32[]{:S(2)}, u32[]{:S(2)}) %collective-permute-start.57) | collective-permute-done | bytes 147488 | tf_op jit(solution)/shard_map/ppermute | solution.py:99
  605.6 9.1 %collective-permute-done.43 = bf16[48,1536]{1,0:T(8,128)(2,1)S(1)} collective-permute-done((bf16[48,1536]{1,0:T(8,128)(2,1)S(1)}, bf16[48,1536]{1,0:T(8,128)(2,1)S(1)}, u32[]{:S(2)}, u32[]{:S(2)}) %collective-permute-start.43) | collective-permute-done | bytes 147488 | tf_op jit(solution)/shard_map/ppermute | solution.py:47
  616.0 3.8 collective-permute-done.59
  625.2 7.2 %collective-permute-done.45 = bf16[1,4,48,896]{3,2,1,0:T(8,128)(2,1)S(1)} collective-permute-done((bf16[1,4,48,896]{3,2,1,0:T(8,128)(2,1)S(1)}, bf16[1,4,48,896]{3,2,1,0:T(8,128)(2,1)S(1)}, u32[]{:S(2)}, u32[]{:S(2)}) %collective-permute-start.45) | collective-permute-done | bytes 344096 | tf_op jit(solution)/shard_map/ppermute | solution.py:99
  634.8 4.0 collective-permute-done.46
  639.0 9.1 %collective-permute-done.52 = bf16[2,1,48,920]{3,2,0,1:T(8,128)(2,1)S(1)} collective-permute-done((bf16[2,1,48,920]{3,2,0,1:T(8,128)(2,1)S(1)}, bf16[2,1,48,920]{3,2,0,1:T(8,128)(2,1)S(1)}, u32[]{:S(2)}, u32[]{:S(2)}) %collective-permute-start.52) | collective-permute-done | bytes 176672 | tf_op jit(solution)/shard_map/ppermute | solution.py:99
  (830 shorter events, 289.2 us)
Async XLA Ops:
  7.2 73.6 %all-gather.5.cloned.1.call-start = ((), (), s32[]{:S(2)}) async-start(), calls=%async_computation | async-start | bytes 5640192 | tf_op jit(solution)/shard_map/all_gather | solution.py:473
  10.1 10.8 %collective-permute-start = (bf16[48,3456]{1,0:T(8,128)(2,1)S(1)}, bf16[48,3456]{1,0:T(8,128)(2,1)S(1)}, u32[]{:S(2)}, u32[]{:S(2)}) collective-permute-start(bf16[48,3456]{1,0:T(8,128)(2,1)S(1)} %pad_maximum_fusion.4), channel_id=1, source_target_pairs={{0,16},{16,0},{1,17},{17,1},{2,18},{18,2},{3,19},{19,3},{4,20},{20... | collective-permute-start | bytes 995336 | tf_op jit(solution)/shard_map/ppermute | solution.py:47
  22.8 115.7 %all-gather.9.cloned.1.call-start = ((), (), s32[]{:S(2)}) async-start(), calls=%async_computation.2 | async-start | bytes 5640192 | tf_op jit(solution)/shard_map/all_gather | solution.py:473
  23.5 182.7 %all-gather.7.cloned.1.call-start = ((), (), s32[]{:S(2)}) async-start(), calls=%async_computation.1 | async-start | bytes 2506752 | tf_op jit(solution)/shard_map/all_gather | solution.py:473
  30.6 243.3 %all-gather.11.cloned.1.call-start = ((), (), s32[]{:S(2)}) async-start(), calls=%async_computation.3 | async-start | bytes 2506752 | tf_op jit(solution)/shard_map/all_gather | solution.py:473
  155.9 14.8 %collective-permute-start.3 = (bf16[128,1536]{1,0:T(8,128)(2,1)}, bf16[128,1536]{1,0:T(8,128)(2,1)}, u32[]{:S(2)}, u32[]{:S(2)}) collective-permute-start(bf16[128,1536]{1,0:T(8,128)(2,1)} %get-tuple-element.241), channel_id=1, source_target_pairs={{0,1},{1,2},{2,3},{4,5},{5,6},{6,7},{8,9},{9,10},{10,11},{12,13},{... | collective-permute-start | bytes 1179656 | tf_op jit(solution)/shard_map/ppermute | solution.py:43
  171.8 13.6 %collective-permute-start.4 = (bf16[128,1536]{1,0:T(8,128)(2,1)S(1)}, bf16[128,1536]{1,0:T(8,128)(2,1)S(1)}, u32[]{:S(2)}, u32[]{:S(2)}) collective-permute-start(bf16[128,1536]{1,0:T(8,128)(2,1)S(1)} %add_convert_fusion.7), channel_id=1, source_target_pairs={{0,1},{1,2},{2,3},{4,5},{5,6},{6,7},{8,9},{9,10},{10,11},{12,13},{... | collective-permute-start | bytes 1179656 | tf_op jit(solution)/shard_map/ppermute | solution.py:43
  185.6 11.5 %collective-permute-start.5 = (bf16[128,1536]{1,0:T(8,128)(2,1)S(1)}, bf16[128,1536]{1,0:T(8,128)(2,1)S(1)}, u32[]{:S(2)}, u32[]{:S(2)}) collective-permute-start(bf16[128,1536]{1,0:T(8,128)(2,1)S(1)} %add_convert_fusion.6), channel_id=1, source_target_pairs={{0,1},{1,2},{2,3},{4,5},{5,6},{6,7},{8,9},{9,10},{10,11},{12,13},{... | collective-permute-start | bytes 1179656 | tf_op jit(solution)/shard_map/ppermute | solution.py:43
  224.2 15.7 %collective-permute-start.8 = (bf16[128,1536]{1,0:T(8,128)(2,1)}, bf16[128,1536]{1,0:T(8,128)(2,1)}, u32[]{:S(2)}, u32[]{:S(2)}) collective-permute-start(bf16[128,1536]{1,0:T(8,128)(2,1)} %get-tuple-element.245), channel_id=1, source_target_pairs={{0,1},{1,2},{2,3},{4,5},{5,6},{6,7},{8,9},{9,10},{10,11},{12,13},{... | collective-permute-start | bytes 1179656 | tf_op jit(solution)/shard_map/ppermute | solution.py:43
  250.3 10.0 %collective-permute-start.10 = (bf16[128,1536]{1,0:T(8,128)(2,1)}, bf16[128,1536]{1,0:T(8,128)(2,1)}, u32[]{:S(2)}, u32[]{:S(2)}) collective-permute-start(bf16[128,1536]{1,0:T(8,128)(2,1)} %add_convert_fusion.4), channel_id=1, source_target_pairs={{0,1},{1,2},{2,3},{4,5},{5,6},{6,7},{8,9},{9,10},{10,11},{12,13},{... | collective-permute-start | bytes 1179656 | tf_op jit(solution)/shard_map/ppermute | solution.py:43
  278.1 44.6 %collective-permute-start.11 = (bf16[256,768]{1,0:T(8,128)(2,1)}, bf16[256,768]{1,0:T(8,128)(2,1)}, u32[]{:S(2)}, u32[]{:S(2)}) collective-permute-start(bf16[256,768]{1,0:T(8,128)(2,1)} %get-tuple-element.247), channel_id=1, source_target_pairs={{0,16},{16,0},{1,17},{17,1},{2,18},{18,2},{3,19},{19,3},{4,20},{20... | collective-permute-start | bytes 1179656 | tf_op jit(solution)/shard_map/ppermute | solution.py:47
  290.7 10.4 %collective-permute-start.12 = (bf16[128,1536]{1,0:T(8,128)(2,1)}, bf16[128,1536]{1,0:T(8,128)(2,1)}, u32[]{:S(2)}, u32[]{:S(2)}) collective-permute-start(bf16[128,1536]{1,0:T(8,128)(2,1)} %convert_element_type.902), channel_id=1, source_target_pairs={{1,0},{2,1},{3,2},{5,4},{6,5},{7,6},{9,8},{10,9},{11,10},{13,12},{... | collective-permute-start | bytes 1179656 | tf_op jit(solution)/shard_map/ppermute | solution.py:43
  302.3 22.8 %collective-permute-start.15 = (bf16[2,4,48,1536]{3,2,1,0:T(8,128)(2,1)}, bf16[2,4,48,1536]{3,2,1,0:T(8,128)(2,1)}, u32[]{:S(2)}, u32[]{:S(2)}) collective-permute-start(bf16[2,4,48,1536]{3,2,1,0:T(8,128)(2,1)} %select_bitcast_fusion.2), channel_id=1, source_target_pairs={{0,4},{4,0},{8,12},{12,8},{1,5},{5,1},{9,13},{13,9},{2,6},{6,2},{1... | collective-permute-start | bytes 3538952 | tf_op jit(solution)/shard_map/ppermute | solution.py:99
  303.5 23.5 %collective-permute-start.14 = (bf16[2,4,96,768]{3,2,1,0:T(8,128)(2,1)}, bf16[2,4,96,768]{3,2,1,0:T(8,128)(2,1)}, u32[]{:S(2)}, u32[]{:S(2)}) collective-permute-start(bf16[2,4,96,768]{3,2,1,0:T(8,128)(2,1)} %fusion.72), channel_id=1, source_target_pairs={{0,4},{4,0},{8,12},{12,8},{1,5},{5,1},{9,13},{13,9},{2,6},{6,2},{1... | collective-permute-start | bytes 3538952 | tf_op jit(solution)/shard_map/ppermute | solution.py:99
  305.8 23.5 %collective-permute-start.13 = (bf16[128,1536]{1,0:T(8,128)(2,1)}, bf16[128,1536]{1,0:T(8,128)(2,1)}, u32[]{:S(2)}, u32[]{:S(2)}) collective-permute-start(bf16[128,1536]{1,0:T(8,128)(2,1)} %add_convert_fusion.3), channel_id=1, source_target_pairs={{1,0},{2,1},{3,2},{5,4},{6,5},{7,6},{9,8},{10,9},{11,10},{13,12},{... | collective-permute-start | bytes 1179656 | tf_op jit(solution)/shard_map/ppermute | solution.py:43
  330.7 15.2 %collective-permute-start.16 = (bf16[128,1536]{1,0:T(8,128)(2,1)S(1)}, bf16[128,1536]{1,0:T(8,128)(2,1)S(1)}, u32[]{:S(2)}, u32[]{:S(2)}) collective-permute-start(bf16[128,1536]{1,0:T(8,128)(2,1)S(1)} %add_convert_fusion.2), channel_id=1, source_target_pairs={{1,0},{2,1},{3,2},{5,4},{6,5},{7,6},{9,8},{10,9},{11,10},{13,12},{... | collective-permute-start | bytes 1179656 | tf_op jit(solution)/shard_map/ppermute | solution.py:43
  332.9 40.3 %collective-permute-start.18 = (bf16[1,4,96,768]{3,2,1,0:T(8,128)(2,1)}, bf16[1,4,96,768]{3,2,1,0:T(8,128)(2,1)}, u32[]{:S(2)}, u32[]{:S(2)}) collective-permute-start(bf16[1,4,96,768]{3,2,1,0:T(8,128)(2,1)} %select_bitcast_fusion.10), channel_id=1, source_target_pairs={{0,8},{4,12},{8,0},{12,4},{1,9},{5,13},{9,1},{13,5},{2,10},{6,14},... | collective-permute-start | bytes 1769480 | tf_op jit(solution)/shard_map/ppermute | solution.py:99
  335.4 40.3 %collective-permute-start.19 = (bf16[4,1,48,1536]{3,2,0,1:T(8,128)(2,1)}, bf16[4,1,48,1536]{3,2,0,1:T(8,128)(2,1)}, u32[]{:S(2)}, u32[]{:S(2)}) collective-permute-start(bf16[4,1,48,1536]{3,2,0,1:T(8,128)(2,1)} %fusion.109), channel_id=1, source_target_pairs={{0,1},{1,0},{2,3},{3,2},{4,5},{5,4},{6,7},{7,6},{8,9},{9,8},{10,11... | collective-permute-start | bytes 1769480 | tf_op jit(solution)/shard_map/ppermute | solution.py:99
  388.4 15.1 %collective-permute-start.20 = (bf16[2,1,96,768]{3,2,0,1:T(8,128)(2,1)}, bf16[2,1,96,768]{3,2,0,1:T(8,128)(2,1)}, u32[]{:S(2)}, u32[]{:S(2)}) collective-permute-start(bf16[2,1,96,768]{3,2,0,1:T(8,128)(2,1)} %fusion.140), channel_id=1, source_target_pairs={{0,1},{1,0},{2,3},{3,2},{4,5},{5,4},{6,7},{7,6},{8,9},{9,8},{10,11... | collective-permute-start | bytes 884744 | tf_op jit(solution)/shard_map/ppermute | solution.py:99
  391.8 16.5 %collective-permute-start.21 = (bf16[2,1,48,1536]{3,2,0,1:T(8,128)(2,1)}, bf16[2,1,48,1536]{3,2,0,1:T(8,128)(2,1)}, u32[]{:S(2)}, u32[]{:S(2)}) collective-permute-start(bf16[2,1,48,1536]{3,2,0,1:T(8,128)(2,1)} %fusion.141), channel_id=1, source_target_pairs={{0,2},{1,3},{2,0},{3,1},{4,6},{5,7},{6,4},{7,5},{8,10},{9,11},{10,... | collective-permute-start | bytes 884744 | tf_op jit(solution)/shard_map/ppermute | solution.py:99
  397.0 13.3 %collective-permute-start.22 = (bf16[2,4,48,896]{3,2,1,0:T(8,128)(2,1)}, bf16[2,4,48,896]{3,2,1,0:T(8,128)(2,1)}, u32[]{:S(2)}, u32[]{:S(2)}) collective-permute-start(bf16[2,4,48,896]{3,2,1,0:T(8,128)(2,1)} %fusion.102), channel_id=1, source_target_pairs={{0,4},{4,0},{8,12},{12,8},{1,5},{5,1},{9,13},{13,9},{2,6},{6,2},{1... | collective-permute-start | bytes 2064392 | tf_op jit(solution)/shard_map/ppermute | solution.py:99
  398.0 13.8 %collective-permute-start.23 = (bf16[2,4,48,920]{3,2,1,0:T(8,128)(2,1)}, bf16[2,4,48,920]{3,2,1,0:T(8,128)(2,1)}, u32[]{:S(2)}, u32[]{:S(2)}) collective-permute-start(bf16[2,4,48,920]{3,2,1,0:T(8,128)(2,1)} %select_bitcast_fusion.6), channel_id=1, source_target_pairs={{0,4},{4,0},{8,12},{12,8},{1,5},{5,1},{9,13},{13,9},{2,6},{6,2},{1... | collective-permute-start | bytes 2119688 | tf_op jit(solution)/shard_map/ppermute | solution.py:99
  426.8 20.5 %collective-permute-start.24 = (bf16[128,1536]{1,0:T(8,128)(2,1)}, bf16[128,1536]{1,0:T(8,128)(2,1)}, u32[]{:S(2)}, u32[]{:S(2)}) collective-permute-start(bf16[128,1536]{1,0:T(8,128)(2,1)} %convert_element_type.952), channel_id=1, source_target_pairs={{1,0},{2,1},{3,2},{5,4},{6,5},{7,6},{9,8},{10,9},{11,10},{13,12},{... | collective-permute-start | bytes 1179656 | tf_op jit(solution)/shard_map/ppermute | solution.py:43
  429.3 13.4 %collective-permute-start.25 = (bf16[1,4,48,896]{3,2,1,0:T(8,128)(2,1)}, bf16[1,4,48,896]{3,2,1,0:T(8,128)(2,1)}, u32[]{:S(2)}, u32[]{:S(2)}) collective-permute-start(bf16[1,4,48,896]{3,2,1,0:T(8,128)(2,1)} %select_bitcast_fusion.15), channel_id=1, source_target_pairs={{0,8},{4,12},{8,0},{12,4},{1,9},{5,13},{9,1},{13,5},{2,10},{6,14},... | collective-permute-start | bytes 1032200 | tf_op jit(solution)/shard_map/ppermute | solution.py:99
  432.3 13.0 %collective-permute-start.26 = (bf16[4,1,48,920]{3,2,0,1:T(8,128)(2,1)}, bf16[4,1,48,920]{3,2,0,1:T(8,128)(2,1)}, u32[]{:S(2)}, u32[]{:S(2)}) collective-permute-start(bf16[4,1,48,920]{3,2,0,1:T(8,128)(2,1)} %fusion.129), channel_id=1, source_target_pairs={{0,1},{1,0},{2,3},{3,2},{4,5},{5,4},{6,7},{7,6},{8,9},{9,8},{10,11... | collective-permute-start | bytes 1059848 | tf_op jit(solution)/shard_map/ppermute | solution.py:99
  439.5 153.9 %collective-permute-start.42 = (bf16[1,1,48,1536]{3,2,1,0:T(8,128)(2,1)}, bf16[1,1,48,1536]{3,2,1,0:T(8,128)(2,1)}, u32[]{:S(2)}, u32[]{:S(2)}) collective-permute-start(bf16[1,1,48,1536]{3,2,1,0:T(8,128)(2,1)} %fusion.160), channel_id=1, source_target_pairs={{0,8},{4,12},{8,0},{12,4},{1,9},{5,13},{9,1},{13,5},{2,10},{6,14},... | collective-permute-start | bytes 442376 | tf_op jit(solution)/shard_map/ppermute | solution.py:99
  441.5 156.2 %collective-permute-start.58 = (bf16[1,1,96,768]{3,2,1,0:T(8,128)(2,1)}, bf16[1,1,96,768]{3,2,1,0:T(8,128)(2,1)}, u32[]{:S(2)}, u32[]{:S(2)}) collective-permute-start(bf16[1,1,96,768]{3,2,1,0:T(8,128)(2,1)} %fusion.159), channel_id=1, source_target_pairs={{0,2},{1,3},{2,0},{3,1},{4,6},{5,7},{6,4},{7,5},{8,10},{9,11},{10,... | collective-permute-start | bytes 442376 | tf_op jit(solution)/shard_map/ppermute | solution.py:99
  449.8 22.6 %collective-permute-start.29 = (bf16[2,1,48,896]{3,2,0,1:T(8,128)(2,1)}, bf16[2,1,48,896]{3,2,0,1:T(8,128)(2,1)}, u32[]{:S(2)}, u32[]{:S(2)}) collective-permute-start(bf16[2,1,48,896]{3,2,0,1:T(8,128)(2,1)} %select_bitcast_fusion.21), channel_id=1, source_target_pairs={{0,1},{1,0},{2,3},{3,2},{4,5},{5,4},{6,7},{7,6},{8,9},{9,8},{10,11... | collective-permute-start | bytes 516104 | tf_op jit(solution)/shard_map/ppermute | solution.py:99
  450.4 20.8 %collective-permute-start.31 = (f32[1,4,1,776]{3,1,2,0:T(4,128)}, f32[1,4,1,776]{3,1,2,0:T(4,128)}, u32[]{:S(2)}, u32[]{:S(2)}) collective-permute-start(f32[1,4,1,776]{3,1,2,0:T(4,128)} %select_bitcast_fusion.30), channel_id=1, source_target_pairs={{0,8},{4,12},{8,0},{12,4},{1,9},{5,13},{9,1},{13,5},{2,10},{6,14},... | collective-permute-start | bytes 37256 | tf_op jit(solution)/shard_map/ppermute | solution.py:99
  455.3 33.2 %collective-permute-start.33 = (bf16[2,4,48,1536]{3,2,1,0:T(8,128)(2,1)}, bf16[2,4,48,1536]{3,2,1,0:T(8,128)(2,1)}, u32[]{:S(2)}, u32[]{:S(2)}) collective-permute-start(bf16[2,4,48,1536]{3,2,1,0:T(8,128)(2,1)} %select_bitcast_fusion), channel_id=1, source_target_pairs={{0,4},{4,0},{8,12},{12,8},{1,5},{5,1},{9,13},{13,9},{2,6},{6,2},{1... | collective-permute-start | bytes 3538952 | tf_op jit(solution)/shard_map/ppermute | solution.py:99
  471.2 19.9 %collective-permute-start.32 = (bf16[2,4,96,768]{3,2,1,0:T(8,128)(2,1)}, bf16[2,4,96,768]{3,2,1,0:T(8,128)(2,1)S(1)}, u32[]{:S(2)}, u32[]{:S(2)}) collective-permute-start(bf16[2,4,96,768]{3,2,1,0:T(8,128)(2,1)} %select_bitcast_fusion.1), channel_id=1, source_target_pairs={{0,4},{4,0},{8,12},{12,8},{1,5},{5,1},{9,13},{13,9},{2,6},{6,2},{1... | collective-permute-start | bytes 3538952 | tf_op jit(solution)/shard_map/ppermute | solution.py:99
  472.4 13.7 %collective-permute-start.30 = (bf16[2,1,48,920]{3,2,0,1:T(8,128)(2,1)}, bf16[2,1,48,920]{3,2,0,1:T(8,128)(2,1)S(1)}, u32[]{:S(2)}, u32[]{:S(2)}) collective-permute-start(bf16[2,1,48,920]{3,2,0,1:T(8,128)(2,1)} %select_bitcast_fusion.19), channel_id=1, source_target_pairs={{0,2},{1,3},{2,0},{3,1},{4,6},{5,7},{6,4},{7,5},{8,10},{9,11},{10,... | collective-permute-start | bytes 529928 | tf_op jit(solution)/shard_map/ppermute | solution.py:99
  486.1 12.6 %collective-permute-start.28 = (bf16[128,1536]{1,0:T(8,128)(2,1)}, bf16[128,1536]{1,0:T(8,128)(2,1)S(1)}, u32[]{:S(2)}, u32[]{:S(2)}) collective-permute-start(bf16[128,1536]{1,0:T(8,128)(2,1)} %add_convert_fusion.1), channel_id=1, source_target_pairs={{1,0},{2,1},{3,2},{5,4},{6,5},{7,6},{9,8},{10,9},{11,10},{13,12},{... | collective-permute-start | bytes 1179656 | tf_op jit(solution)/shard_map/ppermute | solution.py:43
  499.6 12.7 %collective-permute-start.34 = (bf16[128,1536]{1,0:T(8,128)(2,1)}, bf16[128,1536]{1,0:T(8,128)(2,1)S(1)}, u32[]{:S(2)}, u32[]{:S(2)}) collective-permute-start(bf16[128,1536]{1,0:T(8,128)(2,1)} %add_convert_fusion), channel_id=1, source_target_pairs={{1,0},{2,1},{3,2},{5,4},{6,5},{7,6},{9,8},{10,9},{11,10},{13,12},{... | collective-permute-start | bytes 1179656 | tf_op jit(solution)/shard_map/ppermute | solution.py:43
  500.9 10.7 %collective-permute-start.36 = (f32[2,1,1,776]{3,1,2,0:T(1,128)S(1)}, f32[2,1,1,776]{3,1,2,0:T(1,128)S(1)}, u32[]{:S(2)}, u32[]{:S(2)}) collective-permute-start(f32[2,1,1,776]{3,1,2,0:T(1,128)S(1)} %fusion.270), channel_id=1, source_target_pairs={{0,1},{1,0},{2,3},{3,2},{4,5},{5,4},{6,7},{7,6},{8,9},{9,8},{10,11... | collective-permute-start | bytes 18632 | tf_op jit(solution)/shard_map/ppermute | solution.py:99
  505.7 26.9 %collective-permute-start.37 = (bf16[1,4,96,768]{3,2,1,0:T(8,128)(2,1)}, bf16[1,4,96,768]{3,2,1,0:T(8,128)(2,1)}, u32[]{:S(2)}, u32[]{:S(2)}) collective-permute-start(bf16[1,4,96,768]{3,2,1,0:T(8,128)(2,1)} %select_bitcast_fusion.9), channel_id=1, source_target_pairs={{0,8},{4,12},{8,0},{12,4},{1,9},{5,13},{9,1},{13,5},{2,10},{6,14},... | collective-permute-start | bytes 1769480 | tf_op jit(solution)/shard_map/ppermute | solution.py:99
  511.6 23.5 %collective-permute-start.38 = (bf16[4,1,48,1536]{3,2,0,1:T(8,128)(2,1)}, bf16[4,1,48,1536]{3,2,0,1:T(8,128)(2,1)}, u32[]{:S(2)}, u32[]{:S(2)}) collective-permute-start(bf16[4,1,48,1536]{3,2,0,1:T(8,128)(2,1)} %select_bitcast_fusion.8), channel_id=1, source_target_pairs={{0,1},{1,0},{2,3},{3,2},{4,5},{5,4},{6,7},{7,6},{8,9},{9,8},{10,11... | collective-permute-start | bytes 1769480 | tf_op jit(solution)/shard_map/ppermute | solution.py:99
  526.4 124.7 %collective-permute-start.54 = (bf16[1,1,48,920]{3,2,1,0:T(8,128)(2,1)}, bf16[1,1,48,920]{3,2,1,0:T(8,128)(2,1)S(1)}, u32[]{:S(2)}, u32[]{:S(2)}) collective-permute-start(bf16[1,1,48,920]{3,2,1,0:T(8,128)(2,1)} %select_bitcast_fusion.24), channel_id=1, source_target_pairs={{0,8},{4,12},{8,0},{12,4},{1,9},{5,13},{9,1},{13,5},{2,10},{6,14},... | collective-permute-start | bytes 264968 | tf_op jit(solution)/shard_map/ppermute | solution.py:99
  563.1 86.6 %collective-permute-start.48 = (bf16[1,1,48,896]{3,2,1,0:T(8,128)(2,1)}, bf16[1,1,48,896]{3,2,1,0:T(8,128)(2,1)}, u32[]{:S(2)}, u32[]{:S(2)}) collective-permute-start(bf16[1,1,48,896]{3,2,1,0:T(8,128)(2,1)} %select_bitcast_fusion.26), channel_id=1, source_target_pairs={{0,2},{1,3},{2,0},{3,1},{4,6},{5,7},{6,4},{7,5},{8,10},{9,11},{10,... | collective-permute-start | bytes 258056 | tf_op jit(solution)/shard_map/ppermute | solution.py:99
  567.6 14.7 %collective-permute-start.40 = (bf16[2,1,48,1536]{3,2,0,1:T(8,128)(2,1)}, bf16[2,1,48,1536]{3,2,0,1:T(8,128)(2,1)}, u32[]{:S(2)}, u32[]{:S(2)}) collective-permute-start(bf16[2,1,48,1536]{3,2,0,1:T(8,128)(2,1)} %select_bitcast_fusion.17), channel_id=1, source_target_pairs={{0,2},{1,3},{2,0},{3,1},{4,6},{5,7},{6,4},{7,5},{8,10},{9,11},{10,... | collective-permute-start | bytes 884744 | tf_op jit(solution)/shard_map/ppermute | solution.py:99
  582.3 9.2 %collective-permute-start.56 = (bf16[2,1,96,768]{3,2,0,1:T(8,128)(2,1)}, bf16[2,1,96,768]{3,2,0,1:T(8,128)(2,1)S(1)}, u32[]{:S(2)}, u32[]{:S(2)}) collective-permute-start(bf16[2,1,96,768]{3,2,0,1:T(8,128)(2,1)} %select_bitcast_fusion.16), channel_id=1, source_target_pairs={{0,1},{1,0},{2,3},{3,2},{4,5},{5,4},{6,7},{7,6},{8,9},{9,8},{10,11... | collective-permute-start | bytes 884744 | tf_op jit(solution)/shard_map/ppermute | solution.py:99
  593.4 30.4 %collective-permute-start.39 = (f32[256,768]{1,0:T(8,128)S(1)}, f32[256,768]{1,0:T(8,128)S(1)}, u32[]{:S(2)}, u32[]{:S(2)}) collective-permute-start(f32[256,768]{1,0:T(8,128)S(1)} %copy-done.120), channel_id=1, source_target_pairs={{0,16},{16,0},{1,17},{17,1},{2,18},{18,2},{3,19},{19,3},{4,20},{20... | collective-permute-start | bytes 2359304 | tf_op jit(solution)/shard_map/ppermute | solution.py:47
  597.7 23.9 %collective-permute-start.44 = (bf16[2,4,48,896]{3,2,1,0:T(8,128)(2,1)S(1)}, bf16[2,4,48,896]{3,2,1,0:T(8,128)(2,1)S(1)}, u32[]{:S(2)}, u32[]{:S(2)}) collective-permute-start(bf16[2,4,48,896]{3,2,1,0:T(8,128)(2,1)S(1)} %copy-done.121), channel_id=1, source_target_pairs={{0,4},{4,0},{8,12},{12,8},{1,5},{5,1},{9,13},{13,9},{2,6},{6,2},{1... | collective-permute-start | bytes 2064392 | tf_op jit(solution)/shard_map/ppermute | solution.py:99
  604.5 10.1 %collective-permute-start.43 = (bf16[48,1536]{1,0:T(8,128)(2,1)S(1)}, bf16[48,1536]{1,0:T(8,128)(2,1)S(1)}, u32[]{:S(2)}, u32[]{:S(2)}) collective-permute-start(bf16[48,1536]{1,0:T(8,128)(2,1)S(1)} %fusion.157), channel_id=1, source_target_pairs={{0,16},{16,0},{1,17},{17,1},{2,18},{18,2},{3,19},{19,3},{4,20},{20... | collective-permute-start | bytes 442376 | tf_op jit(solution)/shard_map/ppermute | solution.py:47
  621.9 10.5 %collective-permute-start.45 = (bf16[1,4,48,896]{3,2,1,0:T(8,128)(2,1)S(1)}, bf16[1,4,48,896]{3,2,1,0:T(8,128)(2,1)S(1)}, u32[]{:S(2)}, u32[]{:S(2)}) collective-permute-start(bf16[1,4,48,896]{3,2,1,0:T(8,128)(2,1)S(1)} %select_bitcast_fusion.14), channel_id=1, source_target_pairs={{0,8},{4,12},{8,0},{12,4},{1,9},{5,13},{9,1},{13,5},{2,10},{6,14},... | collective-permute-start | bytes 1032200 | tf_op jit(solution)/shard_map/ppermute | solution.py:99
  623.1 11.3 %collective-permute-start.51 = (bf16[4,1,48,920]{3,2,0,1:T(8,128)(2,1)S(1)}, bf16[4,1,48,920]{3,2,0,1:T(8,128)(2,1)S(1)}, u32[]{:S(2)}, u32[]{:S(2)}) collective-permute-start(bf16[4,1,48,920]{3,2,0,1:T(8,128)(2,1)S(1)} %select_bitcast_fusion.11), channel_id=1, source_target_pairs={{0,1},{1,0},{2,3},{3,2},{4,5},{5,4},{6,7},{7,6},{8,9},{9,8},{10,11... | collective-permute-start | bytes 1059848 | tf_op jit(solution)/shard_map/ppermute | solution.py:99
  634.7 13.4 %collective-permute-start.52 = (bf16[2,1,48,920]{3,2,0,1:T(8,128)(2,1)S(1)}, bf16[2,1,48,920]{3,2,0,1:T(8,128)(2,1)S(1)}, u32[]{:S(2)}, u32[]{:S(2)}) collective-permute-start(bf16[2,1,48,920]{3,2,0,1:T(8,128)(2,1)S(1)} %select_bitcast_fusion.18), channel_id=1, source_target_pairs={{0,2},{1,3},{2,0},{3,1},{4,6},{5,7},{6,4},{7,5},{8,10},{9,11},{10,... | collective-permute-start | bytes 529928 | tf_op jit(solution)/shard_map/ppermute | solution.py:99
  638.9 10.8 %collective-permute-start.47 = (bf16[1,1,48,896]{3,2,1,0:T(8,128)(2,1)S(1)}, bf16[1,1,48,896]{3,2,1,0:T(8,128)(2,1)S(1)}, u32[]{:S(2)}, u32[]{:S(2)}) collective-permute-start(bf16[1,1,48,896]{3,2,1,0:T(8,128)(2,1)S(1)} %select_bitcast_fusion.27), channel_id=1, source_target_pairs={{0,2},{1,3},{2,0},{3,1},{4,6},{5,7},{6,4},{7,5},{8,10},{9,11},{10,... | collective-permute-start | bytes 258056 | tf_op jit(solution)/shard_map/ppermute | solution.py:99
  (244 other events, 2839.4 us)
Sparse Core Ops, SparseCore 0:
  22.9 57.8 all-gather.4
  83.5 54.9 all-gather.8
  141.4 41.0 all-gather.6
  190.4 40.8 all-gather.10

commit v3 on v2

--- a/solution.py
+++ b/solution.py
@@ -74,8 +74,7 @@
     def __init__(self, grad, late_dp, wire=bf16):
         sizes = {a: lax.axis_size(a) for a in WEIGHT_AXES}
         self.bits = [(a, b) for a in WEIGHT_AXES for b in reversed(range(sizes[a].bit_length() - 1))]
-        count = sizes["dp"] * sizes["seq"]
-        self.value = grad.astype(wire).reshape(count, grad.shape[0] // count, grad.shape[1])
+        self.value = grad.astype(wire)
         dp = sorted(b for b in self.bits if b[0] == "dp")
         seq = sorted(b for b in self.bits if b[0] == "seq")
         self.order = dp[:1] + (seq + dp[1:] if late_dp else dp[1:] + seq)
@@ -385,14 +384,19 @@
     inv_rms, normed = rms_parts(layer_in.astype(f32))
     un = (normed * norm_g).astype(bf16)
     grad_win_z = rows_dot(un, dz)
-    wout_sum = queue.add(grad_wout, False)
-    winz_sum = queue.add(grad_win_z, True)
+    count = lax.axis_size("dp") * lax.axis_size("seq")
+    early = jnp.concatenate(
+        [*grad_wout.astype(bf16).reshape(count, 2, -1, D).transpose(1, 0, 2, 3), grad_win_z.astype(bf16).reshape(count, -1, DI)],
+        axis=2,
+    )
+    early_sum = queue.add(early, False)
     leave, dy = queue.advance(leave, dy)
     for hop in range(lax.axis_size("seq") - 2):
         leave = shifted((totals_wide * leave.astype(f32) + dheld).astype(bf16), "seq", -1)
         if hop == 0:
             dx, dstep_t, dcum, db, dc = mix_grad(dy, acts, cum_wide, cum_t, dt_t, incoming, skip_wide)
             leave, dx = queue.advance(leave, dx)
+    leave, dx = queue.advance(leave, dx)
     dstep = dstep_t.reshape(H, t).T
     dcum = dcum[:, :H] - dstep * dt
     db = db + cols_dot(weighted, leave)
@@ -413,6 +417,7 @@
     draw = dstep * jax.nn.sigmoid(projected[:, DI + CH : E].astype(f32) + bias_dt)
     grad_dtb = jnp.sum(draw, axis=0)
     dconv = jnp.concatenate([dx, db, dc], axis=1) * silu_slope(conv)
+    dconv = queue.advance(dconv)
     edge = shifted(dconv[:8], "seq", -1)
     grad_cb = jnp.sum(dconv, axis=0)
     grad_cw = jnp.stack([jnp.sum(dconv * padded[k : k + t].astype(f32), axis=0) for k in range(CONVK)])
@@ -422,29 +427,17 @@
         dxbc = dxbc + conv_w[k : k + 1] * ext[CONVK - 1 - k : CONVK - 1 - k + t]
     dxbc = dxbc.astype(bf16)
     draw = draw.astype(bf16)
-    half = CH // 2
-    winx_sum = queue.add(rows_dot(un, dxbc[:, :half]), False)
-    wind_sum = queue.add(rows_dot(un, jnp.concatenate([dxbc[:, half:], draw], axis=1)), True)
+    late = rows_dot(un, jnp.concatenate([dxbc, draw], axis=1)).astype(bf16)
+    late_sum = queue.add(late.reshape(count, -1, CH + H), False)
     dxbc = queue.advance(dxbc)
     filler = jnp.zeros((t, w_in.shape[1] - E), bf16)
     dun = cols_dot(jnp.concatenate([dz, dxbc, draw, filler], axis=1), w_in)
     grad_norm_gain = jnp.sum(dun * normed, axis=0)
     dnorm = dun * norm_g
     grad_u = grad_v.astype(f32) + inv_rms * (dnorm - normed * jnp.mean(dnorm * normed, axis=-1, keepdims=True))
-    count = lax.axis_size("dp") * lax.axis_size("seq")
-    heads = jnp.concatenate([grad_dtb, grad_alog, grad_skip])
-    rest = jnp.concatenate(
-        [
-            grad_cw.reshape(CONVK, count, -1).transpose(1, 0, 2).reshape(count, -1),
-            grad_cb.reshape(count, -1),
-            grad_norm_gain.reshape(count, -1),
-            grad_gate_gain.reshape(count, -1),
-            jnp.broadcast_to(heads[None], (count, 3 * H)),
-        ],
-        axis=1,
-    )
-    rest_sum = queue.add(rest, False, f32)
-    return grad_u, (wout_sum, winz_sum, winx_sum, wind_sum, rest_sum)
+    rest = (grad_cw, grad_cb, grad_norm_gain, grad_gate_gain, grad_dtb, grad_alog, grad_skip)
+    rest = lax.psum(jnp.concatenate([r.reshape(-1) for r in rest]), ("section",) + WEIGHT_AXES)
+    return grad_u, (early_sum, late_sum), rest
 
 
 def body(tokens, cotangent, in_weight, out_weight, conv_weight, conv_bias, norm_gain, gate_gain, dt_bias, a_log, d_skip):
@@ -467,10 +460,12 @@
     other_heads = swapped(heads)
     head_params = (pick(heads, other_heads), pick(other_heads, heads))
     c_loc, n_loc, g_loc = conv_bias.shape[1], norm_gain.shape[1], gate_gain.shape[1]
-    weights = []
+    gathered = []
     for layer in range(2):
         shards = tuple(pick(m, o) if layer == 0 else pick(o, m) for m, o in zip(mine, theirs))
-        w_in, w_out = (lax.all_gather(s, WEIGHT_AXES, axis=0, tiled=True) for s in shards)
+        gathered.append(tuple(lax.all_gather(s, WEIGHT_AXES, axis=0, tiled=True) for s in shards))
+
+    def unpacked(layer, w_in, w_out):
         own = w_in[:, E:].reshape(share_count, rows * extra)[:, :small_count].astype(f32)
         cuts = [0, CONVK * c_loc, CONVK * c_loc + c_loc, CONVK * c_loc + c_loc + n_loc]
         conv_w = own[:, : cuts[1]].reshape(share_count, CONVK, c_loc).transpose(1, 0, 2).reshape(CONVK, CH)
@@ -478,19 +473,23 @@
         norm_g = own[:, cuts[2] : cuts[3]].reshape(1, D)
         gate_g = own[:, cuts[3] :].reshape(1, DI)
         hp = head_params[layer]
-        weights.append((w_in, w_out, conv_w, conv_b, norm_g, gate_g, hp[0:1], hp[1:2], hp[2:3]))
+        return (w_in, w_out, conv_w, conv_b, norm_g, gate_g, hp[0:1], hp[1:2], hp[2:3])
 
     stream = pick(tokens[0, 0], tokens[1, 0])
-    acts, kept = [], []
+    acts, kept, weights = [], [], []
     for layer in range(2):
+        w_in, w_out = gathered[layer]
+        if layer > 0:
+            stream, w_in, w_out = tied(stream, w_in, w_out)
+        weights.append(unpacked(layer, w_in, w_out))
         stream, saved = layer_forward(stream, weights[layer])
         acts.append(stream)
         kept.append(saved)
     grad = pick(cotangent[0, 0], cotangent[1, 0])
-    grads, sums = [None, None], [None, None]
+    grads, sums, rests = [None, None], [None, None], [None, None]
     queue = Queue()
     for layer in (1, 0):
-        grad, sums[layer] = layer_backward(grad, kept[layer], weights[layer], queue)
+        grad, sums[layer], rests[layer] = layer_backward(grad, kept[layer], weights[layer], queue)
         grads[layer] = grad
         grad = grad.astype(bf16)
         if layer == 1:
@@ -512,21 +511,24 @@
         own = pick(low.value[0], high.value[0])
         other = swapped(pick(high.value[0], low.value[0]).astype(low.wire))
         shares.append(own + other.astype(f32))
-    wout, winz, winx, wind, rest = shares
-    rest = rest[0]
+    early, late = shares
+    wout = jnp.concatenate([early[:, :D], early[:, D : 2 * D]], axis=0)
+    rest = pick(*rests)
     parts, start = [], 0
-    for size in [CONVK * c_loc, c_loc, n_loc, g_loc, H, H, H]:
+    for size in [CONVK * CH, CH, D, DI, H, H, H]:
         parts.append(rest[start : start + size])
         start += size
+    share_idx = lax.axis_index("dp") * lax.axis_size("seq") + lax.axis_index("seq")
+    share = lambda a, width: lax.dynamic_slice_in_dim(a, share_idx * width, width, axis=a.ndim - 1)
     return (
         act_out,
         grad_out,
-        jnp.concatenate([winz, winx, wind], axis=1)[None],
+        jnp.concatenate([early[:, 2 * D :], late], axis=1)[None],
         wout[None],
-        parts[0].reshape(CONVK, c_loc)[None],
-        parts[1][None],
-        parts[2][None],
-        parts[3][None],
+        share(parts[0].reshape(CONVK, CH), c_loc)[None],
+        share(parts[1], c_loc)[None],
+        share(parts[2], n_loc)[None],
+        share(parts[3], g_loc)[None],
         parts[4][None],
         parts[5][None],
         parts[6][None],

time: 677 us -> 775 us (1.14)
  waiting for transfers between devices: 242 us -> 408 us
  other arithmetic: 123 us -> 95.3 us
  starting transfers between devices: 99.3 us -> 75.1 us
  matrix products: 71.5 us -> 62.5 us
  local copies, waits for them, and re-layouts: 59.1 us -> 51 us
    psum x0 -> x1, waiting for transfers between devices: none -> 121 us  [layer_backward(): lax.psum(jnp.concatenate([r.reshape(-1) for r in rest]), ('section',) + W...]
    ppermute x40 -> x16, waiting for transfers between devices: 68.3 us -> 99.8 us  [step(): got = lax.ppermute(jnp.where(upper, low, high), axis, pairs)]
    ppermute x40 -> x16, starting transfers between devices: 47.1 us -> 21.8 us  [step(): got = lax.ppermute(jnp.where(upper, low, high), axis, pairs)]
    ppermute x16, waiting for transfers between devices: 36.4 us -> 53.2 us  [shifted(): return lax.ppermute(x, axis, pairs)]
    ppermute x10 -> x7, waiting for transfers between devices: 29.9 us -> 14.3 us  [swapped(): return lax.ppermute(x, 'section', [(0, 1), (1, 0)])]
    select_n x40 -> x16, other arithmetic: 25.8 us -> 12.2 us  [step(): got = lax.ppermute(jnp.where(upper, low, high), axis, pairs)]
    all_gather x4, waiting for transfers between devices: 106 us -> 118 us  [body(): lax.all_gather(s, WEIGHT_AXES, axis=0, tiled=True)]
    reshape x12 -> x6, other arithmetic: 20.1 us -> 9 us  [step(): self.value = total.reshape(2 ** len(self.bits), rows, cols)]
  transfers between devices with their start and end apart: 70 -> 44, of which waited for: 33 -> 26; matrix products, arithmetic and copies ran while one was open for 31% -> 19% of each run, Pallas kernels for 7% -> 5%
where the time goes in v3:
time: 775 us; the launch traced here: 763 us
  waiting for transfers between devices  408 us (53%)
  other arithmetic  95.3 us (12%)
  starting transfers between devices  75.1 us (10%)
  matrix products  62.5 us (8%)
  Pallas kernels  53.7 us (7%)
  local copies, waits for them, and re-layouts  51 us (7%)
  between operations  17.4 us (2%)
    psum x1, waiting for transfers between devices, layer_backward(): lax.psum(jnp.concatenate([r.reshape(-1) for r in rest]), ('section',) + W...  121 us
    all_gather x4, waiting for transfers between devices, body(): lax.all_gather(s, WEIGHT_AXES, axis=0, tiled=True)  118 us
    ppermute x16, waiting for transfers between devices, step(): got = lax.ppermute(jnp.where(upper, low, high), axis, pairs)  99.8 us
    dot_general x38, matrix products, dot(): lax.dot_general(left, right, (dims, ((), ())), preferred_element_type=f32...  62.5 us
    ppermute x16, waiting for transfers between devices, shifted(): return lax.ppermute(x, axis, pairs)  53.2 us
    ppermute x16, starting transfers between devices, shifted(): return lax.ppermute(x, axis, pairs)  41.9 us
    pallas_call x2, Pallas kernels, mix_grad(): call(mix_grad_kernel, (shaped(t, DI), shaped(PAIRS, 2, t), shaped(t, PAIR...  22.5 us
    ppermute x16, starting transfers between devices, step(): got = lax.ppermute(jnp.where(upper, low, high), axis, pairs)  21.8 us
  transfers between devices with their start and end apart: 44, of which 26 were waited for; matrix products, arithmetic and copies ran while one was open for 19% of the time, Pallas kernels for 5%

profile of v3, /device:TPU:0, one launch (start us, length us, event | category | flops | bytes accessed | tf_op | source)
XLA Modules:
  0.0 763.2 jit_solution(1292705420316475580)
XLA Ops:
  13.0 7.8 %collective-permute-done = bf16[48,3456]{1,0:T(8,128)(2,1)S(1)} collective-permute-done((bf16[48,3456]{1,0:T(8,128)(2,1)S(1)}, bf16[48,3456]{1,0:T(8,128)(2,1)S(1)}, u32[]{:S(2)}, u32[]{:S(2)}) %collective-permute-start) | collective-permute-done | bytes 331808 | tf_op jit(solution)/shard_map/ppermute | solution.py:47
  24.6 3.4 collective-permute-done.6
  34.7 46.1 %all-gather.5.cloned.1.call-done = bf16[768,3456]{1,0:T(8,128)(2,1)} async-done(((bf16[48,3456]{1,0:T(8,128)(2,1)}), bf16[768,3456]{1,0:T(8,128)(2,1)}) %all-gather.5.cloned.1.call-update) | async-done | bytes 5308432 | tf_op jit(solution)/shard_map/all_gather | solution.py:466
  82.3 4.2 convolution_convert_fusion.1
  86.6 3.4 collective-permute-start.1
  97.6 3.7 collective-permute-start.3
  104.8 4.7 shard_map.194.part_ref
  113.8 4.4 collective-permute-start.4
  118.2 8.9 %collective-permute-done.4 = bf16[128,1536]{1,0:T(8,128)(2,1)S(1)} collective-permute-done((bf16[128,1536]{1,0:T(8,128)(2,1)S(1)}, bf16[128,1536]{1,0:T(8,128)(2,1)S(1)}, u32[]{:S(2)}, u32[]{:S(2)}) %collective-permute-start.4) | collective-permute-done | bytes 393248 | tf_op jit(solution)/shard_map/ppermute | solution.py:43
  127.2 4.4 collective-permute-start.5
  132.0 9.9 %collective-permute-done.5.held_ref = bf16[128,1536]{1,0:T(8,128)(2,1)S(1)} collective-permute-done((bf16[128,1536]{1,0:T(8,128)(2,1)S(1)}, bf16[128,1536]{1,0:T(8,128)(2,1)S(1)}, u32[]{:S(2)}, u32[]{:S(2)}) %collective-permute-start.5) | collective-permute-done | bytes 393248 | tf_op jit(solution)/shard_map/ppermute | solution.py:43
  143.3 4.3 shard_map.195
  147.7 3.3 multiply_reduce_fusion.5
  154.4 15.2 %all-gather.11.cloned.1.call-done = bf16[1536,768]{1,0:T(8,128)(2,1)} async-done(((bf16[96,768]{1,0:T(8,128)(2,1)}), bf16[1536,768]{1,0:T(8,128)(2,1)}) %all-gather.11.cloned.1.call-update) | async-done | bytes 2359312 | tf_op jit(solution)/shard_map/all_gather | solution.py:466
  169.5 57.2 %all-gather.9.cloned.1.call-done = bf16[768,3456]{1,0:T(8,128)(2,1)} async-done(((bf16[48,3456]{1,0:T(8,128)(2,1)}), bf16[768,3456]{1,0:T(8,128)(2,1)}) %all-gather.9.cloned.1.call-update) | async-done | bytes 5308432 | tf_op jit(solution)/shard_map/all_gather | solution.py:466
  228.4 4.2 convolution_convert_fusion
  235.0 3.8 collective-permute-start.7
  244.5 3.7 multiply_convert_fusion.x_ref.b_ref.c_ref
  249.6 3.6 collective-permute-start.8
  259.6 4.7 shard_map.196.part_ref
  268.3 8.2 %collective-permute-done.9 = bf16[128,1536]{1,0:T(8,128)(2,1)S(1)} collective-permute-done((bf16[128,1536]{1,0:T(8,128)(2,1)S(1)}, bf16[128,1536]{1,0:T(8,128)(2,1)S(1)}, u32[]{:S(2)}, u32[]{:S(2)}) %collective-permute-start.9) | collective-permute-done | bytes 393248 | tf_op jit(solution)/shard_map/ppermute | solution.py:43
  277.4 5.2 collective-permute-start.10
  283.4 6.0 collective-permute-done.10.held_ref
  292.2 7.0 shard_map.197
  305.7 5.2 shard_map.198
  314.1 8.5 %collective-permute-done.12 = bf16[128,1536]{1,0:T(8,128)(2,1)S(1)} collective-permute-done((bf16[128,1536]{1,0:T(8,128)(2,1)S(1)}, bf16[128,1536]{1,0:T(8,128)(2,1)S(1)}, u32[]{:S(2)}, u32[]{:S(2)}) %collective-permute-start.12) | collective-permute-done | bytes 393248 | tf_op jit(solution)/shard_map/ppermute | solution.py:43
  328.6 11.6 %shard_map.199 = (f32[256,1536]{1,0:T(8,128)S(1)}, f32[12,2,256]{2,1,0:T(2,128)S(1)}, f32[256,128]{1,0:T(8,128)S(1)}, f32[256,128]{1,0:T(8,128)S(1)}, f32[256,128]{1,0:T(8,128)S(1)}) custom-call(bf16[256,1536]{1,0:T(8,128)(2,1)S(1)} %copy-done.7, bf16[256,1792]{1,0:T(8,128)(2,1)S(1)} %multiply_convert_fusion.x_ref.b_ref.c_ref, ...), custom_call_target="tpu_custom_call" | custom-call | tf_op jit(solution)/shard_map/pallas_call | solution.py:297
  340.3 3.6 fusion.1
  351.1 24.1 %collective-permute-done.16 = bf16[1,4,48,3072]{3,2,1,0:T(8,128)(2,1)} collective-permute-done((bf16[1,4,48,3072]{3,2,1,0:T(8,128)(2,1)}, bf16[1,4,48,3072]{3,2,1,0:T(8,128)(2,1)}, u32[]{:S(2)}, u32[]{:S(2)}) %collective-permute-start.16) | collective-permute-done | bytes 1179680 | tf_op jit(solution)/shard_map/ppermute | solution.py:98
  392.0 8.5 %collective-permute-done.17 = bf16[2,1,48,3072]{3,2,0,1:T(8,128)(2,1)} collective-permute-done((bf16[2,1,48,3072]{3,2,0,1:T(8,128)(2,1)}, bf16[2,1,48,3072]{3,2,0,1:T(8,128)(2,1)}, u32[]{:S(2)}, u32[]{:S(2)}) %collective-permute-start.17) | collective-permute-done | bytes 589856 | tf_op jit(solution)/shard_map/ppermute | solution.py:98
  405.2 3.5 collective-permute-done.18
  415.0 4.6 copy.190
  426.9 3.8 concatenate.62
  430.7 5.4 fusion.98
  446.5 5.2 shard_map.200
  455.9 16.3 %collective-permute-done.21 = bf16[1,4,48,1816]{3,2,1,0:T(8,128)(2,1)S(1)} collective-permute-done((bf16[1,4,48,1816]{3,2,1,0:T(8,128)(2,1)S(1)}, bf16[1,4,48,1816]{3,2,1,0:T(8,128)(2,1)S(1)}, u32[]{:S(2)}, u32[]{:S(2)}) %collective-permute-start.21) | collective-permute-done | bytes 697376 | tf_op jit(solution)/shard_map/ppermute | solution.py:98
  476.5 3.5 collective-permute-start.31
  483.3 10.8 %shard_map.201 = (f32[256,1536]{1,0:T(8,128)S(1)}, f32[12,2,256]{2,1,0:T(2,128)S(1)}, f32[256,128]{1,0:T(8,128)S(1)}, f32[256,128]{1,0:T(8,128)S(1)}, f32[256,128]{1,0:T(8,128)S(1)}) custom-call(bf16[256,1536]{1,0:T(8,128)(2,1)S(1)} %get-tuple-element.85.dy_ref, bf16[256,1792]{1,0:T(8,128)(2,1)S(1)} %multiply_convert_fusion.1.x_ref.b_ref.c_ref, ...), custom_call_target="tpu_custom_call" | custom-call | tf_op jit(solution)/shard_map/pallas_call | solution.py:297
  498.2 5.4 collective-permute-done.22
  512.9 18.7 %collective-permute-done.26 = bf16[1,4,48,3072]{3,2,1,0:T(8,128)(2,1)} collective-permute-done((bf16[1,4,48,3072]{3,2,1,0:T(8,128)(2,1)}, bf16[1,4,48,3072]{3,2,1,0:T(8,128)(2,1)}, u32[]{:S(2)}, u32[]{:S(2)}) %collective-permute-start.26) | collective-permute-done | bytes 1179680 | tf_op jit(solution)/shard_map/ppermute | solution.py:98
  548.7 5.4 collective-permute-done.27
  557.0 3.6 collective-permute-start.30
  566.4 4.7 copy.208
  573.1 5.7 fusion.105
  583.8 121.2 %all-reduce.4.cloned.1.call-done = (f32[11336]{0:T(1024)}, f32[11336]{0:T(1024)}) async-done(((f32[11336]{0:T(1024)}, f32[11336]{0:T(1024)}), (f32[11336]{0:T(1024)}, f32[11336]{0:T(1024)})) %all-reduce.4.cloned.1.call-update) | async-done | bytes 90704 | tf_op jit(solution)/shard_map/psum | solution.py:439
  715.7 13.9 %collective-permute-done.34 = bf16[1,4,48,1816]{3,2,1,0:T(8,128)(2,1)S(1)} collective-permute-done((bf16[1,4,48,1816]{3,2,1,0:T(8,128)(2,1)S(1)}, bf16[1,4,48,1816]{3,2,1,0:T(8,128)(2,1)S(1)}, u32[]{:S(2)}, u32[]{:S(2)}) %collective-permute-start.34) | collective-permute-done | bytes 697376 | tf_op jit(solution)/shard_map/ppermute | solution.py:98
  733.4 5.5 collective-permute-done.35
  742.6 5.0 collective-permute-done.36
  (689 shorter events, 214.8 us)
Async XLA Ops:
  7.2 73.6 %all-gather.5.cloned.1.call-start = ((), (), s32[]{:S(2)}) async-start(), calls=%async_computation | async-start | bytes 5640192 | tf_op jit(solution)/shard_map/all_gather | solution.py:466
  10.1 10.8 %collective-permute-start = (bf16[48,3456]{1,0:T(8,128)(2,1)S(1)}, bf16[48,3456]{1,0:T(8,128)(2,1)S(1)}, u32[]{:S(2)}, u32[]{:S(2)}) collective-permute-start(bf16[48,3456]{1,0:T(8,128)(2,1)S(1)} %pad_maximum_fusion.6), channel_id=1, source_target_pairs={{0,16},{16,0},{1,17},{17,1},{2,18},{18,2},{3,19},{19,3},{4,20},{20... | collective-permute-start | bytes 995336 | tf_op jit(solution)/shard_map/ppermute | solution.py:47
  22.8 128.3 %all-gather.7.cloned.1.call-start = ((), (), s32[]{:S(2)}) async-start(), calls=%async_computation.1 | async-start | bytes 2506752 | tf_op jit(solution)/shard_map/all_gather | solution.py:466
  22.8 5.2 collective-permute-start.6
  28.8 140.7 %all-gather.11.cloned.1.call-start = ((), (), s32[]{:S(2)}) async-start(), calls=%async_computation.3 | async-start | bytes 2506752 | tf_op jit(solution)/shard_map/all_gather | solution.py:466
  29.5 197.2 %all-gather.9.cloned.1.call-start = ((), (), s32[]{:S(2)}) async-start(), calls=%async_computation.2 | async-start | bytes 5640192 | tf_op jit(solution)/shard_map/all_gather | solution.py:466
  30.1 674.9 %all-reduce.4.cloned.1.call-start = ((), (), s32[]{:S(2)}) async-start(), calls=%async_computation.4 | async-start | bytes 196608 | tf_op jit(solution)/shard_map/psum | solution.py:439
  30.2 3.7 collective-permute-start.2
  32.0 394.1 %copy-start.95 = (s32[1536]{0:T(1024)}, s32[1536]{0:T(1024)S(1)}, u32[]{:S(2)}) copy-start(s32[1536]{0:T(1024)S(1)} %iota_shift-right-logical_fusion) | copy-start | bytes 18436
  32.0 225.9 %copy-start.98 = (s32[1536]{0:T(1024)}, s32[1536]{0:T(1024)S(1)}, u32[]{:S(2)}) copy-start(s32[1536]{0:T(1024)S(1)} %broadcast_add_fusion) | copy-start | bytes 18436
  86.6 7.7 %collective-permute-start.1 = (bf16[16,1792]{1,0:T(8,128)(2,1)S(1)}, bf16[16,1792]{1,0:T(8,128)(2,1)S(1)}, u32[]{:S(2)}, u32[]{:S(2)}) collective-permute-start(bf16[16,1792]{1,0:T(8,128)(2,1)S(1)} %slice.466), channel_id=1, source_target_pairs={{0,1},{1,2},{2,3},{4,5},{5,6},{6,7},{8,9},{9,10},{10,11},{12,13},{... | collective-permute-start | bytes 172040 | tf_op jit(solution)/shard_map/ppermute | solution.py:43
  97.6 15.1 %collective-permute-start.3 = (bf16[128,1536]{1,0:T(8,128)(2,1)}, bf16[128,1536]{1,0:T(8,128)(2,1)}, u32[]{:S(2)}, u32[]{:S(2)}) collective-permute-start(bf16[128,1536]{1,0:T(8,128)(2,1)} %get-tuple-element.234), channel_id=1, source_target_pairs={{0,1},{1,2},{2,3},{4,5},{5,6},{6,7},{8,9},{9,10},{10,11},{12,13},{... | collective-permute-start | bytes 1179656 | tf_op jit(solution)/shard_map/ppermute | solution.py:43
  113.8 13.3 %collective-permute-start.4 = (bf16[128,1536]{1,0:T(8,128)(2,1)S(1)}, bf16[128,1536]{1,0:T(8,128)(2,1)S(1)}, u32[]{:S(2)}, u32[]{:S(2)}) collective-permute-start(bf16[128,1536]{1,0:T(8,128)(2,1)S(1)} %add_convert_fusion.7), channel_id=1, source_target_pairs={{0,1},{1,2},{2,3},{4,5},{5,6},{6,7},{8,9},{9,10},{10,11},{12,13},{... | collective-permute-start | bytes 1179656 | tf_op jit(solution)/shard_map/ppermute | solution.py:43
  127.2 14.7 %collective-permute-start.5 = (bf16[128,1536]{1,0:T(8,128)(2,1)S(1)}, bf16[128,1536]{1,0:T(8,128)(2,1)S(1)}, u32[]{:S(2)}, u32[]{:S(2)}) collective-permute-start(bf16[128,1536]{1,0:T(8,128)(2,1)S(1)} %add_convert_fusion.6), channel_id=1, source_target_pairs={{0,1},{1,2},{2,3},{4,5},{5,6},{6,7},{8,9},{9,10},{10,11},{12,13},{... | collective-permute-start | bytes 1179656 | tf_op jit(solution)/shard_map/ppermute | solution.py:43
  131.7 100.9 %copy-start.198 = (f32[24]{0:T(128)}, f32[24]{0:T(128)S(1)}, u32[]{:S(2)}) copy-start(f32[24]{0:T(128)S(1)} %get-tuple-element.231) | copy-start | bytes 292
  131.7 107.1 %copy-start.176 = (f32[24]{0:T(128)}, f32[24]{0:T(128)S(1)}, u32[]{:S(2)}) copy-start(f32[24]{0:T(128)S(1)} %get-tuple-element.230) | copy-start | bytes 292
  235.0 9.4 %collective-permute-start.7 = (bf16[16,1792]{1,0:T(8,128)(2,1)S(1)}, bf16[16,1792]{1,0:T(8,128)(2,1)S(1)}, u32[]{:S(2)}, u32[]{:S(2)}) collective-permute-start(bf16[16,1792]{1,0:T(8,128)(2,1)S(1)} %slice.487), channel_id=1, source_target_pairs={{0,1},{1,2},{2,3},{4,5},{5,6},{6,7},{8,9},{9,10},{10,11},{12,13},{... | collective-permute-start | bytes 172040 | tf_op jit(solution)/shard_map/ppermute | solution.py:43
  249.6 15.9 %collective-permute-start.8 = (bf16[128,1536]{1,0:T(8,128)(2,1)}, bf16[128,1536]{1,0:T(8,128)(2,1)}, u32[]{:S(2)}, u32[]{:S(2)}) collective-permute-start(bf16[128,1536]{1,0:T(8,128)(2,1)} %get-tuple-element.236), channel_id=1, source_target_pairs={{0,1},{1,2},{2,3},{4,5},{5,6},{6,7},{8,9},{9,10},{10,11},{12,13},{... | collective-permute-start | bytes 1179656 | tf_op jit(solution)/shard_map/ppermute | solution.py:43
  266.6 10.0 %collective-permute-start.9 = (bf16[128,1536]{1,0:T(8,128)(2,1)S(1)}, bf16[128,1536]{1,0:T(8,128)(2,1)S(1)}, u32[]{:S(2)}, u32[]{:S(2)}) collective-permute-start(bf16[128,1536]{1,0:T(8,128)(2,1)S(1)} %add_convert_fusion.5), channel_id=1, source_target_pairs={{0,1},{1,2},{2,3},{4,5},{5,6},{6,7},{8,9},{9,10},{10,11},{12,13},{... | collective-permute-start | bytes 1179656 | tf_op jit(solution)/shard_map/ppermute | solution.py:43
  277.4 12.0 %collective-permute-start.10 = (bf16[128,1536]{1,0:T(8,128)(2,1)}, bf16[128,1536]{1,0:T(8,128)(2,1)}, u32[]{:S(2)}, u32[]{:S(2)}) collective-permute-start(bf16[128,1536]{1,0:T(8,128)(2,1)} %add_convert_fusion.4), channel_id=1, source_target_pairs={{0,1},{1,2},{2,3},{4,5},{5,6},{6,7},{8,9},{9,10},{10,11},{12,13},{... | collective-permute-start | bytes 1179656 | tf_op jit(solution)/shard_map/ppermute | solution.py:43
  311.0 11.6 %collective-permute-start.12 = (bf16[128,1536]{1,0:T(8,128)(2,1)S(1)}, bf16[128,1536]{1,0:T(8,128)(2,1)S(1)}, u32[]{:S(2)}, u32[]{:S(2)}) collective-permute-start(bf16[128,1536]{1,0:T(8,128)(2,1)S(1)} %convert_element_type.602), channel_id=1, source_target_pairs={{1,0},{2,1},{3,2},{5,4},{6,5},{7,6},{9,8},{10,9},{11,10},{13,12},{... | collective-permute-start | bytes 1179656 | tf_op jit(solution)/shard_map/ppermute | solution.py:43
  324.3 16.0 %collective-permute-start.14 = (bf16[2,4,48,3072]{3,2,1,0:T(8,128)(2,1)}, bf16[2,4,48,3072]{3,2,1,0:T(8,128)(2,1)}, u32[]{:S(2)}, u32[]{:S(2)}) collective-permute-start(bf16[2,4,48,3072]{3,2,1,0:T(8,128)(2,1)} %fusion.4), channel_id=1, source_target_pairs={{0,4},{4,0},{8,12},{12,8},{1,5},{5,1},{9,13},{13,9},{2,6},{6,2},{1... | collective-permute-start | bytes 7077896 | tf_op jit(solution)/shard_map/ppermute | solution.py:98
  325.8 18.2 %collective-permute-start.13 = (bf16[128,1536]{1,0:T(8,128)(2,1)S(1)}, bf16[128,1536]{1,0:T(8,128)(2,1)S(1)}, u32[]{:S(2)}, u32[]{:S(2)}) collective-permute-start(bf16[128,1536]{1,0:T(8,128)(2,1)S(1)} %add_convert_fusion.3), channel_id=1, source_target_pairs={{1,0},{2,1},{3,2},{5,4},{6,5},{7,6},{9,8},{10,9},{11,10},{13,12},{... | collective-permute-start | bytes 1179656 | tf_op jit(solution)/shard_map/ppermute | solution.py:43
  346.5 28.7 %collective-permute-start.16 = (bf16[1,4,48,3072]{3,2,1,0:T(8,128)(2,1)}, bf16[1,4,48,3072]{3,2,1,0:T(8,128)(2,1)}, u32[]{:S(2)}, u32[]{:S(2)}) collective-permute-start(bf16[1,4,48,3072]{3,2,1,0:T(8,128)(2,1)} %select_bitcast_fusion.4), channel_id=1, source_target_pairs={{0,8},{4,12},{8,0},{12,4},{1,9},{5,13},{9,1},{13,5},{2,10},{6,14},... | collective-permute-start | bytes 3538952 | tf_op jit(solution)/shard_map/ppermute | solution.py:98
  349.7 28.1 %collective-permute-start.15 = (bf16[128,1536]{1,0:T(8,128)(2,1)S(1)}, bf16[128,1536]{1,0:T(8,128)(2,1)S(1)}, u32[]{:S(2)}, u32[]{:S(2)}) collective-permute-start(bf16[128,1536]{1,0:T(8,128)(2,1)S(1)} %add_convert_fusion.2), channel_id=1, source_target_pairs={{1,0},{2,1},{3,2},{5,4},{6,5},{7,6},{9,8},{10,9},{11,10},{13,12},{... | collective-permute-start | bytes 1179656 | tf_op jit(solution)/shard_map/ppermute | solution.py:43
  384.9 15.6 %collective-permute-start.17 = (bf16[2,1,48,3072]{3,2,0,1:T(8,128)(2,1)}, bf16[2,1,48,3072]{3,2,0,1:T(8,128)(2,1)}, u32[]{:S(2)}, u32[]{:S(2)}) collective-permute-start(bf16[2,1,48,3072]{3,2,0,1:T(8,128)(2,1)} %fusion.112), channel_id=1, source_target_pairs={{0,1},{1,0},{2,3},{3,2},{4,5},{5,4},{6,7},{7,6},{8,9},{9,8},{10,11... | collective-permute-start | bytes 1769480 | tf_op jit(solution)/shard_map/ppermute | solution.py:98
  402.6 6.1 collective-permute-start.18
  422.9 14.5 %collective-permute-start.19 = (bf16[2,4,48,1816]{3,2,1,0:T(8,128)(2,1)}, bf16[2,4,48,1816]{3,2,1,0:T(8,128)(2,1)}, u32[]{:S(2)}, u32[]{:S(2)}) collective-permute-start(bf16[2,4,48,1816]{3,2,1,0:T(8,128)(2,1)} %select_bitcast_fusion.2), channel_id=1, source_target_pairs={{0,4},{4,0},{8,12},{12,8},{1,5},{5,1},{9,13},{13,9},{2,6},{6,2},{1... | collective-permute-start | bytes 4184072 | tf_op jit(solution)/shard_map/ppermute | solution.py:98
  424.6 48.3 %collective-permute-start.11 = (bf16[256,768]{1,0:T(8,128)(2,1)}, bf16[256,768]{1,0:T(8,128)(2,1)}, u32[]{:S(2)}, u32[]{:S(2)}) collective-permute-start(bf16[256,768]{1,0:T(8,128)(2,1)} %get-tuple-element.238), channel_id=1, source_target_pairs={{0,16},{16,0},{1,17},{17,1},{2,18},{18,2},{3,19},{19,3},{4,20},{20... | collective-permute-start | bytes 1179656 | tf_op jit(solution)/shard_map/ppermute | solution.py:47
  451.9 20.7 %collective-permute-start.20 = (bf16[128,1536]{1,0:T(8,128)(2,1)S(1)}, bf16[128,1536]{1,0:T(8,128)(2,1)S(1)}, u32[]{:S(2)}, u32[]{:S(2)}) collective-permute-start(bf16[128,1536]{1,0:T(8,128)(2,1)S(1)} %convert_element_type.634), channel_id=1, source_target_pairs={{1,0},{2,1},{3,2},{5,4},{6,5},{7,6},{9,8},{10,9},{11,10},{13,12},{... | collective-permute-start | bytes 1179656 | tf_op jit(solution)/shard_map/ppermute | solution.py:43
  453.6 18.7 %collective-permute-start.21 = (bf16[1,4,48,1816]{3,2,1,0:T(8,128)(2,1)S(1)}, bf16[1,4,48,1816]{3,2,1,0:T(8,128)(2,1)S(1)}, u32[]{:S(2)}, u32[]{:S(2)}) collective-permute-start(bf16[1,4,48,1816]{3,2,1,0:T(8,128)(2,1)S(1)} %select_bitcast_fusion.8), channel_id=1, source_target_pairs={{0,8},{4,12},{8,0},{12,4},{1,9},{5,13},{9,1},{13,5},{2,10},{6,14},... | collective-permute-start | bytes 2092040 | tf_op jit(solution)/shard_map/ppermute | solution.py:98
  472.8 24.1 %collective-permute-start.24 = (bf16[2,4,48,3072]{3,2,1,0:T(8,128)(2,1)S(1)}, bf16[2,4,48,3072]{3,2,1,0:T(8,128)(2,1)S(1)}, u32[]{:S(2)}, u32[]{:S(2)}) collective-permute-start(bf16[2,4,48,3072]{3,2,1,0:T(8,128)(2,1)S(1)} %select_bitcast_fusion), channel_id=1, source_target_pairs={{0,4},{4,0},{8,12},{12,8},{1,5},{5,1},{9,13},{13,9},{2,6},{6,2},{1... | collective-permute-start | bytes 7077896 | tf_op jit(solution)/shard_map/ppermute | solution.py:98
  476.5 236.9 %collective-permute-start.31 = (bf16[1,1,48,3072]{3,2,1,0:T(8,128)(2,1)}, bf16[1,1,48,3072]{3,2,1,0:T(8,128)(2,1)}, u32[]{:S(2)}, u32[]{:S(2)}) collective-permute-start(bf16[1,1,48,3072]{3,2,1,0:T(8,128)(2,1)} %fusion.126), channel_id=1, source_target_pairs={{0,2},{1,3},{2,0},{3,1},{4,6},{5,7},{6,4},{7,5},{8,10},{9,11},{10,... | collective-permute-start | bytes 884744 | tf_op jit(solution)/shard_map/ppermute | solution.py:98
  480.1 16.6 %collective-permute-start.23 = (bf16[2,1,48,1816]{3,2,0,1:T(8,128)(2,1)S(1)}, bf16[2,1,48,1816]{3,2,0,1:T(8,128)(2,1)S(1)}, u32[]{:S(2)}, u32[]{:S(2)}) collective-permute-start(bf16[2,1,48,1816]{3,2,0,1:T(8,128)(2,1)S(1)} %fusion.121), channel_id=1, source_target_pairs={{0,1},{1,0},{2,3},{3,2},{4,5},{5,4},{6,7},{7,6},{8,9},{9,8},{10,11... | collective-permute-start | bytes 1046024 | tf_op jit(solution)/shard_map/ppermute | solution.py:98
  482.0 21.6 %collective-permute-start.22 = (bf16[128,1536]{1,0:T(8,128)(2,1)S(1)}, bf16[128,1536]{1,0:T(8,128)(2,1)S(1)}, u32[]{:S(2)}, u32[]{:S(2)}) collective-permute-start(bf16[128,1536]{1,0:T(8,128)(2,1)S(1)} %add_convert_fusion.1), channel_id=1, source_target_pairs={{1,0},{2,1},{3,2},{5,4},{6,5},{7,6},{9,8},{10,9},{11,10},{13,12},{... | collective-permute-start | bytes 1179656 | tf_op jit(solution)/shard_map/ppermute | solution.py:43
  504.8 26.7 %collective-permute-start.26 = (bf16[1,4,48,3072]{3,2,1,0:T(8,128)(2,1)}, bf16[1,4,48,3072]{3,2,1,0:T(8,128)(2,1)}, u32[]{:S(2)}, u32[]{:S(2)}) collective-permute-start(bf16[1,4,48,3072]{3,2,1,0:T(8,128)(2,1)} %select_bitcast_fusion.3), channel_id=1, source_target_pairs={{0,8},{4,12},{8,0},{12,4},{1,9},{5,13},{9,1},{13,5},{2,10},{6,14},... | collective-permute-start | bytes 3538952 | tf_op jit(solution)/shard_map/ppermute | solution.py:98
  508.6 25.5 %collective-permute-start.25 = (bf16[128,1536]{1,0:T(8,128)(2,1)S(1)}, bf16[128,1536]{1,0:T(8,128)(2,1)S(1)}, u32[]{:S(2)}, u32[]{:S(2)}) collective-permute-start(bf16[128,1536]{1,0:T(8,128)(2,1)S(1)} %add_convert_fusion), channel_id=1, source_target_pairs={{1,0},{2,1},{3,2},{5,4},{6,5},{7,6},{9,8},{10,9},{11,10},{13,12},{... | collective-permute-start | bytes 1179656 | tf_op jit(solution)/shard_map/ppermute | solution.py:43
  510.6 232.0 %collective-permute-start.37 = (bf16[1,1,48,1816]{3,2,1,0:T(8,128)(2,1)}, bf16[1,1,48,1816]{3,2,1,0:T(8,128)(2,1)}, u32[]{:S(2)}, u32[]{:S(2)}) collective-permute-start(bf16[1,1,48,1816]{3,2,1,0:T(8,128)(2,1)} %fusion.132), channel_id=1, source_target_pairs={{0,2},{1,3},{2,0},{3,1},{4,6},{5,7},{6,4},{7,5},{8,10},{9,11},{10,... | collective-permute-start | bytes 523016 | tf_op jit(solution)/shard_map/ppermute | solution.py:98
  540.8 13.2 %collective-permute-start.27 = (bf16[2,1,48,3072]{3,2,0,1:T(8,128)(2,1)}, bf16[2,1,48,3072]{3,2,0,1:T(8,128)(2,1)}, u32[]{:S(2)}, u32[]{:S(2)}) collective-permute-start(bf16[2,1,48,3072]{3,2,0,1:T(8,128)(2,1)} %select_bitcast_fusion.9), channel_id=1, source_target_pairs={{0,1},{1,0},{2,3},{3,2},{4,5},{5,4},{6,7},{7,6},{8,9},{9,8},{10,11... | collective-permute-start | bytes 1769480 | tf_op jit(solution)/shard_map/ppermute | solution.py:98
  555.4 6.1 collective-permute-start.28
  557.0 156.4 %collective-permute-start.30 = (bf16[1,1,48,3072]{3,2,1,0:T(8,128)(2,1)S(1)}, bf16[1,1,48,3072]{3,2,1,0:T(8,128)(2,1)S(1)}, u32[]{:S(2)}, u32[]{:S(2)}) collective-permute-start(bf16[1,1,48,3072]{3,2,1,0:T(8,128)(2,1)S(1)} %select_bitcast_fusion.13), channel_id=1, source_target_pairs={{0,2},{1,3},{2,0},{3,1},{4,6},{5,7},{6,4},{7,5},{8,10},{9,11},{10,... | collective-permute-start | bytes 884744 | tf_op jit(solution)/shard_map/ppermute | solution.py:98
  580.1 128.8 %collective-permute-start.33 = (bf16[2,4,48,1816]{3,2,1,0:T(8,128)(2,1)}, bf16[2,4,48,1816]{3,2,1,0:T(8,128)(2,1)}, u32[]{:S(2)}, u32[]{:S(2)}) collective-permute-start(bf16[2,4,48,1816]{3,2,1,0:T(8,128)(2,1)} %select_bitcast_fusion.1), channel_id=1, source_target_pairs={{0,4},{4,0},{8,12},{12,8},{1,5},{5,1},{9,13},{13,9},{2,6},{6,2},{1... | collective-permute-start | bytes 4184072 | tf_op jit(solution)/shard_map/ppermute | solution.py:98
  583.3 166.8 %collective-permute-start.29 = (f32[256,768]{1,0:T(8,128)}, f32[256,768]{1,0:T(8,128)}, u32[]{:S(2)}, u32[]{:S(2)}) collective-permute-start(f32[256,768]{1,0:T(8,128)} %get-tuple-element.195), channel_id=1, source_target_pairs={{0,16},{16,0},{1,17},{17,1},{2,18},{18,2},{3,19},{19,3},{4,20},{20... | collective-permute-start | bytes 2359304 | tf_op jit(solution)/shard_map/ppermute | solution.py:47
  711.8 17.8 %collective-permute-start.34 = (bf16[1,4,48,1816]{3,2,1,0:T(8,128)(2,1)S(1)}, bf16[1,4,48,1816]{3,2,1,0:T(8,128)(2,1)S(1)}, u32[]{:S(2)}, u32[]{:S(2)}) collective-permute-start(bf16[1,4,48,1816]{3,2,1,0:T(8,128)(2,1)S(1)} %select_bitcast_fusion.7), channel_id=1, source_target_pairs={{0,8},{4,12},{8,0},{12,4},{1,9},{5,13},{9,1},{13,5},{2,10},{6,14},... | collective-permute-start | bytes 2092040 | tf_op jit(solution)/shard_map/ppermute | solution.py:98
  714.6 17.5 %collective-permute-start.32 = (bf16[48,3072]{1,0:T(8,128)(2,1)S(1)}, bf16[48,3072]{1,0:T(8,128)(2,1)S(1)}, u32[]{:S(2)}, u32[]{:S(2)}) collective-permute-start(bf16[48,3072]{1,0:T(8,128)(2,1)S(1)} %fusion.125), channel_id=1, source_target_pairs={{0,16},{16,0},{1,17},{17,1},{2,18},{18,2},{3,19},{19,3},{4,20},{20... | collective-permute-start | bytes 884744 | tf_op jit(solution)/shard_map/ppermute | solution.py:47
  730.0 9.0 %collective-permute-start.35 = (bf16[2,1,48,1816]{3,2,0,1:T(8,128)(2,1)S(1)}, bf16[2,1,48,1816]{3,2,0,1:T(8,128)(2,1)S(1)}, u32[]{:S(2)}, u32[]{:S(2)}) collective-permute-start(bf16[2,1,48,1816]{3,2,0,1:T(8,128)(2,1)S(1)} %select_bitcast_fusion.12), channel_id=1, source_target_pairs={{0,1},{1,0},{2,3},{3,2},{4,5},{5,4},{6,7},{7,6},{8,9},{9,8},{10,11... | collective-permute-start | bytes 1046024 | tf_op jit(solution)/shard_map/ppermute | solution.py:98
  739.1 8.5 %collective-permute-start.36 = (bf16[1,1,48,1816]{3,2,1,0:T(8,128)(2,1)S(1)}, bf16[1,1,48,1816]{3,2,1,0:T(8,128)(2,1)S(1)}, u32[]{:S(2)}, u32[]{:S(2)}) collective-permute-start(bf16[1,1,48,1816]{3,2,1,0:T(8,128)(2,1)S(1)} %select_bitcast_fusion.14), channel_id=1, source_target_pairs={{0,2},{1,3},{2,0},{3,1},{4,6},{5,7},{6,4},{7,5},{8,10},{9,11},{10,... | collective-permute-start | bytes 523016 | tf_op jit(solution)/shard_map/ppermute | solution.py:98
  748.6 5.6 collective-permute-start.38
  (200 other events, 1568.2 us)
Sparse Core Ops, SparseCore 0:
  22.9 57.8 all-gather.4
  83.1 41.0 all-gather.6
  127.0 42.4 all-gather.10
  171.6 55.1 all-gather.8
  581.1 123.9 all-reduce.3

commit v4 on v2

--- a/solution.py
+++ b/solution.py
@@ -74,8 +74,7 @@
     def __init__(self, grad, late_dp, wire=bf16):
         sizes = {a: lax.axis_size(a) for a in WEIGHT_AXES}
         self.bits = [(a, b) for a in WEIGHT_AXES for b in reversed(range(sizes[a].bit_length() - 1))]
-        count = sizes["dp"] * sizes["seq"]
-        self.value = grad.astype(wire).reshape(count, grad.shape[0] // count, grad.shape[1])
+        self.value = grad.astype(wire)
         dp = sorted(b for b in self.bits if b[0] == "dp")
         seq = sorted(b for b in self.bits if b[0] == "seq")
         self.order = dp[:1] + (seq + dp[1:] if late_dp else dp[1:] + seq)
@@ -326,7 +325,7 @@
     return inv_rms, values * inv_rms
 
 
-def layer_forward(layer_in, weights):
+def layer_forward(layer_in, weights, awaited=()):
     w_in, w_out, conv_w, conv_b, norm_g, gate_g, bias_dt, log_rate, skip_gain = weights
     t = layer_in.shape[0]
     _, normed = rms_parts(layer_in.astype(f32))
@@ -352,7 +351,7 @@
     dt_t = dt.T.reshape(PAIRS, 2, t)
     skip_wide = expand(skip_gain)
     part = intra(acts, cum_wide, cum_t, dt_t, skip_wide)
-    incoming, part = tied(incoming, part)
+    incoming, part, *awaited = tied(incoming, part, *awaited)
     for _ in range(lax.axis_size("seq") - 2):
         incoming = shifted((totals_wide * incoming.astype(f32) + states).astype(bf16), "seq", 1)
     y = inter(acts, cum_wide, incoming, part)
@@ -360,7 +359,7 @@
     _, q = rms_parts(y * jax.nn.silu(gate_cols))
     mixed = layer_in.astype(f32) + dot((q * gate_g).astype(bf16), w_out)
     kept = (layer_in, projected, padded, acts, conv, dt, cum, cum_wide, cum_t, dt_t, skip_wide, incoming, y, weighted, factor_wide, totals, totals_wide)
-    return mixed.astype(bf16), kept
+    return mixed.astype(bf16), kept, awaited
 
 
 def layer_backward(grad_v, kept, weights, queue):
@@ -385,14 +384,19 @@
     inv_rms, normed = rms_parts(layer_in.astype(f32))
     un = (normed * norm_g).astype(bf16)
     grad_win_z = rows_dot(un, dz)
-    wout_sum = queue.add(grad_wout, False)
-    winz_sum = queue.add(grad_win_z, True)
+    count = lax.axis_size("dp") * lax.axis_size("seq")
+    early = jnp.concatenate(
+        [*grad_wout.astype(bf16).reshape(count, 2, -1, D).transpose(1, 0, 2, 3), grad_win_z.astype(bf16).reshape(count, -1, DI)],
+        axis=2,
+    )
+    early_sum = queue.add(early, False)
     leave, dy = queue.advance(leave, dy)
     for hop in range(lax.axis_size("seq") - 2):
         leave = shifted((totals_wide * leave.astype(f32) + dheld).astype(bf16), "seq", -1)
         if hop == 0:
             dx, dstep_t, dcum, db, dc = mix_grad(dy, acts, cum_wide, cum_t, dt_t, incoming, skip_wide)
             leave, dx = queue.advance(leave, dx)
+    leave, dx = queue.advance(leave, dx)
     dstep = dstep_t.reshape(H, t).T
     dcum = dcum[:, :H] - dstep * dt
     db = db + cols_dot(weighted, leave)
@@ -413,6 +417,7 @@
     draw = dstep * jax.nn.sigmoid(projected[:, DI + CH : E].astype(f32) + bias_dt)
     grad_dtb = jnp.sum(draw, axis=0)
     dconv = jnp.concatenate([dx, db, dc], axis=1) * silu_slope(conv)
+    dconv = queue.advance(dconv)
     edge = shifted(dconv[:8], "seq", -1)
     grad_cb = jnp.sum(dconv, axis=0)
     grad_cw = jnp.stack([jnp.sum(dconv * padded[k : k + t].astype(f32), axis=0) for k in range(CONVK)])
@@ -422,16 +427,14 @@
         dxbc = dxbc + conv_w[k : k + 1] * ext[CONVK - 1 - k : CONVK - 1 - k + t]
     dxbc = dxbc.astype(bf16)
     draw = draw.astype(bf16)
-    half = CH // 2
-    winx_sum = queue.add(rows_dot(un, dxbc[:, :half]), False)
-    wind_sum = queue.add(rows_dot(un, jnp.concatenate([dxbc[:, half:], draw], axis=1)), True)
+    late = rows_dot(un, jnp.concatenate([dxbc, draw], axis=1)).astype(bf16)
+    late_sum = queue.add(late.reshape(count, -1, CH + H), False)
     dxbc = queue.advance(dxbc)
     filler = jnp.zeros((t, w_in.shape[1] - E), bf16)
     dun = cols_dot(jnp.concatenate([dz, dxbc, draw, filler], axis=1), w_in)
     grad_norm_gain = jnp.sum(dun * normed, axis=0)
     dnorm = dun * norm_g
     grad_u = grad_v.astype(f32) + inv_rms * (dnorm - normed * jnp.mean(dnorm * normed, axis=-1, keepdims=True))
-    count = lax.axis_size("dp") * lax.axis_size("seq")
     heads = jnp.concatenate([grad_dtb, grad_alog, grad_skip])
     rest = jnp.concatenate(
         [
@@ -443,8 +446,8 @@
         ],
         axis=1,
     )
-    rest_sum = queue.add(rest, False, f32)
-    return grad_u, (wout_sum, winz_sum, winx_sum, wind_sum, rest_sum)
+    rest_sum = queue.add(rest[:, None], False, f32)
+    return grad_u, (early_sum, late_sum, rest_sum)
 
 
 def body(tokens, cotangent, in_weight, out_weight, conv_weight, conv_bias, norm_gain, gate_gain, dt_bias, a_log, d_skip):
@@ -467,10 +470,12 @@
     other_heads = swapped(heads)
     head_params = (pick(heads, other_heads), pick(other_heads, heads))
     c_loc, n_loc, g_loc = conv_bias.shape[1], norm_gain.shape[1], gate_gain.shape[1]
-    weights = []
+    gathered = []
     for layer in range(2):
         shards = tuple(pick(m, o) if layer == 0 else pick(o, m) for m, o in zip(mine, theirs))
-        w_in, w_out = (lax.all_gather(s, WEIGHT_AXES, axis=0, tiled=True) for s in shards)
+        gathered.append(tuple(lax.all_gather(s, WEIGHT_AXES, axis=0, tiled=True) for s in shards))
+
+    def unpacked(layer, w_in, w_out):
         own = w_in[:, E:].reshape(share_count, rows * extra)[:, :small_count].astype(f32)
         cuts = [0, CONVK * c_loc, CONVK * c_loc + c_loc, CONVK * c_loc + c_loc + n_loc]
         conv_w = own[:, : cuts[1]].reshape(share_count, CONVK, c_loc).transpose(1, 0, 2).reshape(CONVK, CH)
@@ -478,12 +483,17 @@
         norm_g = own[:, cuts[2] : cuts[3]].reshape(1, D)
         gate_g = own[:, cuts[3] :].reshape(1, DI)
         hp = head_params[layer]
-        weights.append((w_in, w_out, conv_w, conv_b, norm_g, gate_g, hp[0:1], hp[1:2], hp[2:3]))
+        return (w_in, w_out, conv_w, conv_b, norm_g, gate_g, hp[0:1], hp[1:2], hp[2:3])
 
     stream = pick(tokens[0, 0], tokens[1, 0])
-    acts, kept = [], []
+    acts, kept, weights = [], [], []
     for layer in range(2):
-        stream, saved = layer_forward(stream, weights[layer])
+        if layer == 0:
+            weights.append(unpacked(0, *gathered[0]))
+            stream, saved, (next_in,) = layer_forward(stream, weights[0], (gathered[1][0],))
+        else:
+            weights.append(unpacked(1, next_in, gathered[1][1]))
+            stream, saved, _ = layer_forward(stream, weights[1])
         acts.append(stream)
         kept.append(saved)
     grad = pick(cotangent[0, 0], cotangent[1, 0])
@@ -512,7 +522,8 @@
         own = pick(low.value[0], high.value[0])
         other = swapped(pick(high.value[0], low.value[0]).astype(low.wire))
         shares.append(own + other.astype(f32))
-    wout, winz, winx, wind, rest = shares
+    early, late, rest = shares
+    wout = jnp.concatenate([early[:, :D], early[:, D : 2 * D]], axis=0)
     rest = rest[0]
     parts, start = [], 0
     for size in [CONVK * c_loc, c_loc, n_loc, g_loc, H, H, H]:
@@ -521,7 +532,7 @@
     return (
         act_out,
         grad_out,
-        jnp.concatenate([winz, winx, wind], axis=1)[None],
+        jnp.concatenate([early[:, 2 * D :], late], axis=1)[None],
         wout[None],
         parts[0].reshape(CONVK, c_loc)[None],
         parts[1][None],

time: 677 us -> 643 us (0.950)
  starting transfers between devices: 99.3 us -> 87.9 us
  other arithmetic: 123 us -> 114 us
  local copies, waits for them, and re-layouts: 59.1 us -> 52 us
    ppermute x40 -> x24, waiting for transfers between devices: 68.3 us -> 94 us  [step(): got = lax.ppermute(jnp.where(upper, low, high), axis, pairs)]
    all_gather x4, waiting for transfers between devices: 106 us -> 81.6 us  [body(): lax.all_gather(s, WEIGHT_AXES, axis=0, tiled=True)]
    ppermute x10 -> x8, waiting for transfers between devices: 29.9 us -> 15.3 us  [swapped(): return lax.ppermute(x, 'section', [(0, 1), (1, 0)])]
    ppermute x40 -> x24, starting transfers between devices: 47.1 us -> 32.9 us  [step(): got = lax.ppermute(jnp.where(upper, low, high), axis, pairs)]
    ppermute x16, waiting for transfers between devices: 36.4 us -> 45.9 us  [shifted(): return lax.ppermute(x, axis, pairs)]
    reshape x12 -> x8, other arithmetic: 20.1 us -> 13.1 us  [step(): self.value = total.reshape(2 ** len(self.bits), rows, cols)]
    select_n x40 -> x24, other arithmetic: 25.8 us -> 22.2 us  [step(): got = lax.ppermute(jnp.where(upper, low, high), axis, pairs)]
    unnamed x444 -> x408, local copies, waits for them, and re-layouts: 18.2 us -> 15.3 us
  transfers between devices with their start and end apart: 70 -> 52, of which waited for: 33 -> 28; matrix products, arithmetic and copies ran while one was open for 31% -> 27% of each run, Pallas kernels for 7% -> 7%
where the time goes in v4:
time: 643 us; the launch traced here: 631 us
  waiting for transfers between devices  238 us (37%)
  other arithmetic  114 us (18%)
  starting transfers between devices  87.9 us (14%)
  matrix products  69.2 us (11%)
  Pallas kernels  53.4 us (8%)
  local copies, waits for them, and re-layouts  52 us (8%)
  between operations  17.3 us (3%)
    ppermute x24, waiting for transfers between devices, step(): got = lax.ppermute(jnp.where(upper, low, high), axis, pairs)  94 us
    all_gather x4, waiting for transfers between devices, body(): lax.all_gather(s, WEIGHT_AXES, axis=0, tiled=True)  81.6 us
    dot_general x38, matrix products, dot(): lax.dot_general(left, right, (dims, ((), ())), preferred_element_type=f32...  69.2 us
    ppermute x16, waiting for transfers between devices, shifted(): return lax.ppermute(x, axis, pairs)  45.9 us
    ppermute x16, starting transfers between devices, shifted(): return lax.ppermute(x, axis, pairs)  44.7 us
    ppermute x24, starting transfers between devices, step(): got = lax.ppermute(jnp.where(upper, low, high), axis, pairs)  32.9 us
    pallas_call x2, Pallas kernels, mix_grad(): call(mix_grad_kernel, (shaped(t, DI), shaped(PAIRS, 2, t), shaped(t, PAIR...  22.3 us
    select_n x24, other arithmetic, step(): got = lax.ppermute(jnp.where(upper, low, high), axis, pairs)  22.2 us
  transfers between devices with their start and end apart: 52, of which 28 were waited for; matrix products, arithmetic and copies ran while one was open for 27% of the time, Pallas kernels for 7%

profile of v4, /device:TPU:0, one launch (start us, length us, event | category | flops | bytes accessed | tf_op | source)
XLA Modules:
  0.0 631.1 jit_solution(14375923283451576189)
XLA Ops:
  13.0 7.8 %collective-permute-done = bf16[48,3456]{1,0:T(8,128)(2,1)S(1)} collective-permute-done((bf16[48,3456]{1,0:T(8,128)(2,1)S(1)}, bf16[48,3456]{1,0:T(8,128)(2,1)S(1)}, u32[]{:S(2)}, u32[]{:S(2)}) %collective-permute-start) | collective-permute-done | bytes 331808 | tf_op jit(solution)/shard_map/ppermute | solution.py:47
  30.7 50.1 %all-gather.5.cloned.1.call-done = bf16[768,3456]{1,0:T(8,128)(2,1)} async-done(((bf16[48,3456]{1,0:T(8,128)(2,1)}), bf16[768,3456]{1,0:T(8,128)(2,1)}) %all-gather.5.cloned.1.call-update) | async-done | bytes 5308432 | tf_op jit(solution)/shard_map/all_gather | solution.py:476
  82.3 4.2 convolution_convert_fusion.1
  86.5 3.4 collective-permute-start.1
  97.6 3.7 collective-permute-start.3
  104.9 4.7 shard_map.194.part_ref
  110.8 29.0 %all-gather.7.cloned.1.call-done = bf16[768,3456]{1,0:T(8,128)(2,1)} async-done(((bf16[48,3456]{1,0:T(8,128)(2,1)}), bf16[768,3456]{1,0:T(8,128)(2,1)}) %all-gather.7.cloned.1.call-update) | async-done | bytes 5308432 | tf_op jit(solution)/shard_map/all_gather | solution.py:476
  140.8 3.4 collective-permute-start.4
  144.5 11.5 %collective-permute-done.4 = bf16[128,1536]{1,0:T(8,128)(2,1)S(1)} collective-permute-done((bf16[128,1536]{1,0:T(8,128)(2,1)S(1)}, bf16[128,1536]{1,0:T(8,128)(2,1)S(1)}, u32[]{:S(2)}, u32[]{:S(2)}) %collective-permute-start.4) | collective-permute-done | bytes 393248 | tf_op jit(solution)/shard_map/ppermute | solution.py:43
  156.8 4.4 collective-permute-start.5
  164.8 7.4 %collective-permute-done.5.held_ref = bf16[128,1536]{1,0:T(8,128)(2,1)S(1)} collective-permute-done((bf16[128,1536]{1,0:T(8,128)(2,1)}, bf16[128,1536]{1,0:T(8,128)(2,1)S(1)}, u32[]{:S(2)}, u32[]{:S(2)}) %collective-permute-start.5) | collective-permute-done | bytes 393248 | tf_op jit(solution)/shard_map/ppermute | solution.py:43
  173.6 4.3 shard_map.195
  177.9 3.3 multiply_reduce_fusion.5
  186.9 4.3 convolution_convert_fusion
  201.8 5.1 collective-permute-start.8
  212.5 4.7 shard_map.196.part_ref
  221.4 4.4 collective-permute-start.9
  225.8 6.3 collective-permute-done.9
  233.0 5.1 collective-permute-start.10
  245.9 6.9 %shard_map.197 = f32[256,1536]{1,0:T(8,128)S(1)} custom-call(bf16[256,1792]{1,0:T(8,128)(2,1)S(1)} %multiply_convert_fusion.x_ref.b_ref.c_ref, f32[256,1536]{1,0:T(8,128)S(1)} %copy-done.1, bf16[128,1536]{1,0:T(8,128)(2,1)} %collective-permute-done.10.held_ref, f32[256,1536]{1,0:T(8,128)S(1)} %copy-done.18), custom_call_target="tpu_custom_call" | custom-call | tf_op jit(solution)/shard_map/pallas_call | solution.py:277
  258.6 4.0 multiply_reduce_fusion.2
  265.9 5.2 shard_map.198
  274.6 7.0 %collective-permute-done.12 = bf16[128,1536]{1,0:T(8,128)(2,1)S(1)} collective-permute-done((bf16[128,1536]{1,0:T(8,128)(2,1)S(1)}, bf16[128,1536]{1,0:T(8,128)(2,1)S(1)}, u32[]{:S(2)}, u32[]{:S(2)}) %collective-permute-start.12) | collective-permute-done | bytes 393248 | tf_op jit(solution)/shard_map/ppermute | solution.py:43
  283.4 4.2 broadcast_select_fusion.2
  291.3 11.5 %shard_map.199 = (f32[256,1536]{1,0:T(8,128)S(1)}, f32[12,2,256]{2,1,0:T(2,128)S(1)}, f32[256,128]{1,0:T(8,128)S(1)}, f32[256,128]{1,0:T(8,128)S(1)}, f32[256,128]{1,0:T(8,128)S(1)}) custom-call(bf16[256,1536]{1,0:T(8,128)(2,1)S(1)} %copy-done.14, bf16[256,1792]{1,0:T(8,128)(2,1)S(1)} %multiply_convert_fusion.x_ref.b_ref.c_ref, ...), custom_call_target="tpu_custom_call" | custom-call | tf_op jit(solution)/shard_map/pallas_call | solution.py:297
  302.9 3.6 fusion.1
  318.2 20.1 %collective-permute-done.16 = bf16[1,4,48,3072]{3,2,1,0:T(8,128)(2,1)} collective-permute-done((bf16[1,4,48,3072]{3,2,1,0:T(8,128)(2,1)}, bf16[1,4,48,3072]{3,2,1,0:T(8,128)(2,1)}, u32[]{:S(2)}, u32[]{:S(2)}) %collective-permute-start.16) | collective-permute-done | bytes 1179680 | tf_op jit(solution)/shard_map/ppermute | solution.py:98
  354.4 8.4 %collective-permute-done.17 = bf16[2,1,48,3072]{3,2,0,1:T(8,128)(2,1)} collective-permute-done((bf16[2,1,48,3072]{3,2,0,1:T(8,128)(2,1)}, bf16[2,1,48,3072]{3,2,0,1:T(8,128)(2,1)}, u32[]{:S(2)}, u32[]{:S(2)}) %collective-permute-start.17) | collective-permute-done | bytes 589856 | tf_op jit(solution)/shard_map/ppermute | solution.py:98
  367.0 4.0 collective-permute-done.18
  376.7 4.7 copy.236
  385.8 3.8 concatenate.79
  389.6 5.6 fusion.98
  408.0 5.2 shard_map.200
  423.1 12.4 %collective-permute-done.21 = bf16[1,4,48,1816]{3,2,1,0:T(8,128)(2,1)} collective-permute-done((bf16[1,4,48,1816]{3,2,1,0:T(8,128)(2,1)}, bf16[1,4,48,1816]{3,2,1,0:T(8,128)(2,1)}, u32[]{:S(2)}, u32[]{:S(2)}) %collective-permute-start.21) | collective-permute-done | bytes 697376 | tf_op jit(solution)/shard_map/ppermute | solution.py:98
  438.2 4.1 select_bitcast_fusion
  443.0 3.5 collective-permute-start.34
  457.8 10.8 %shard_map.201 = (f32[256,1536]{1,0:T(8,128)S(1)}, f32[12,2,256]{2,1,0:T(2,128)S(1)}, f32[256,128]{1,0:T(8,128)S(1)}, f32[256,128]{1,0:T(8,128)S(1)}, f32[256,128]{1,0:T(8,128)S(1)}) custom-call(bf16[256,1536]{1,0:T(8,128)(2,1)S(1)} %copy-done.12, bf16[256,1792]{1,0:T(8,128)(2,1)S(1)} %multiply_convert_fusion.1.x_ref.b_ref.c_ref, ...), custom_call_target="tpu_custom_call" | custom-call | tf_op jit(solution)/shard_map/pallas_call | solution.py:297
  474.0 4.4 fusion
  483.5 3.3 collective-permute-start.28
  489.1 6.8 %collective-permute-done.28 = f32[2,1,1,776]{3,1,2,0:T(1,128)S(1)} collective-permute-done((f32[2,1,1,776]{3,1,2,0:T(1,128)S(1)}, f32[2,1,1,776]{3,1,2,0:T(1,128)S(1)}, u32[]{:S(2)}, u32[]{:S(2)}) %collective-permute-start.28) | collective-permute-done | bytes 6240 | tf_op jit(solution)/shard_map/ppermute | solution.py:98
  496.5 11.2 %collective-permute-done.29 = bf16[1,4,48,3072]{3,2,1,0:T(8,128)(2,1)} collective-permute-done((bf16[1,4,48,3072]{3,2,1,0:T(8,128)(2,1)}, bf16[1,4,48,3072]{3,2,1,0:T(8,128)(2,1)}, u32[]{:S(2)}, u32[]{:S(2)}) %collective-permute-start.29) | collective-permute-done | bytes 1179680 | tf_op jit(solution)/shard_map/ppermute | solution.py:98
  525.1 6.3 %collective-permute-done.30 = bf16[2,1,48,3072]{3,2,0,1:T(8,128)(2,1)} collective-permute-done((bf16[2,1,48,3072]{3,2,0,1:T(8,128)(2,1)}, bf16[2,1,48,3072]{3,2,0,1:T(8,128)(2,1)}, u32[]{:S(2)}, u32[]{:S(2)}) %collective-permute-start.30) | collective-permute-done | bytes 589856 | tf_op jit(solution)/shard_map/ppermute | solution.py:98
  534.4 4.4 collective-permute-done.31
  543.7 4.7 copy.259
  551.1 5.6 fusion.105
  587.1 11.4 %collective-permute-done.37 = bf16[1,4,48,1816]{3,2,1,0:T(8,128)(2,1)S(1)} collective-permute-done((bf16[1,4,48,1816]{3,2,1,0:T(8,128)(2,1)S(1)}, bf16[1,4,48,1816]{3,2,1,0:T(8,128)(2,1)S(1)}, u32[]{:S(2)}, u32[]{:S(2)}) %collective-permute-start.37) | collective-permute-done | bytes 697376 | tf_op jit(solution)/shard_map/ppermute | solution.py:98
  601.1 5.6 collective-permute-done.38
  610.3 5.1 collective-permute-done.39
  (731 shorter events, 252.5 us)
Async XLA Ops:
  7.2 73.6 %all-gather.5.cloned.1.call-start = ((), (), s32[]{:S(2)}) async-start(), calls=%async_computation | async-start | bytes 5640192 | tf_op jit(solution)/shard_map/all_gather | solution.py:476
  10.1 10.8 %collective-permute-start = (bf16[48,3456]{1,0:T(8,128)(2,1)S(1)}, bf16[48,3456]{1,0:T(8,128)(2,1)S(1)}, u32[]{:S(2)}, u32[]{:S(2)}) collective-permute-start(bf16[48,3456]{1,0:T(8,128)(2,1)S(1)} %pad_maximum_fusion.6), channel_id=1, source_target_pairs={{0,16},{16,0},{1,17},{17,1},{2,18},{18,2},{3,19},{19,3},{4,20},{20... | collective-permute-start | bytes 995336 | tf_op jit(solution)/shard_map/ppermute | solution.py:47
  22.8 116.9 %all-gather.7.cloned.1.call-start = ((), (), s32[]{:S(2)}) async-start(), calls=%async_computation.1 | async-start | bytes 5640192 | tf_op jit(solution)/shard_map/all_gather | solution.py:476
  23.5 160.3 %all-gather.9.cloned.1.call-start = ((), (), s32[]{:S(2)}) async-start(), calls=%async_computation.2 | async-start | bytes 2506752 | tf_op jit(solution)/shard_map/all_gather | solution.py:476
  23.6 6.3 collective-permute-start.6
  30.6 228.0 %all-gather.11.cloned.1.call-start = ((), (), s32[]{:S(2)}) async-start(), calls=%async_computation.3 | async-start | bytes 2506752 | tf_op jit(solution)/shard_map/all_gather | solution.py:476
  86.5 7.7 %collective-permute-start.1 = (bf16[16,1792]{1,0:T(8,128)(2,1)S(1)}, bf16[16,1792]{1,0:T(8,128)(2,1)S(1)}, u32[]{:S(2)}, u32[]{:S(2)}) collective-permute-start(bf16[16,1792]{1,0:T(8,128)(2,1)S(1)} %slice.537), channel_id=1, source_target_pairs={{0,1},{1,2},{2,3},{4,5},{5,6},{6,7},{8,9},{9,10},{10,11},{12,13},{... | collective-permute-start | bytes 172040 | tf_op jit(solution)/shard_map/ppermute | solution.py:43
  97.6 42.1 %collective-permute-start.3 = (bf16[128,1536]{1,0:T(8,128)(2,1)}, bf16[128,1536]{1,0:T(8,128)(2,1)}, u32[]{:S(2)}, u32[]{:S(2)}) collective-permute-start(bf16[128,1536]{1,0:T(8,128)(2,1)} %get-tuple-element.239), channel_id=1, source_target_pairs={{0,1},{1,2},{2,3},{4,5},{5,6},{6,7},{8,9},{9,10},{10,11},{12,13},{... | collective-permute-start | bytes 1179656 | tf_op jit(solution)/shard_map/ppermute | solution.py:43
  140.8 15.2 %collective-permute-start.4 = (bf16[128,1536]{1,0:T(8,128)(2,1)S(1)}, bf16[128,1536]{1,0:T(8,128)(2,1)S(1)}, u32[]{:S(2)}, u32[]{:S(2)}) collective-permute-start(bf16[128,1536]{1,0:T(8,128)(2,1)S(1)} %add_convert_fusion.7), channel_id=1, source_target_pairs={{0,1},{1,2},{2,3},{4,5},{5,6},{6,7},{8,9},{9,10},{10,11},{12,13},{... | collective-permute-start | bytes 1179656 | tf_op jit(solution)/shard_map/ppermute | solution.py:43
  156.8 15.3 %collective-permute-start.5 = (bf16[128,1536]{1,0:T(8,128)(2,1)}, bf16[128,1536]{1,0:T(8,128)(2,1)S(1)}, u32[]{:S(2)}, u32[]{:S(2)}) collective-permute-start(bf16[128,1536]{1,0:T(8,128)(2,1)} %add_convert_fusion.6), channel_id=1, source_target_pairs={{0,1},{1,2},{2,3},{4,5},{5,6},{6,7},{8,9},{9,10},{10,11},{12,13},{... | collective-permute-start | bytes 1179656 | tf_op jit(solution)/shard_map/ppermute | solution.py:43
  193.7 5.4 collective-permute-start.7
  201.8 18.5 %collective-permute-start.8 = (bf16[128,1536]{1,0:T(8,128)(2,1)}, bf16[128,1536]{1,0:T(8,128)(2,1)}, u32[]{:S(2)}, u32[]{:S(2)}) collective-permute-start(bf16[128,1536]{1,0:T(8,128)(2,1)} %get-tuple-element.243), channel_id=1, source_target_pairs={{0,1},{1,2},{2,3},{4,5},{5,6},{6,7},{8,9},{9,10},{10,11},{12,13},{... | collective-permute-start | bytes 1179656 | tf_op jit(solution)/shard_map/ppermute | solution.py:43
  221.4 10.7 %collective-permute-start.9 = (bf16[128,1536]{1,0:T(8,128)(2,1)S(1)}, bf16[128,1536]{1,0:T(8,128)(2,1)S(1)}, u32[]{:S(2)}, u32[]{:S(2)}) collective-permute-start(bf16[128,1536]{1,0:T(8,128)(2,1)S(1)} %add_convert_fusion.5), channel_id=1, source_target_pairs={{0,1},{1,2},{2,3},{4,5},{5,6},{6,7},{8,9},{9,10},{10,11},{12,13},{... | collective-permute-start | bytes 1179656 | tf_op jit(solution)/shard_map/ppermute | solution.py:43
  233.0 10.1 %collective-permute-start.10 = (bf16[128,1536]{1,0:T(8,128)(2,1)}, bf16[128,1536]{1,0:T(8,128)(2,1)}, u32[]{:S(2)}, u32[]{:S(2)}) collective-permute-start(bf16[128,1536]{1,0:T(8,128)(2,1)} %add_convert_fusion.4), channel_id=1, source_target_pairs={{0,1},{1,2},{2,3},{4,5},{5,6},{6,7},{8,9},{9,10},{10,11},{12,13},{... | collective-permute-start | bytes 1179656 | tf_op jit(solution)/shard_map/ppermute | solution.py:43
  271.2 10.4 %collective-permute-start.12 = (bf16[128,1536]{1,0:T(8,128)(2,1)S(1)}, bf16[128,1536]{1,0:T(8,128)(2,1)S(1)}, u32[]{:S(2)}, u32[]{:S(2)}) collective-permute-start(bf16[128,1536]{1,0:T(8,128)(2,1)S(1)} %convert_element_type.602), channel_id=1, source_target_pairs={{1,0},{2,1},{3,2},{5,4},{6,5},{7,6},{9,8},{10,9},{11,10},{13,12},{... | collective-permute-start | bytes 1179656 | tf_op jit(solution)/shard_map/ppermute | solution.py:43
  283.3 19.5 %collective-permute-start.14 = (bf16[2,4,48,3072]{3,2,1,0:T(8,128)(2,1)}, bf16[2,4,48,3072]{3,2,1,0:T(8,128)(2,1)}, u32[]{:S(2)}, u32[]{:S(2)}) collective-permute-start(bf16[2,4,48,3072]{3,2,1,0:T(8,128)(2,1)} %fusion.4), channel_id=1, source_target_pairs={{0,4},{4,0},{8,12},{12,8},{1,5},{5,1},{9,13},{13,9},{2,6},{6,2},{1... | collective-permute-start | bytes 7077896 | tf_op jit(solution)/shard_map/ppermute | solution.py:98
  287.5 26.9 %collective-permute-start.11 = (bf16[256,768]{1,0:T(8,128)(2,1)}, bf16[256,768]{1,0:T(8,128)(2,1)}, u32[]{:S(2)}, u32[]{:S(2)}) collective-permute-start(bf16[256,768]{1,0:T(8,128)(2,1)} %get-tuple-element.245), channel_id=1, source_target_pairs={{0,16},{16,0},{1,17},{17,1},{2,18},{18,2},{3,19},{19,3},{4,20},{20... | collective-permute-start | bytes 1179656 | tf_op jit(solution)/shard_map/ppermute | solution.py:47
  289.3 17.2 %collective-permute-start.13 = (bf16[128,1536]{1,0:T(8,128)(2,1)S(1)}, bf16[128,1536]{1,0:T(8,128)(2,1)S(1)}, u32[]{:S(2)}, u32[]{:S(2)}) collective-permute-start(bf16[128,1536]{1,0:T(8,128)(2,1)S(1)} %add_convert_fusion.3), channel_id=1, source_target_pairs={{1,0},{2,1},{3,2},{5,4},{6,5},{7,6},{9,8},{10,9},{11,10},{13,12},{... | collective-permute-start | bytes 1179656 | tf_op jit(solution)/shard_map/ppermute | solution.py:43
  309.1 29.2 %collective-permute-start.16 = (bf16[1,4,48,3072]{3,2,1,0:T(8,128)(2,1)}, bf16[1,4,48,3072]{3,2,1,0:T(8,128)(2,1)}, u32[]{:S(2)}, u32[]{:S(2)}) collective-permute-start(bf16[1,4,48,3072]{3,2,1,0:T(8,128)(2,1)} %select_bitcast_fusion.4), channel_id=1, source_target_pairs={{0,8},{4,12},{8,0},{12,4},{1,9},{5,13},{9,1},{13,5},{2,10},{6,14},... | collective-permute-start | bytes 3538952 | tf_op jit(solution)/shard_map/ppermute | solution.py:98
  316.8 23.3 %collective-permute-start.15 = (bf16[128,1536]{1,0:T(8,128)(2,1)S(1)}, bf16[128,1536]{1,0:T(8,128)(2,1)S(1)}, u32[]{:S(2)}, u32[]{:S(2)}) collective-permute-start(bf16[128,1536]{1,0:T(8,128)(2,1)S(1)} %add_convert_fusion.2), channel_id=1, source_target_pairs={{1,0},{2,1},{3,2},{5,4},{6,5},{7,6},{9,8},{10,9},{11,10},{13,12},{... | collective-permute-start | bytes 1179656 | tf_op jit(solution)/shard_map/ppermute | solution.py:43
  347.3 15.5 %collective-permute-start.17 = (bf16[2,1,48,3072]{3,2,0,1:T(8,128)(2,1)}, bf16[2,1,48,3072]{3,2,0,1:T(8,128)(2,1)}, u32[]{:S(2)}, u32[]{:S(2)}) collective-permute-start(bf16[2,1,48,3072]{3,2,0,1:T(8,128)(2,1)} %fusion.112), channel_id=1, source_target_pairs={{0,1},{1,0},{2,3},{3,2},{4,5},{5,4},{6,7},{7,6},{8,9},{9,8},{10,11... | collective-permute-start | bytes 1769480 | tf_op jit(solution)/shard_map/ppermute | solution.py:98
  364.9 6.1 collective-permute-start.18
  384.5 13.7 %collective-permute-start.19 = (bf16[2,4,48,1816]{3,2,1,0:T(8,128)(2,1)}, bf16[2,4,48,1816]{3,2,1,0:T(8,128)(2,1)}, u32[]{:S(2)}, u32[]{:S(2)}) collective-permute-start(bf16[2,4,48,1816]{3,2,1,0:T(8,128)(2,1)} %select_bitcast_fusion.2), channel_id=1, source_target_pairs={{0,4},{4,0},{8,12},{12,8},{1,5},{5,1},{9,13},{13,9},{2,6},{6,2},{1... | collective-permute-start | bytes 4184072 | tf_op jit(solution)/shard_map/ppermute | solution.py:98
  414.0 24.2 %collective-permute-start.20 = (bf16[128,1536]{1,0:T(8,128)(2,1)}, bf16[128,1536]{1,0:T(8,128)(2,1)}, u32[]{:S(2)}, u32[]{:S(2)}) collective-permute-start(bf16[128,1536]{1,0:T(8,128)(2,1)} %convert_element_type.635), channel_id=1, source_target_pairs={{1,0},{2,1},{3,2},{5,4},{6,5},{7,6},{9,8},{10,9},{11,10},{13,12},{... | collective-permute-start | bytes 1179656 | tf_op jit(solution)/shard_map/ppermute | solution.py:43
  416.3 19.2 %collective-permute-start.21 = (bf16[1,4,48,1816]{3,2,1,0:T(8,128)(2,1)}, bf16[1,4,48,1816]{3,2,1,0:T(8,128)(2,1)}, u32[]{:S(2)}, u32[]{:S(2)}) collective-permute-start(bf16[1,4,48,1816]{3,2,1,0:T(8,128)(2,1)} %select_bitcast_fusion.8), channel_id=1, source_target_pairs={{0,8},{4,12},{8,0},{12,4},{1,9},{5,13},{9,1},{13,5},{2,10},{6,14},... | collective-permute-start | bytes 2092040 | tf_op jit(solution)/shard_map/ppermute | solution.py:98
  417.8 5.3 collective-permute-start.22
  442.3 31.7 %collective-permute-start.26 = (bf16[2,4,48,3072]{3,2,1,0:T(8,128)(2,1)}, bf16[2,4,48,3072]{3,2,1,0:T(8,128)(2,1)}, u32[]{:S(2)}, u32[]{:S(2)}) collective-permute-start(bf16[2,4,48,3072]{3,2,1,0:T(8,128)(2,1)} %select_bitcast_fusion), channel_id=1, source_target_pairs={{0,4},{4,0},{8,12},{12,8},{1,5},{5,1},{9,13},{13,9},{2,6},{6,2},{1... | collective-permute-start | bytes 7077896 | tf_op jit(solution)/shard_map/ppermute | solution.py:98
  443.0 139.5 %collective-permute-start.34 = (bf16[1,1,48,3072]{3,2,1,0:T(8,128)(2,1)}, bf16[1,1,48,3072]{3,2,1,0:T(8,128)(2,1)}, u32[]{:S(2)}, u32[]{:S(2)}) collective-permute-start(bf16[1,1,48,3072]{3,2,1,0:T(8,128)(2,1)} %fusion.126), channel_id=1, source_target_pairs={{0,2},{1,3},{2,0},{3,1},{4,6},{5,7},{6,4},{7,5},{8,10},{9,11},{10,... | collective-permute-start | bytes 884744 | tf_op jit(solution)/shard_map/ppermute | solution.py:98
  449.8 22.7 %collective-permute-start.24 = (bf16[2,1,48,1816]{3,2,0,1:T(8,128)(2,1)}, bf16[2,1,48,1816]{3,2,0,1:T(8,128)(2,1)}, u32[]{:S(2)}, u32[]{:S(2)}) collective-permute-start(bf16[2,1,48,1816]{3,2,0,1:T(8,128)(2,1)} %fusion.121), channel_id=1, source_target_pairs={{0,1},{1,0},{2,3},{3,2},{4,5},{5,4},{6,7},{7,6},{8,9},{9,8},{10,11... | collective-permute-start | bytes 1046024 | tf_op jit(solution)/shard_map/ppermute | solution.py:98
  453.0 18.9 %collective-permute-start.25 = (f32[1,4,1,776]{3,1,2,0:T(4,128)}, f32[1,4,1,776]{3,1,2,0:T(4,128)}, u32[]{:S(2)}, u32[]{:S(2)}) collective-permute-start(f32[1,4,1,776]{3,1,2,0:T(4,128)} %select_bitcast_fusion.17), channel_id=1, source_target_pairs={{0,8},{4,12},{8,0},{12,4},{1,9},{5,13},{9,1},{13,5},{2,10},{6,14},... | collective-permute-start | bytes 37256 | tf_op jit(solution)/shard_map/ppermute | solution.py:98
  456.2 22.2 %collective-permute-start.23 = (bf16[128,1536]{1,0:T(8,128)(2,1)}, bf16[128,1536]{1,0:T(8,128)(2,1)}, u32[]{:S(2)}, u32[]{:S(2)}) collective-permute-start(bf16[128,1536]{1,0:T(8,128)(2,1)} %add_convert_fusion.1), channel_id=1, source_target_pairs={{1,0},{2,1},{3,2},{5,4},{6,5},{7,6},{9,8},{10,9},{11,10},{13,12},{... | collective-permute-start | bytes 1179656 | tf_op jit(solution)/shard_map/ppermute | solution.py:43
  479.8 27.9 %collective-permute-start.29 = (bf16[1,4,48,3072]{3,2,1,0:T(8,128)(2,1)}, bf16[1,4,48,3072]{3,2,1,0:T(8,128)(2,1)}, u32[]{:S(2)}, u32[]{:S(2)}) collective-permute-start(bf16[1,4,48,3072]{3,2,1,0:T(8,128)(2,1)} %select_bitcast_fusion.3), channel_id=1, source_target_pairs={{0,8},{4,12},{8,0},{12,4},{1,9},{5,13},{9,1},{13,5},{2,10},{6,14},... | collective-permute-start | bytes 3538952 | tf_op jit(solution)/shard_map/ppermute | solution.py:98
  482.2 28.0 %collective-permute-start.27 = (bf16[128,1536]{1,0:T(8,128)(2,1)}, bf16[128,1536]{1,0:T(8,128)(2,1)S(1)}, u32[]{:S(2)}, u32[]{:S(2)}) collective-permute-start(bf16[128,1536]{1,0:T(8,128)(2,1)} %add_convert_fusion), channel_id=1, source_target_pairs={{1,0},{2,1},{3,2},{5,4},{6,5},{7,6},{9,8},{10,9},{11,10},{13,12},{... | collective-permute-start | bytes 1179656 | tf_op jit(solution)/shard_map/ppermute | solution.py:43
  483.5 12.3 %collective-permute-start.28 = (f32[2,1,1,776]{3,1,2,0:T(1,128)S(1)}, f32[2,1,1,776]{3,1,2,0:T(1,128)S(1)}, u32[]{:S(2)}, u32[]{:S(2)}) collective-permute-start(f32[2,1,1,776]{3,1,2,0:T(1,128)S(1)} %fusion.240), channel_id=1, source_target_pairs={{0,1},{1,0},{2,3},{3,2},{4,5},{5,4},{6,7},{7,6},{8,9},{9,8},{10,11... | collective-permute-start | bytes 18632 | tf_op jit(solution)/shard_map/ppermute | solution.py:98
  487.6 122.7 %collective-permute-start.40 = (bf16[1,1,48,1816]{3,2,1,0:T(8,128)(2,1)}, bf16[1,1,48,1816]{3,2,1,0:T(8,128)(2,1)}, u32[]{:S(2)}, u32[]{:S(2)}) collective-permute-start(bf16[1,1,48,1816]{3,2,1,0:T(8,128)(2,1)} %fusion.132), channel_id=1, source_target_pairs={{0,2},{1,3},{2,0},{3,1},{4,6},{5,7},{6,4},{7,5},{8,10},{9,11},{10,... | collective-permute-start | bytes 523016 | tf_op jit(solution)/shard_map/ppermute | solution.py:98
  516.7 14.7 %collective-permute-start.30 = (bf16[2,1,48,3072]{3,2,0,1:T(8,128)(2,1)}, bf16[2,1,48,3072]{3,2,0,1:T(8,128)(2,1)}, u32[]{:S(2)}, u32[]{:S(2)}) collective-permute-start(bf16[2,1,48,3072]{3,2,0,1:T(8,128)(2,1)} %select_bitcast_fusion.9), channel_id=1, source_target_pairs={{0,1},{1,0},{2,3},{3,2},{4,5},{5,4},{6,7},{7,6},{8,9},{9,8},{10,11... | collective-permute-start | bytes 1769480 | tf_op jit(solution)/shard_map/ppermute | solution.py:98
  532.8 6.1 collective-permute-start.31
  557.0 12.0 %collective-permute-start.46 = (f32[1,1,1,776]{3,2,1,0:T(1,128)S(1)}, f32[1,1,1,776]{3,2,1,0:T(1,128)S(1)}, u32[]{:S(2)}, u32[]{:S(2)}) collective-permute-start(f32[1,1,1,776]{3,2,1,0:T(1,128)S(1)} %fusion.253), channel_id=1, source_target_pairs={{0,2},{1,3},{2,0},{3,1},{4,6},{5,7},{6,4},{7,5},{8,10},{9,11},{10,... | collective-permute-start | bytes 9320 | tf_op jit(solution)/shard_map/ppermute | solution.py:98
  562.7 4.4 collective-permute-start.44
  567.1 11.9 %collective-permute-start.36 = (bf16[2,4,48,1816]{3,2,1,0:T(8,128)(2,1)}, bf16[2,4,48,1816]{3,2,1,0:T(8,128)(2,1)}, u32[]{:S(2)}, u32[]{:S(2)}) collective-permute-start(bf16[2,4,48,1816]{3,2,1,0:T(8,128)(2,1)} %select_bitcast_fusion.1), channel_id=1, source_target_pairs={{0,4},{4,0},{8,12},{12,8},{1,5},{5,1},{9,13},{13,9},{2,6},{6,2},{1... | collective-permute-start | bytes 4184072 | tf_op jit(solution)/shard_map/ppermute | solution.py:98
  567.1 4.6 collective-permute-start.45
  569.0 16.3 %collective-permute-start.33 = (bf16[1,1,48,3072]{3,2,1,0:T(8,128)(2,1)}, bf16[1,1,48,3072]{3,2,1,0:T(8,128)(2,1)S(1)}, u32[]{:S(2)}, u32[]{:S(2)}) collective-permute-start(bf16[1,1,48,3072]{3,2,1,0:T(8,128)(2,1)} %select_bitcast_fusion.13), channel_id=1, source_target_pairs={{0,2},{1,3},{2,0},{3,1},{4,6},{5,7},{6,4},{7,5},{8,10},{9,11},{10,... | collective-permute-start | bytes 884744 | tf_op jit(solution)/shard_map/ppermute | solution.py:98
  575.4 42.7 %collective-permute-start.32 = (f32[256,768]{1,0:T(8,128)}, f32[256,768]{1,0:T(8,128)S(1)}, u32[]{:S(2)}, u32[]{:S(2)}) collective-permute-start(f32[256,768]{1,0:T(8,128)} %get-tuple-element.196), channel_id=1, source_target_pairs={{0,16},{16,0},{1,17},{17,1},{2,18},{18,2},{3,19},{19,3},{4,20},{20... | collective-permute-start | bytes 2359304 | tf_op jit(solution)/shard_map/ppermute | solution.py:47
  581.9 16.7 %collective-permute-start.37 = (bf16[1,4,48,1816]{3,2,1,0:T(8,128)(2,1)S(1)}, bf16[1,4,48,1816]{3,2,1,0:T(8,128)(2,1)S(1)}, u32[]{:S(2)}, u32[]{:S(2)}) collective-permute-start(bf16[1,4,48,1816]{3,2,1,0:T(8,128)(2,1)S(1)} %select_bitcast_fusion.7), channel_id=1, source_target_pairs={{0,8},{4,12},{8,0},{12,4},{1,9},{5,13},{9,1},{13,5},{2,10},{6,14},... | collective-permute-start | bytes 2092040 | tf_op jit(solution)/shard_map/ppermute | solution.py:98
  586.5 13.4 %collective-permute-start.35 = (bf16[48,3072]{1,0:T(8,128)(2,1)S(1)}, bf16[48,3072]{1,0:T(8,128)(2,1)S(1)}, u32[]{:S(2)}, u32[]{:S(2)}) collective-permute-start(bf16[48,3072]{1,0:T(8,128)(2,1)S(1)} %fusion.125), channel_id=1, source_target_pairs={{0,16},{16,0},{1,17},{17,1},{2,18},{18,2},{3,19},{19,3},{4,20},{20... | collective-permute-start | bytes 884744 | tf_op jit(solution)/shard_map/ppermute | solution.py:47
  598.9 7.9 %collective-permute-start.38 = (bf16[2,1,48,1816]{3,2,0,1:T(8,128)(2,1)S(1)}, bf16[2,1,48,1816]{3,2,0,1:T(8,128)(2,1)S(1)}, u32[]{:S(2)}, u32[]{:S(2)}) collective-permute-start(bf16[2,1,48,1816]{3,2,0,1:T(8,128)(2,1)S(1)} %select_bitcast_fusion.12), channel_id=1, source_target_pairs={{0,1},{1,0},{2,3},{3,2},{4,5},{5,4},{6,7},{7,6},{8,9},{9,8},{10,11... | collective-permute-start | bytes 1046024 | tf_op jit(solution)/shard_map/ppermute | solution.py:98
  606.9 8.5 %collective-permute-start.39 = (bf16[1,1,48,1816]{3,2,1,0:T(8,128)(2,1)S(1)}, bf16[1,1,48,1816]{3,2,1,0:T(8,128)(2,1)S(1)}, u32[]{:S(2)}, u32[]{:S(2)}) collective-permute-start(bf16[1,1,48,1816]{3,2,1,0:T(8,128)(2,1)S(1)} %select_bitcast_fusion.14), channel_id=1, source_target_pairs={{0,2},{1,3},{2,0},{3,1},{4,6},{5,7},{6,4},{7,5},{8,10},{9,11},{10,... | collective-permute-start | bytes 523016 | tf_op jit(solution)/shard_map/ppermute | solution.py:98
  616.5 5.6 collective-permute-start.41
  (209 other events, 2426.4 us)
Sparse Core Ops, SparseCore 0:
  22.9 57.8 all-gather.4
  83.0 56.6 all-gather.6
  142.6 41.1 all-gather.8
  186.0 41.2 all-gather.10
